TPU v7x, 32 devices: a whole 2x2x4 slice. The times are simulated.
32 devices in a mesh: dp: 2 (over x), seq: 16 (over z, y, core).
Axes of the slice: x: 2, y: 2, z: 4, core: 2. Of those that a mesh axis runs over, the one named last changes fastest.
Arguments:
- tokens: bfloat16 [2, 4096, 1600], P('dp', 'seq'), may hold values from -6 to 6
- cotangent: bfloat16 [2, 4096, 1600], P('dp', 'seq'), may hold values from -6 to 6
- input_gain: bfloat16 [1600], replicated, may hold values from 0.25 to 1.75
- merged_weight: bfloat16 [1600, 8640], P('seq', 'dp'), may hold values from -0.15625 to 0.15625
- meta_tokens: bfloat16 [1600, 128], P('seq', 'dp'), may hold values from -6 to 6
- select_weight: bfloat16 [3200, 132], P('seq', 'dp'), may hold values from -0.109375 to 0.109375
- step_weight: bfloat16 [3200, 100], P('seq', 'dp'), may hold values from -0.625 to 0.625
- decay_log: bfloat16 [3200, 16], P('seq', 'dp'), may hold values from -7 to 1.5
- conv_weight: bfloat16 [3200, 4], P('seq', 'dp'), may hold values from -3 to 3
- conv_bias: bfloat16 [3200], replicated, may hold values from -3 to 3
- step_bias: bfloat16 [3200], replicated, may hold values from -6 to -1
- skip_gain: bfloat16 [3200], replicated, may hold values from 0.5 to 1.5
- attention_gain: bfloat16 [1600], replicated, may hold values from 0.25 to 1.75
- mamba_gain: bfloat16 [3200], replicated, may hold values from 0.25 to 1.75
- output_weight: bfloat16 [4800, 1600], P('seq', 'dp'), may hold values from -0.1875 to 0.1875
- second_gain: bfloat16 [1600], replicated, may hold values from 0.25 to 1.75
- expand_weight: bfloat16 [1600, 11008], P('seq', 'dp'), may hold values from -0.15625 to 0.15625
- down_weight: bfloat16 [5504, 1600], P('seq', 'dp'), may hold values from -0.078125 to 0.078125
Outputs:
- block_output: bfloat16 [2, 4096, 1600], P('dp', 'seq')
- tokens_grad: float32 [2, 4096, 1600], P('dp', 'seq')
- input_gain_grad: float32 [1600], replicated
- merged_weight_grad: float32 [1600, 8640], P('seq', 'dp')
- meta_tokens_grad: float32 [1600, 128], P('seq', 'dp')
- select_weight_grad: float32 [3200, 132], P('seq', 'dp')
- step_weight_grad: float32 [3200, 100], P('seq', 'dp')
- decay_log_grad: float32 [3200, 16], P('seq', 'dp')
- conv_weight_grad: float32 [3200, 4], P('seq', 'dp')
- conv_bias_grad: float32 [3200], replicated
- step_bias_grad: float32 [3200], replicated
- skip_gain_grad: float32 [3200], replicated
- attention_gain_grad: float32 [1600], replicated
- mamba_gain_grad: float32 [3200], replicated
- output_weight_grad: float32 [4800, 1600], P('seq', 'dp')
- second_gain_grad: float32 [1600], replicated
- expand_weight_grad: float32 [1600, 11008], P('seq', 'dp')
- down_weight_grad: float32 [5504, 1600], P('seq', 'dp')
All inputs are finite; a program needn't handle non-finite values.
Results may differ from a plain program's by a relative error of at most 0.015.
Values may be sent and summed in bfloat16 or wider, within the bound.
A program may use at most 576 MiB of HBM per device.

v0:
```python
import math

import jax
import jax.numpy as jnp
from jax import lax
from jax.sharding import PartitionSpec as P

HEADS = 25
KVHEADS = 5
HEAD = 64
MINNER = 3200
STATE = 16
DTR = 100
FF = 5504
META = 128
WINDOW = 1024
CONV = 4


highest = lax.Precision.HIGHEST
epsilon = 1e-06


def from_behind(array, axis, by):
    size = lax.axis_size(axis)
    pairs = [(i, i + by) for i in range(size) if 0 <= i + by < size]
    return lax.ppermute(array, axis, pairs)


def carried_in(array, axis, combine, identity, reverse):
    size, mine = (lax.axis_size(axis), lax.axis_index(axis))
    everything = jax.tree.map(lambda part: lax.all_gather(part, axis), array)
    start = jax.tree.map(
        lambda part, zero: jnp.broadcast_to(jnp.asarray(zero, part.dtype), part.shape),
        array,
        identity,
    )

    def step(k, before):
        at = size - 1 - k if reverse else k
        reached = at > mine if reverse else at < mine
        new = combine(before, jax.tree.map(lambda part: part[at], everything))
        return jax.tree.map(lambda a, b: jnp.where(reached, a, b), new, before)

    return lax.fori_loop(0, size, step, start)


def rms_norm(values, gain_row):
    return (
        values * lax.rsqrt(jnp.mean(values * values, axis=-1, keepdims=True) + epsilon) * gain_row
    )


def silu_gate(values):
    return values * jax.nn.sigmoid(values)


def softplus(values):
    return jnp.log1p(jnp.exp(values))


def spread(part_one, part_two, part_three):
    halves = (
        lax.all_gather(part_one, "dp", axis=1, tiled=True),
        lax.all_gather(part_two, "dp", axis=1, tiled=True),
        lax.all_gather(part_three, "dp", axis=1, tiled=True),
    )
    return (
        lax.all_gather(halves[0], "seq", axis=0, tiled=True),
        lax.all_gather(halves[1], "seq", axis=0, tiled=True),
        lax.all_gather(halves[2], "seq", axis=0, tiled=True),
    )


def reduce_three(part_one, part_two, part_three):
    sliced = (
        lax.psum_scatter(part_one, "seq", scatter_dimension=0, tiled=True),
        lax.psum_scatter(part_two, "seq", scatter_dimension=0, tiled=True),
        lax.psum_scatter(part_three, "seq", scatter_dimension=0, tiled=True),
    )
    return (
        lax.psum_scatter(
            sliced[0].astype(jnp.bfloat16), "dp", scatter_dimension=1, tiled=True
        ).astype(jnp.float32),
        lax.psum_scatter(
            sliced[1].astype(jnp.bfloat16), "dp", scatter_dimension=1, tiled=True
        ).astype(jnp.float32),
        lax.psum_scatter(
            sliced[2].astype(jnp.bfloat16), "dp", scatter_dimension=1, tiled=True
        ).astype(jnp.float32),
    )


def convolve(extended, kernel, bias_row):
    length = extended.shape[1] - kernel.shape[1] + 1
    convolved = bias_row
    for offset in range(kernel.shape[1]):
        convolved = convolved + kernel[:, offset] * extended[:, offset : offset + length, :]
    return convolved


def chain_step(earlier, later):
    return (earlier[0] * later[0], later[0] * earlier[1] + later[1])


def sub_blocks(array, sub_len):
    return jnp.moveaxis(array, 1, 0).reshape(
        array.shape[1] // sub_len, sub_len, array.shape[0], array.shape[2]
    )


def weighted_sum(exponent, decays, left_side, right_side):
    sub_len = math.gcd(16, exponent.shape[1])

    def one_block(totals, inputs):
        step_rows, left_rows, right_rows = inputs
        factor = jnp.exp(step_rows[:, :, None, :] * decays)
        return (
            totals + jnp.sum(factor * left_rows[:, :, :, None] * right_rows[:, :, None, :], axis=0),
            None,
        )

    initial = jnp.zeros((exponent.shape[0], decays.shape[0], decays.shape[1]), jnp.float32)
    pieces = (
        sub_blocks(exponent, sub_len),
        sub_blocks(left_side, sub_len),
        sub_blocks(right_side, sub_len),
    )
    return lax.scan(one_block, initial, pieces)[0]


def local_scan(signal, step_size, write_mix, read_mix, initial, decays, skip_gain):
    sub_len = math.gcd(16, signal.shape[1])

    def one_step(states, inputs):
        value_row, step_row, write_row, read_row = inputs
        states = (
            jnp.exp(step_row[:, None, :] * decays) * states
            + (step_row * value_row)[:, None, :] * write_row[:, :, None]
        )
        return (states, jnp.sum(read_row[:, :, None] * states, axis=1))

    def run_block(states, inputs):
        return lax.scan(one_step, states, inputs)

    pieces = tuple(
        (sub_blocks(member, sub_len) for member in (signal, step_size, write_mix, read_mix))
    )
    final_state, outputs = lax.scan(jax.checkpoint(run_block), initial, pieces)
    outputs = jnp.moveaxis(outputs.reshape(signal.shape[1], signal.shape[0], signal.shape[2]), 0, 1)
    return (outputs + skip_gain * signal, final_state)


def head_scores(single_query_head, single_key_head, meta_head, visible, score_scale):
    nearby = (
        jnp.einsum(
            "fkjw,fiw->fjki", single_query_head, single_key_head, preferred_element_type=jnp.float32
        )
        * score_scale
    )
    distant = (
        jnp.einsum(
            "sqgd,md->sgqm", single_query_head, meta_head, preferred_element_type=jnp.float32
        )
        * score_scale
    )
    return (distant, jnp.where(visible, nearby, -1e30))


def decay_rates(decay_wide):
    return -jnp.exp(decay_wide.T)


def gating(scanned, gate_path):
    return scanned * silu_gate(gate_path)


def activate(gate_pre, up_pre):
    return silu_gate(gate_pre) * up_pre


def combine_paths(attended, mamba_path, attention_row, mamba_row):
    return jnp.concatenate(
        [rms_norm(attended, attention_row), rms_norm(mamba_path, mamba_row)], axis=-1
    )


def shards(
    tokens,
    cotangent,
    input_gain,
    merged_weight,
    meta_tokens,
    select_weight,
    step_weight,
    decay_log,
    conv_weight,
    conv_bias,
    step_bias,
    skip_gain,
    attention_gain,
    mamba_gain,
    output_weight,
    second_gain,
    expand_weight,
    down_weight,
):
    sequences = tokens.shape[0]
    local_len = tokens.shape[1]
    query_width = HEADS * HEAD
    key_width = KVHEADS * HEAD
    group_size = HEADS // KVHEADS
    inner_start = query_width + 2 * key_width
    reach_count = (WINDOW - 1) // local_len + 1
    window_len = (reach_count + 1) * local_len
    score_scale = HEAD ** (-0.5)
    position = lax.axis_index("seq")
    input_wide = input_gain.astype(jnp.float32)
    conv_bias_wide = conv_bias.astype(jnp.float32)
    step_bias_wide = step_bias.astype(jnp.float32)
    skip_wide = skip_gain.astype(jnp.float32)
    attention_wide = attention_gain.astype(jnp.float32)
    mamba_wide = mamba_gain.astype(jnp.float32)
    second_wide = second_gain.astype(jnp.float32)
    merged_full, meta_full, select_full = spread(merged_weight, meta_tokens, select_weight)
    step_full, decay_full, kernel_full = spread(step_weight, decay_log, conv_weight)
    tokens_wide = tokens.astype(jnp.float32)
    normed_wide, norm_back = jax.vjp(rms_norm, tokens_wide, input_wide)
    normed = normed_wide.astype(jnp.bfloat16)
    meta_normed = rms_norm(meta_full.astype(jnp.float32).T, input_wide).astype(jnp.bfloat16)
    meta_pairs = jnp.dot(
        meta_normed, merged_full[:, query_width:inner_start], preferred_element_type=jnp.float32
    ).astype(jnp.bfloat16)
    projected = jnp.einsum("scd,df->scf", normed, merged_full, preferred_element_type=jnp.float32)
    queries = projected[..., :query_width].astype(jnp.bfloat16)
    pairs_own = projected[..., query_width:inner_start].astype(jnp.bfloat16)
    inner_path = projected[..., inner_start : inner_start + MINNER].astype(jnp.bfloat16)
    gate_path = projected[..., inner_start + MINNER :]
    window = jnp.concatenate(
        [from_behind(pairs_own, "seq", behind) for behind in range(reach_count, 0, -1)]
        + [pairs_own],
        axis=1,
    )
    lowest = (position - reach_count) * local_len
    target = jnp.arange(local_len, dtype=jnp.int32)
    source = jnp.arange(window_len, dtype=jnp.int32)
    distance = target[:, None] - source[None, :] + reach_count * local_len
    visible = (distance >= 0) & (distance < WINDOW) & (lowest + source[None, :] >= 0)
    query_heads = jnp.moveaxis(
        queries.reshape(sequences, local_len, KVHEADS, group_size, HEAD), 2, 0
    )
    key_heads = jnp.moveaxis(
        window[..., :key_width].reshape(sequences, window_len, KVHEADS, HEAD), 2, 0
    )
    value_heads = jnp.moveaxis(
        window[..., key_width:].reshape(sequences, window_len, KVHEADS, HEAD), 2, 0
    )
    meta_keys = jnp.moveaxis(meta_pairs[:, :key_width].reshape(META, KVHEADS, HEAD), 1, 0)
    meta_values = jnp.moveaxis(meta_pairs[:, key_width:].reshape(META, KVHEADS, HEAD), 1, 0)

    def attend_head(inputs):
        single_query_head, single_key_head, single_value_head, meta_key, meta_value = inputs
        distant, nearby = head_scores(
            single_query_head, single_key_head, meta_key, visible, score_scale
        )
        row_max = jnp.maximum(jnp.max(distant, axis=-1), jnp.max(nearby, axis=-1))[..., None]
        distant = jnp.exp(distant - row_max)
        nearby = jnp.exp(nearby - row_max)
        totals = jnp.sum(distant, axis=-1, keepdims=True) + jnp.sum(nearby, axis=-1, keepdims=True)
        result = jnp.einsum(
            "sgqm,md->sqgd",
            (distant / totals).astype(jnp.bfloat16),
            meta_value,
            preferred_element_type=jnp.float32,
        )
        result = result + jnp.einsum(
            "kxja,kab->kjxb",
            (nearby / totals).astype(jnp.bfloat16),
            single_value_head,
            preferred_element_type=jnp.float32,
        )
        return (result, row_max[..., 0] + jnp.log(totals[..., 0]))

    attended_heads, log_totals = lax.map(
        attend_head, (query_heads, key_heads, value_heads, meta_keys, meta_values)
    )
    attended = jnp.moveaxis(attended_heads, 0, 2).reshape(sequences, local_len, query_width)
    tail_rows = inner_path[:, local_len - (CONV - 1) :]
    previous = from_behind(tail_rows, "seq", 1)
    extended = jnp.concatenate([previous, inner_path], axis=1).astype(jnp.float32)
    kernel = kernel_full.astype(jnp.float32)
    convolved, convolve_back = jax.vjp(convolve, extended, kernel, conv_bias_wide)
    activated, silu_back = jax.vjp(silu_gate, convolved)
    signal = activated.astype(jnp.bfloat16)
    selected = jnp.einsum("scm,mr->scr", signal, select_full, preferred_element_type=jnp.float32)
    step_raw = selected[..., :DTR].astype(jnp.bfloat16)
    write_mix = selected[..., DTR : DTR + STATE]
    read_mix = selected[..., DTR + STATE :]
    step_pre = (
        jnp.einsum("scr,mr->scm", step_raw, step_full, preferred_element_type=jnp.float32)
        + step_bias_wide
    )
    step_size = softplus(step_pre)
    decays, decay_back = jax.vjp(decay_rates, decay_full.astype(jnp.float32))
    signal_wide = signal.astype(jnp.float32)
    lower_ones = (target[:, None] >= target[None, :]).astype(jnp.float32)
    running_total = jnp.einsum("ts,bsm->btm", lower_ones, step_size, precision=highest)
    step_totals = running_total[:, local_len - 1, :]
    through = jnp.exp(decays[None, :, :] * step_totals[:, None, :])
    local_end = weighted_sum(
        step_totals[:, None, :] - running_total, decays, write_mix, step_size * signal_wide
    )
    carried = carried_in(
        (through, local_end),
        "seq",
        chain_step,
        (jnp.ones_like(through), jnp.zeros_like(local_end)),
        False,
    )
    (scanned, final_state), scan_back = jax.vjp(
        local_scan, signal_wide, step_size, write_mix, read_mix, carried[1], decays, skip_wide
    )
    mamba_path, gating_back = jax.vjp(gating, scanned, gate_path)
    joined_wide, paths_back = jax.vjp(
        combine_paths, attended, mamba_path, attention_wide, mamba_wide
    )
    joined = joined_wide.astype(jnp.bfloat16)
    output_full, expand_full, down_full = spread(output_weight, expand_weight, down_weight)
    hidden = tokens_wide + 0.5 * jnp.einsum(
        "scj,jd->scd", joined, output_full, preferred_element_type=jnp.float32
    )
    normed_two_wide, norm_two_back = jax.vjp(rms_norm, hidden, second_wide)
    normed_two = normed_two_wide.astype(jnp.bfloat16)
    expanded = jnp.einsum(
        "scd,df->scf", normed_two, expand_full, preferred_element_type=jnp.float32
    )
    active_wide, activate_back = jax.vjp(activate, expanded[..., :FF], expanded[..., FF:])
    active = active_wide.astype(jnp.bfloat16)
    block_output = (
        hidden + jnp.einsum("scf,fd->scd", active, down_full, preferred_element_type=jnp.float32)
    ).astype(jnp.bfloat16)
    output_full, expand_full, down_full = spread(output_weight, expand_weight, down_weight)
    down_grad = jnp.einsum("scf,scd->fd", active, cotangent, preferred_element_type=jnp.float32)
    active_grad = jnp.einsum(
        "scd,fd->scf", cotangent, down_full, preferred_element_type=jnp.float32
    )
    gate_grad, up_grad = activate_back(active_grad)
    expand_in = jnp.concatenate([gate_grad, up_grad], axis=-1).astype(jnp.bfloat16)
    expand_grad = jnp.einsum(
        "scd,scf->df", normed_two, expand_in, preferred_element_type=jnp.float32
    )
    second_normed_grad = jnp.einsum(
        "scf,df->scd", expand_in, expand_full, preferred_element_type=jnp.float32
    )
    hidden_part, second_gain_grad = norm_two_back(second_normed_grad)
    hidden_grad = hidden_part + cotangent.astype(jnp.float32)
    mixed_in = hidden_grad.astype(jnp.bfloat16)
    output_grad = 0.5 * jnp.einsum(
        "scj,scd->jd", joined, mixed_in, preferred_element_type=jnp.float32
    )
    joined_grad = 0.5 * jnp.einsum(
        "scd,jd->scj", mixed_in, output_full, preferred_element_type=jnp.float32
    )
    output_sum, expand_sum, down_sum = reduce_three(output_grad, expand_grad, down_grad)
    merged_full, meta_full, select_full = spread(merged_weight, meta_tokens, select_weight)
    attended_grad, mamba_grad, attention_gain_grad, mamba_gain_grad = paths_back(joined_grad)
    scanned_grad, gate_path_grad = gating_back(mamba_grad)
    local_pull = weighted_sum(running_total, decays, read_mix, scanned_grad)
    returned = carried_in(
        (through, local_pull),
        "seq",
        chain_step,
        (jnp.ones_like(through), jnp.zeros_like(local_pull)),
        True,
    )
    scan_grads = scan_back((scanned_grad, returned[1]))
    step_preactivation_grad = scan_grads[1] * jax.nn.sigmoid(step_pre)
    step_bias_grad = jnp.sum(step_preactivation_grad, axis=(0, 1))
    step_in = step_preactivation_grad.astype(jnp.bfloat16)
    step_weight_grad = jnp.einsum(
        "scm,scr->mr", step_in, step_raw, preferred_element_type=jnp.float32
    )
    step_raw_grad = jnp.einsum(
        "scm,mr->scr", step_in, step_full, preferred_element_type=jnp.float32
    )
    selected_in = jnp.concatenate([step_raw_grad, scan_grads[2], scan_grads[3]], axis=-1).astype(
        jnp.bfloat16
    )
    select_grad = jnp.einsum("scm,scr->mr", signal, selected_in, preferred_element_type=jnp.float32)
    signal_grad = scan_grads[0] + jnp.einsum(
        "scr,mr->scm", selected_in, select_full, preferred_element_type=jnp.float32
    )
    extended_grad, kernel_grad, conv_bias_grad = convolve_back(silu_back(signal_grad)[0])
    returned_tail = from_behind(
        extended_grad[:, : CONV - 1].astype(jnp.bfloat16), "seq", -1
    ).astype(jnp.float32)
    inner_grad = extended_grad[:, CONV - 1 :] + jnp.pad(
        returned_tail, ((0, 0), (local_len - (CONV - 1), 0), (0, 0))
    )
    decay_grad = decay_back(scan_grads[5])[0]
    attended_in = jnp.moveaxis(
        attended_grad.astype(jnp.bfloat16).reshape(sequences, local_len, KVHEADS, group_size, HEAD),
        2,
        0,
    )

    def head_back(inputs):
        (
            single_query_head,
            single_key_head,
            single_value_head,
            meta_key,
            meta_value,
            log_total,
            result_gradient,
        ) = inputs
        distant, nearby = head_scores(
            single_query_head, single_key_head, meta_key, visible, score_scale
        )
        distant = jnp.exp(distant - log_total[..., None])
        nearby = jnp.exp(nearby - log_total[..., None])
        distant_prob_grad = jnp.einsum(
            "sqgd,md->sgqm", result_gradient, meta_value, preferred_element_type=jnp.float32
        )
        nearby_prob_grad = jnp.einsum(
            "fkjw,fiw->fjki", result_gradient, single_value_head, preferred_element_type=jnp.float32
        )
        row_dot = jnp.sum(distant_prob_grad * distant, axis=-1, keepdims=True) + jnp.sum(
            nearby_prob_grad * nearby, axis=-1, keepdims=True
        )
        distant_score = (distant * (distant_prob_grad - row_dot)).astype(jnp.bfloat16)
        neighbor_score = (nearby * (nearby_prob_grad - row_dot)).astype(jnp.bfloat16)
        query_grad = score_scale * (
            jnp.einsum("sgqm,md->sqgd", distant_score, meta_key, preferred_element_type=jnp.float32)
            + jnp.einsum(
                "kxja,kab->kjxb",
                neighbor_score,
                single_key_head,
                preferred_element_type=jnp.float32,
            )
        )
        key_grad = score_scale * jnp.einsum(
            "ozty,otzx->oyx", neighbor_score, single_query_head, preferred_element_type=jnp.float32
        )
        meta_key_grad = score_scale * jnp.einsum(
            "sgqm,sqgd->md", distant_score, single_query_head, preferred_element_type=jnp.float32
        )
        value_grad = jnp.einsum(
            "ozty,otzx->oyx",
            nearby.astype(jnp.bfloat16),
            result_gradient,
            preferred_element_type=jnp.float32,
        )
        meta_value_grad = jnp.einsum(
            "sgqm,sqgd->md",
            distant.astype(jnp.bfloat16),
            result_gradient,
            preferred_element_type=jnp.float32,
        )
        return (query_grad, key_grad, value_grad, meta_key_grad, meta_value_grad)

    head_grads = lax.map(
        head_back,
        (query_heads, key_heads, value_heads, meta_keys, meta_values, log_totals, attended_in),
    )
    query_grad = jnp.moveaxis(head_grads[0], 0, 2).reshape(sequences, local_len, query_width)
    window_grad = jnp.concatenate(
        [
            jnp.moveaxis(head_grads[1], 0, 2).reshape(sequences, window_len, key_width),
            jnp.moveaxis(head_grads[2], 0, 2).reshape(sequences, window_len, key_width),
        ],
        axis=-1,
    )
    meta_pair_grad = jnp.concatenate(
        [
            jnp.moveaxis(head_grads[3], 0, 1).reshape(META, key_width),
            jnp.moveaxis(head_grads[4], 0, 1).reshape(META, key_width),
        ],
        axis=-1,
    )
    own_grad = window_grad[:, reach_count * local_len :]
    for behind in range(1, reach_count + 1):
        own_grad = own_grad + from_behind(
            window_grad[
                :, (reach_count - behind) * local_len : (reach_count - behind + 1) * local_len
            ].astype(jnp.bfloat16),
            "seq",
            -behind,
        ).astype(jnp.float32)
    projected_in = jnp.concatenate(
        [
            query_grad.astype(jnp.bfloat16),
            own_grad.astype(jnp.bfloat16),
            inner_grad.astype(jnp.bfloat16),
            gate_path_grad.astype(jnp.bfloat16),
        ],
        axis=-1,
    )
    merged_grad = jnp.einsum(
        "scd,scf->df", normed, projected_in, preferred_element_type=jnp.float32
    )
    normed_grad = jnp.einsum(
        "scf,df->scd", projected_in, merged_full, preferred_element_type=jnp.float32
    )
    meta_rows = meta_full.astype(jnp.float32).T
    meta_again, meta_back = jax.vjp(rms_norm, meta_rows, input_wide)
    pair_columns = merged_full[:, query_width:inner_start].astype(jnp.float32)
    merged_grad = merged_grad.at[:, query_width:inner_start].add(
        jnp.dot(
            meta_again.astype(jnp.bfloat16).astype(jnp.float32).T, meta_pair_grad, precision=highest
        )
    )
    meta_rows_grad, meta_gain_grad = meta_back(
        jnp.dot(meta_pair_grad, pair_columns.T, precision=highest)
    )
    tokens_part, input_gain_part = norm_back(normed_grad)
    tokens_grad = hidden_grad + tokens_part
    merged_sum, meta_sum, select_sum = reduce_three(merged_grad, meta_rows_grad.T, select_grad)
    step_sum, decay_sum, kernel_sum = reduce_three(step_weight_grad, decay_grad, kernel_grad)
    small_sums = lax.psum(
        (
            input_gain_part + meta_gain_grad,
            conv_bias_grad,
            step_bias_grad,
            scan_grads[6],
            attention_gain_grad,
            mamba_gain_grad,
            second_gain_grad,
        ),
        ("dp", "seq"),
    )
    return (
        block_output,
        tokens_grad,
        small_sums[0],
        merged_sum,
        meta_sum,
        select_sum,
        step_sum,
        decay_sum,
        kernel_sum,
        small_sums[1],
        small_sums[2],
        small_sums[3],
        small_sums[4],
        small_sums[5],
        output_sum,
        small_sums[6],
        expand_sum,
        down_sum,
    )


def solution(mesh):
    placed = (
        P("dp", "seq", None),
        P("dp", "seq", None),
        P(),
        P("seq", "dp"),
        P("seq", "dp"),
        P("seq", "dp"),
        P("seq", "dp"),
        P("seq", "dp"),
        P("seq", "dp"),
        P(),
        P(),
        P(),
        P(),
        P(),
        P("seq", "dp"),
        P(),
        P("seq", "dp"),
        P("seq", "dp"),
    )
    return jax.shard_map(
        shards,
        mesh=mesh,
        in_specs=placed,
        out_specs=(
            P("dp", "seq", None),
            P("dp", "seq", None),
            P(),
            P("seq", "dp"),
            P("seq", "dp"),
            P("seq", "dp"),
            P("seq", "dp"),
            P("seq", "dp"),
            P("seq", "dp"),
            P(),
            P(),
            P(),
            P(),
            P(),
            P("seq", "dp"),
            P(),
            P("seq", "dp"),
            P("seq", "dp"),
        ),
        check_vma=False,
    )
```

profile of v0, /device:TPU:0, one launch (start us, length us, event | category | flops | bytes accessed | tf_op | source)
XLA Modules:
  0.0 4568.1 jit_solution(13167952155977195817)
XLA Ops:
  8.0 34.2 all-gather.38.cloned.1.call-done
  71.1 21.8 all-gather.8
  125.2 27.5 all_gather.97
  152.7 28.3 all-gather.10
  181.0 32.8 all-gather.40.cloned.1.call-done
  213.8 25.4 reshape.1345
  298.5 29.6 while.269
  334.8 23.1 all-gather.3
  361.9 43.3 all-gather.42.cloned.1.call-done
  474.3 37.2 while.267
  537.9 119.3 %while.266 = (s32[]{:T(128)}, f32[1,16,3200]{2,1,0:T(8,128)S(1)}, f32[16,16,1,3200]{3,1,2,0:T(8,128)}, f32[16,1,16,3200]{3,2,1,0:T(8,128)}, f32[16,16,1,3200]{3,...) while((s32[]{:T(128)}, f32[1,16,3200]{2,1,0:T(8,128)S(1)}, ...), condition=%wide.region_18.19_spmd.clone, body=%wide.region_14.18_spmd.sunk.clone | while | flops 307204 | bytes 2376390 | solution.py:149
  694.3 43.5 reshape.1363
  737.8 20.5 convolution_bitcast_fusion.7
  758.3 34.6 all-gather.30.cloned.1.call-done
  856.9 40.7 while.271
  903.9 112.1 %while.268 = (s32[]{:T(128)}, bf16[5,1,256,5,64]{2,4,3,1,0:T(8,128)(2,1)}, f32[5,1,1280,64]{2,3,1,0:T(8,128)}, f32[5,1,1280,64]{2,3,1,0:T(8,128)}, f32[5,128,64]...) while((s32[]{:T(128)}, ...), condition=%wide.region_26.27_spmd.clone.clone, body=%wide.region_23.26_spmd.clone.sunk.clone | while | flops 1171708672 | bytes 67526120 | solution.py:462
  1035.3 330.8 %fusion.231 = (f32[112,128]{1,0:T(8,128)S(1)}, f32[304,1600]{1,0:T(8,128)S(1)}) fusion(f32[1600,128]{1,0:T(8,128)S(1)} %add_add_fusion.4, f32[4800,1600]{1,0:T(8,128)} %convolution_multiply_fusion.2), kind=kCustom, calls=%all-reduce-scatter.5 | all-reduce-scatter fusion | flops 8011778 | bytes 33542656
  1429.3 841.0 %while.275 = (s32[]{:T(128)}, f32[16,3200]{1,0:T(8,128)S(1)}, f32[1,16,3200]{2,1,0:T(8,128)S(1)}, f32[16,16,1,3200]{3,1,2,0:T(8,128)}, f32[16,16,1,3200]{3,1,2,0...) while((s32[]{:T(128)}, f32[16,3200]{1,0:T(8,128)S(1)}, ...), condition=%wide.region_42.43_spmd.clone.clone, body=%wide.region_33.42_spmd.clone.sunk.clone | while | flops 1187178 | bytes 7589443 | solution.py:149
  1452.1 28.9 while.274
  1504.7 28.9 while.274
  1557.3 28.9 while.274
  1609.8 28.9 while.274
  1662.4 28.9 while.274
  1715.0 28.9 while.274
  1767.5 28.9 while.274
  1820.1 28.9 while.274
  1872.7 28.9 while.274
  1925.2 28.9 while.274
  1977.8 28.9 while.274
  2030.4 28.9 while.274
  2082.9 28.9 while.274
  2135.5 28.9 while.274
  2188.0 28.9 while.274
  2240.6 28.9 while.274
  2287.6 20.4 multiply_reduce_fusion.14
  2311.0 62.5 %all-reduce.33 = (bf16[3200,16]{0,1:T(8,128)(2,1)S(1)}, bf16[3200,4]{0,1:T(4,128)(2,1)}) all-reduce(f32[3200,16]{0,1:T(8,128)S(1)} %copy-done.47, f32[3200,4]{0,1:T(4,128)S(1)} %pad_add_fusion.1), channel_id=13, replica_groups=mesh['dp'=2,'seq'=16] {'seq'}, use_global_device_ids=true, to_apply=%region_57.58.clone | all-reduce | flops 64000 | bytes 384000
  2395.3 34.5 fusion.136
  2429.7 919.8 %fusion.8 = f32[112,11008]{1,0:T(8,128)} fusion(f32[1600,11008]{1,0:T(8,128)} %fusion.136), kind=kCustom, calls=%all-reduce-scatter.4 | all-reduce-scatter fusion | flops 19726336 | bytes 75383296
  3352.2 34.0 collective-permute-start.16
  3391.3 35.0 collective-permute-done.17
  3427.5 40.5 concatenate.76
  3487.9 22.9 collective-permute-done.7
  3535.3 23.0 fusion.195
  3565.6 23.0 scatter-add.4
  3588.6 652.4 %fusion.4 = f32[112,8640]{1,0:T(8,128)} fusion(f32[1600,8640]{1,0:T(8,128)} %scatter-add.4), kind=kCustom, calls=%all-reduce-scatter | all-reduce-scatter fusion | flops 15482881 | bytes 59167232
  4270.5 28.5 collective-permute-done.11
  4298.9 30.3 concatenate.72
  4423.2 128.7 %all-reduce.32.cloned.1.call-done = (f32[1600]{0:T(1024)}, f32[3200]{0:T(1024)}, f32[3200]{0:T(1024)}, f32[3200]{0:T(1024)}, f32[1600]{0:T(1024)}, /*index=5*/f32[3200]{0:T(1024)}, f32[1600]{0:T(1024)}) async-done(((f32[1600]{0:T(1024)}, f32[3200]{0:T(1024)}, f32[3200]{0:T(1024)}, f32[3200]{0:T(1024)}, f32[1600]{0:T(1024)}, /*index=5*/f32[3200]{0:T(1024)}, f32[1600]{0:T(1024)}), (f32[1600]{0:T(1024)}, ...) | async-done | bytes 70416 | tf_op jit(solution)/shard_map/psum | solution.py:520
  (5595 shorter events, 2168.6 us)
Async XLA Ops:
  7.2 35.0 all-gather.38.cloned.1.call-start
  7.9 205.8 %all-gather.40.cloned.1.call-start = ((), (), s32[]{:S(2)}) async-start(), calls=%async_computation.17 | async-start | bytes 30777344 | tf_op jit(solution)/shard_map/all_gather | solution.py:69
  47.8 281.2 %all-gather.26.cloned.1.call-start = ((), (), s32[]{:S(2)}) async-start(), calls=%async_computation.9 | async-start | bytes 3434496 | tf_op jit(solution)/shard_map/all_gather | solution.py:65
  48.5 310.9 %all-gather.28.cloned.1.call-start = ((), (), s32[]{:S(2)}) async-start(), calls=%async_computation.10 | async-start | bytes 1843200 | tf_op jit(solution)/shard_map/all_gather | solution.py:66
  49.1 356.2 %all-gather.42.cloned.1.call-start = ((), (), s32[]{:S(2)}) async-start(), calls=%async_computation.18 | async-start | bytes 17199104 | tf_op jit(solution)/shard_map/all_gather | solution.py:69
  66.7 449.2 %all-gather.32.cloned.1.call-start = ((), (), s32[]{:S(2)}) async-start(), calls=%async_computation.13 | async-start | bytes 3481600 | tf_op jit(solution)/shard_map/all_gather | solution.py:32
  66.8 370.2 %copy-start.48 = (f32[1600]{0:T(1024)}, f32[1600]{0:T(1024)S(1)}, u32[]{:S(2)}) copy-start(f32[1600]{0:T(1024)S(1)} %convert_element_type.225) | copy-start | bytes 19204
  125.1 114.1 %copy-start.74 = (f32[256]{0:T(256)}, f32[256]{0:T(256)S(1)}, u32[]{:S(2)}) copy-start(f32[256]{0:T(256)S(1)} %fusion.164) | copy-start | bytes 3076
  125.1 114.1 %copy-start.69 = (f32[256]{0:T(256)}, f32[256]{0:T(256)S(1)}, u32[]{:S(2)}) copy-start(f32[256]{0:T(256)S(1)} %fusion.213) | copy-start | bytes 3076
  261.0 8.2 collective-permute-start.4
  278.3 563.8 %copy-start.2 = (bf16[1,256,3200]{1,2,0:T(8,128)(2,1)}, bf16[1,256,3200]{1,2,0:T(8,128)(2,1)S(1)}, u32[]{:S(2)}) copy-start(bf16[1,256,3200]{1,2,0:T(8,128)(2,1)S(1)} %get-tuple-element.2431) | copy-start | bytes 4915204
  298.4 217.5 %all-gather.34.cloned.1.call-start = ((), (), s32[]{:S(2)}) async-start(), calls=%async_computation.14 | async-start | bytes 3481600 | tf_op jit(solution)/shard_map/all_gather | solution.py:32
  328.9 365.4 %all-gather.44.cloned.1.call-start = ((), (), s32[]{:S(2)}) async-start(), calls=%async_computation.19 | async-start | bytes 38924288 | tf_op jit(solution)/shard_map/all_gather | solution.py:70
  329.6 463.3 %all-gather.30.cloned.1.call-start = ((), (), s32[]{:S(2)}) async-start(), calls=%async_computation.11 | async-start | bytes 19462144 | tf_op jit(solution)/shard_map/all_gather | solution.py:71
  329.8 512.4 %copy-start.57 = (f32[3200]{0:T(1024)}, f32[3200]{0:T(1024)S(1)}, u32[]{:S(2)}) copy-start(f32[3200]{0:T(1024)S(1)} %convert_element_type.237) | copy-start | bytes 38404
  358.0 470.2 %copy-start.40 = (f32[1600]{0:T(1024)}, f32[1600]{0:T(1024)S(1)}, u32[]{:S(2)}) copy-start(f32[1600]{0:T(1024)S(1)} %convert_element_type.239) | copy-start | bytes 19204
  361.9 1043.4 %all-gather.36.cloned.1.call-start = ((), (), s32[]{:S(2)}) async-start(), calls=%async_computation.15 | async-start | bytes 3481600 | tf_op jit(solution)/shard_map/all_gather | solution.py:32
  424.5 43.5 collective-permute-start
  427.0 42.0 collective-permute-start.1
  429.8 40.2 collective-permute-start.2
  435.0 36.0 collective-permute-start.3
  683.6 144.6 %copy-start.53 = (f32[256]{0:T(256)}, f32[256]{0:T(256)S(1)}, u32[]{:S(2)}) copy-start(f32[256]{0:T(256)S(1)} %fusion.216) | copy-start | bytes 3076
  898.4 3453.0 %reduce-scatter.43.cloned.1.call-start = ((), (), s32[]{:S(2)}) async-start(), calls=%async_computation.21 | async-start | bytes 49152
  903.9 112.1 %copy-start.84 = (f32[128]{0:T(128)S(1)}, f32[128]{0:T(128)}, u32[]{:S(2)}) copy-start(f32[128]{0:T(128)} %copy-done.83) | copy-start | bytes 1540
  1035.3 356.5 %copy-start.90 = (u32[32]{0:T(128)S(1)}, u32[32]{0:T(128)}, u32[]{:S(2)}) copy-start(u32[32]{0:T(128)} %constant.434) | copy-start | bytes 388
  1035.3 356.5 %copy-start.91 = (u32[32]{0:T(128)S(1)}, u32[32]{0:T(128)}, u32[]{:S(2)}) copy-start(u32[32]{0:T(128)} %constant.426) | copy-start | bytes 388
  1366.1 29.6 collective-permute-start.15
  1385.5 8.9 collective-permute-start.12
  1389.9 4.5 collective-permute-start.13
  1395.6 2957.3 %reduce-scatter.47.cloned.1.call-start = ((), (), s32[]{:S(2)}) async-start(), calls=%async_computation.23 | async-start | bytes 1843200
  1405.3 2950.9 %reduce-scatter.39.cloned.1.call-start = ((), (), s32[]{:S(2)}) async-start(), calls=%async_computation.12 | async-start | bytes 12288 | tf_op jit(solution)/shard_map/reduce_scatter | solution.py:85
  2374.2 1983.2 %reduce-scatter.55.cloned.1.call-start = ((), (), s32[]{:S(2)}) async-start(), calls=%async_computation.27 | async-start | bytes 38924288
  2393.8 1990.6 %reduce-scatter.49.cloned.1.call-start = ((), (), s32[]{:S(2)}) async-start(), calls=%async_computation.24 | async-start | bytes 4227072
  3352.2 75.3 %collective-permute-start.16 = (bf16[112,11008]{1,0:T(8,128)(2,1)S(1)}, bf16[112,11008]{1,0:T(8,128)(2,1)}, u32[]{:S(2)}, u32[]{:S(2)}) collective-permute-start(bf16[112,11008]{1,0:T(8,128)(2,1)S(1)} %convert.158), channel_id=1, source_target_pairs={{0,1},{1,2},{2,3},{3,4},{4,5},{5,6},{6,7},{7,8},{8,9},{9,10},{10,1... | collective-permute-start | bytes 7397384
  3388.3 38.0 collective-permute-start.17
  3476.1 911.8 %reduce-scatter.53.cloned.1.call-start = ((), (), s32[]{:S(2)}) async-start(), calls=%async_computation.26 | async-start | bytes 1740800
  3478.6 9.4 collective-permute-start.8
  3480.1 30.7 collective-permute-start.7
  3481.6 29.3 collective-permute-start.6
  3483.3 27.6 collective-permute-start.5
  3520.6 9.6 collective-permute-start.9
  3525.2 872.6 %reduce-scatter.45.cloned.1.call-start = ((), (), s32[]{:S(2)}) async-start(), calls=%async_computation.22 | async-start | bytes 3481600
  4244.7 54.2 %collective-permute-start.10 = (bf16[112,8640]{1,0:T(8,128)(2,1)}, bf16[112,8640]{1,0:T(8,128)(2,1)}, u32[]{:S(2)}, u32[]{:S(2)}) collective-permute-start(bf16[112,8640]{1,0:T(8,128)(2,1)} %convert.156), channel_id=1, source_target_pairs={{0,1},{1,2},{2,3},{3,4},{4,5},{5,6},{6,7},{7,8},{8,9},{9,10},{10,1... | collective-permute-start | bytes 5806088
  4264.3 146.8 %reduce-scatter.41.cloned.1.call-start = ((), (), s32[]{:S(2)}) async-start(), calls=%async_computation.20 | async-start | bytes 3317760
  4266.3 32.6 collective-permute-start.11
  4336.6 83.9 %reduce-scatter.51.cloned.1.call-start = ((), (), s32[]{:S(2)}) async-start(), calls=%async_computation.25 | async-start | bytes 1843200
  4360.9 191.0 %all-reduce.32.cloned.1.call-start = ((), (), s32[]{:S(2)}) async-start(), calls=%async_computation.28 | async-start | bytes 180224 | tf_op jit(solution)/shard_map/psum | solution.py:520
  4404.8 5.5 collective-permute-start.14
  (97 other events, 1438.0 us)
Sparse Core Ops, SparseCore 0:
  9.6 32.5 all-gather.37
  47.9 165.8 all-gather.39
  215.3 35.5 all-gather.25
  252.3 23.3 all-gather.27
  278.3 126.8 all-gather.41
  407.9 45.7 all-gather.31
  456.6 54.6 all-gather.33
  512.9 181.4 all-gather.43
  696.5 96.3 all-gather.29
  898.5 46.4 all-gather.35
  1395.7 11.7 reduce-scatter.42
  1410.3 22.2 reduce-scatter.46
  2374.3 6.9 reduce-scatter.38
  2394.0 728.1 reduce-scatter.54
  3476.3 65.8 reduce-scatter.48
  3546.2 59.4 reduce-scatter.52
  4264.5 78.8 reduce-scatter.44
  4345.6 48.9 reduce-scatter.40
  4397.6 22.8 reduce-scatter.50
  4427.9 123.9 all-reduce.31
where the time goes:
time: 4590 us; the launch traced here: 4570 us
  blocking collectives  2140 us (47%)
  other arithmetic  880 us (19%)
  local copies, waits for them, and re-layouts  591 us (13%)
  matrix products  403 us (9%)
  waiting for transfers between devices  388 us (8%)
  starting transfers between devices  112 us (2%)
    unnamed x6, blocking collectives  1980 us
    reduce_sum x256, other arithmetic, one_step(): (step_row * value_row)[:, None, :] * write_row[:, :, None]  378 us
    dynamic_update_slice x256, other arithmetic, local_scan(): final_state, outputs = lax.scan(jax.checkpoint(run_block), initial, pieces)  234 us
    unnamed x232, local copies, waits for them, and re-layouts  224 us
    psum x1, waiting for transfers between devices, shards(): lax.psum((input_gain_part + meta_gain_grad, conv_bias_grad, step_bias_gra...  129 us

commit v1 on v0

v1 whole, which is shorter than its diff:
```python
import functools

import jax
import jax.numpy as jnp
from jax import lax
from jax.experimental import pallas as pl
from jax.experimental.pallas import tpu as pltpu
from jax.sharding import Mesh
from jax.sharding import PartitionSpec as P

HEADS = 25
KVHEADS = 5
HEAD = 64
MINNER = 3200
STATE = 16
DTR = 100
META = 128
WINDOW = 1024
CONV = 4
epsilon = 1e-06
LANES = 128
STEPS = 8
LOG2E = 1.4426950408889634
VMEM_LIMIT = 60 * 1024 * 1024


def lane_tiles(width):
    return [slice(at, min(at + LANES, width)) for at in range(0, width, LANES)]


def chunk_of(channels):
    for tiles in (5, 4, 6, 3, 2, 7, 1):
        if channels % (tiles * LANES) == 0:
            return tiles * LANES
    return channels


def fold(rows):
    sub = lax.broadcasted_iota(jnp.int32, rows[0].shape, 0)
    for bit in (1, 2, 4):
        clear = (sub & bit) == 0
        rows = [
            jnp.where(clear, one, two) + pltpu.roll(jnp.where(clear, two, one), bit, 0)
            for one, two in zip(rows[0::2], rows[1::2])
        ]
    return rows[0]


def halves(product):
    return product[:8] + product[8:]


def ends_kernel(step_ref, signal_ref, write_ref, decay_ref, end_ref):
    length, width = step_ref.shape
    tiles = lane_tiles(width)
    rates = [decay_ref[:, tile] * LOG2E for tile in tiles]

    def block(at, states):
        states = list(states)
        rows = pl.ds(pl.multiple_of(at * STEPS, STEPS), STEPS)
        step = step_ref[rows, :]
        drive = step * signal_ref[rows, :].astype(jnp.float32)
        for i in range(STEPS):
            write = write_ref[at * STEPS + i]
            for j, tile in enumerate(tiles):
                factor = jnp.exp2(step[i : i + 1, tile] * rates[j])
                states[j] = factor * states[j] + drive[i : i + 1, tile] * write[:, : tile.stop - tile.start]
        return tuple(states)

    zero = tuple(jnp.zeros((STATE, tile.stop - tile.start), jnp.float32) for tile in tiles)
    final = lax.fori_loop(0, length // STEPS, block, zero)
    for j, tile in enumerate(tiles):
        end_ref[:, tile] = final[j]


def pull_kernel(step_ref, grad_ref, read_ref, decay_ref, end_ref):
    length, width = step_ref.shape
    tiles = lane_tiles(width)
    rates = [decay_ref[:, tile] * LOG2E for tile in tiles]
    blocks = length // STEPS

    def block(k, states):
        at = blocks - 1 - k
        states = list(states)
        rows = pl.ds(pl.multiple_of(at * STEPS, STEPS), STEPS)
        step = step_ref[rows, :]
        grad = grad_ref[rows, :]
        for i in reversed(range(STEPS)):
            read = read_ref[at * STEPS + i]
            for j, tile in enumerate(tiles):
                factor = jnp.exp2(step[i : i + 1, tile] * rates[j])
                states[j] = factor * (states[j] + grad[i : i + 1, tile] * read[:, : tile.stop - tile.start])
        return tuple(states)

    zero = tuple(jnp.zeros((STATE, tile.stop - tile.start), jnp.float32) for tile in tiles)
    final = lax.fori_loop(0, blocks, block, zero)
    for j, tile in enumerate(tiles):
        end_ref[:, tile] = final[j]


def carry_over(position, count, reverse, rates, totals_ref, ends_ref, tile):
    def step(k, state):
        at = count - 1 - k if reverse else k
        reached = at > position if reverse else at < position
        factor = jnp.exp2(totals_ref[at, :, tile] * rates)
        new = factor * state + ends_ref[at, :, tile].astype(jnp.float32)
        return jnp.where(reached, new, state)

    return lax.fori_loop(0, count, step, jnp.zeros(rates.shape, jnp.float32))


def scan_kernel(
    position_ref, step_ref, signal_ref, write_ref, read_ref, decay_ref, skip_ref,
    totals_ref, ends_ref, out_ref, enter_ref,
):
    length, width = step_ref.shape
    tiles = lane_tiles(width)
    rates = [decay_ref[:, tile] * LOG2E for tile in tiles]
    enter = tuple(
        carry_over(position_ref[0], totals_ref.shape[0], False, rates[j], totals_ref, ends_ref, tile)
        for j, tile in enumerate(tiles)
    )
    for j, tile in enumerate(tiles):
        enter_ref[:, tile] = enter[j]

    def block(at, states):
        states = list(states)
        rows = pl.ds(pl.multiple_of(at * STEPS, STEPS), STEPS)
        step = step_ref[rows, :]
        signal = signal_ref[rows, :].astype(jnp.float32)
        drive = step * signal
        parts = [[] for tile in tiles]
        for i in range(STEPS):
            write = write_ref[at * STEPS + i]
            read = read_ref[at * STEPS + i]
            for j, tile in enumerate(tiles):
                wide = tile.stop - tile.start
                factor = jnp.exp2(step[i : i + 1, tile] * rates[j])
                states[j] = factor * states[j] + drive[i : i + 1, tile] * write[:, :wide]
                parts[j].append(halves(read[:, :wide] * states[j]))
        for j, tile in enumerate(tiles):
            out_ref[rows, tile] = fold(parts[j]) + skip_ref[:, tile] * signal[:, tile]
        return tuple(states)

    lax.fori_loop(0, length // STEPS, block, enter)


def scan_back_kernel(
    position_ref, step_ref, signal_ref, grad_ref, write_ref, read_ref, decay_ref, skip_ref,
    enter_ref, totals_ref, pulls_ref,
    signal_grad_ref, step_grad_ref, write_grad_ref, read_grad_ref, decay_grad_ref, skip_grad_ref,
    states_ref, factors_ref,
):
    length, width = step_ref.shape
    tiles = lane_tiles(width)
    blocks = length // STEPS
    decays = [decay_ref[:, tile] for tile in tiles]

    @pl.when(pl.program_id(0) == 0)
    def _():
        write_grad_ref[...] = jnp.zeros_like(write_grad_ref)
        read_grad_ref[...] = jnp.zeros_like(read_grad_ref)

    rates = [decay * LOG2E for decay in decays]
    states_ref[0] = enter_ref[...]

    def forward(at, states):
        states = list(states)
        rows = pl.ds(pl.multiple_of(at * STEPS, STEPS), STEPS)
        step = step_ref[rows, :]
        drive = step * signal_ref[rows, :].astype(jnp.float32)
        for i in range(STEPS):
            write = write_ref[at * STEPS + i]
            for j, tile in enumerate(tiles):
                factor = jnp.exp2(step[i : i + 1, tile] * rates[j])
                states[j] = factor * states[j] + drive[i : i + 1, tile] * write[:, : tile.stop - tile.start]
                factors_ref[at * STEPS + i, :, tile] = factor
                states_ref[at * STEPS + i + 1, :, tile] = states[j]
        return tuple(states)

    lax.fori_loop(0, blocks, forward, tuple(enter_ref[:, tile] for tile in tiles))

    leaving = tuple(
        carry_over(position_ref[0], totals_ref.shape[0], True, rates[j], totals_ref, pulls_ref, tile)
        for j, tile in enumerate(tiles)
    )
    zero = tuple(jnp.zeros_like(decay) for decay in decays)
    zero_row = tuple(jnp.zeros((STEPS, tile.stop - tile.start), jnp.float32) for tile in tiles)

    def backward(k, carry):
        at = blocks - 1 - k
        adjoint, decay_sum, skip_sum = (list(part) for part in carry)
        rows = pl.ds(pl.multiple_of(at * STEPS, STEPS), STEPS)
        step = step_ref[rows, :]
        signal = signal_ref[rows, :].astype(jnp.float32)
        grad = grad_ref[rows, :]
        drive = step * signal
        by_write = [[None] * STEPS for tile in tiles]
        by_decay = [[None] * STEPS for tile in tiles]
        for i in reversed(range(STEPS)):
            write = write_ref[at * STEPS + i]
            read = read_ref[at * STEPS + i]
            write_sum = None
            read_sum = None
            for j, tile in enumerate(tiles):
                wide = tile.stop - tile.start
                row = grad[i : i + 1, tile]
                whole = adjoint[j] + read[:, :wide] * row
                adjoint[j] = factors_ref[at * STEPS + i, :, tile] * whole
                kept = adjoint[j] * states_ref[at * STEPS + i, :, tile]
                decay_sum[j] = decay_sum[j] + step[i : i + 1, tile] * kept
                by_decay[j][i] = halves(decays[j] * kept)
                by_write[j][i] = halves(write[:, :wide] * whole)
                write_part = drive[i : i + 1, tile] * whole
                read_part = row * states_ref[at * STEPS + i + 1, :, tile]
                write_sum = write_part if write_sum is None else write_sum + write_part
                read_sum = read_part if read_sum is None else read_sum + read_part
            write_grad_ref[at * STEPS + i] += write_sum
            read_grad_ref[at * STEPS + i] += read_sum
        for j, tile in enumerate(tiles):
            written = fold(by_write[j])
            signal_grad_ref[rows, tile] = step[:, tile] * written + skip_ref[:, tile] * grad[:, tile]
            step_grad_ref[rows, tile] = signal[:, tile] * written + fold(by_decay[j])
            skip_sum[j] = skip_sum[j] + grad[:, tile] * signal[:, tile]
        return tuple(adjoint), tuple(decay_sum), tuple(skip_sum)

    carry = lax.fori_loop(0, blocks, backward, (leaving, zero, zero_row))
    for j, tile in enumerate(tiles):
        decay_grad_ref[:, tile] = carry[1][j]
        skip_grad_ref[:, tile] = carry[2][j]


def by_chunk(rows, chunk):
    return pl.BlockSpec((rows, chunk), lambda c: (0, c))


def stacked(count, rows, chunk):
    return pl.BlockSpec((count, rows, chunk), lambda c: (0, 0, c))


def whole(shape):
    return pl.BlockSpec(shape, lambda c: (0,) * len(shape))


def params():
    return pltpu.CompilerParams(vmem_limit_bytes=VMEM_LIMIT, dimension_semantics=("arbitrary",))


def scan_ends(step_size, signal, write_wide, decays):
    length, channels = step_size.shape
    chunk = chunk_of(channels)
    return pl.pallas_call(
        ends_kernel,
        grid=(channels // chunk,),
        in_specs=[by_chunk(length, chunk), by_chunk(length, chunk), whole(write_wide.shape), by_chunk(STATE, chunk)],
        out_specs=by_chunk(STATE, chunk),
        out_shape=jax.ShapeDtypeStruct((STATE, channels), jnp.float32),
        compiler_params=params(),
        name="scan_ends",
    )(step_size, signal, write_wide, decays)


def scan_pulls(step_size, grad, read_wide, decays):
    length, channels = step_size.shape
    chunk = chunk_of(channels)
    return pl.pallas_call(
        pull_kernel,
        grid=(channels // chunk,),
        in_specs=[by_chunk(length, chunk), by_chunk(length, chunk), whole(read_wide.shape), by_chunk(STATE, chunk)],
        out_specs=by_chunk(STATE, chunk),
        out_shape=jax.ShapeDtypeStruct((STATE, channels), jnp.float32),
        compiler_params=params(),
        name="scan_pulls",
    )(step_size, grad, read_wide, decays)


def scan_forward(position, step_size, signal, write_wide, read_wide, decays, skip, totals, ends):
    length, channels = step_size.shape
    chunk = chunk_of(channels)
    parts = totals.shape[0]
    return pl.pallas_call(
        scan_kernel,
        grid=(channels // chunk,),
        in_specs=[
            pl.BlockSpec(memory_space=pltpu.SMEM),
            by_chunk(length, chunk), by_chunk(length, chunk), whole(write_wide.shape), whole(read_wide.shape),
            by_chunk(STATE, chunk), by_chunk(1, chunk), stacked(parts, 1, chunk), stacked(parts, STATE, chunk),
        ],
        out_specs=[by_chunk(length, chunk), by_chunk(STATE, chunk)],
        out_shape=[
            jax.ShapeDtypeStruct((length, channels), jnp.float32),
            jax.ShapeDtypeStruct((STATE, channels), jnp.float32),
        ],
        compiler_params=params(),
        name="scan_forward",
    )(position, step_size, signal, write_wide, read_wide, decays, skip, totals, ends)


def scan_backward(position, step_size, signal, grad, write_wide, read_wide, decays, skip, enter, totals, pulls):
    length, channels = step_size.shape
    chunk = chunk_of(channels)
    parts = totals.shape[0]
    return pl.pallas_call(
        scan_back_kernel,
        grid=(channels // chunk,),
        in_specs=[
            pl.BlockSpec(memory_space=pltpu.SMEM),
            by_chunk(length, chunk), by_chunk(length, chunk), by_chunk(length, chunk),
            whole(write_wide.shape), whole(read_wide.shape),
            by_chunk(STATE, chunk), by_chunk(1, chunk), by_chunk(STATE, chunk), stacked(parts, 1, chunk),
            stacked(parts, STATE, chunk),
        ],
        out_specs=[
            by_chunk(length, chunk), by_chunk(length, chunk), whole(write_wide.shape), whole(read_wide.shape),
            by_chunk(STATE, chunk), by_chunk(STEPS, chunk),
        ],
        out_shape=[
            jax.ShapeDtypeStruct((length, channels), jnp.float32),
            jax.ShapeDtypeStruct((length, channels), jnp.float32),
            jax.ShapeDtypeStruct(write_wide.shape, jnp.float32),
            jax.ShapeDtypeStruct(read_wide.shape, jnp.float32),
            jax.ShapeDtypeStruct((STATE, channels), jnp.float32),
            jax.ShapeDtypeStruct((STEPS, channels), jnp.float32),
        ],
        scratch_shapes=[
            pltpu.VMEM((length + 1, STATE, chunk), jnp.float32),
            pltpu.VMEM((length, STATE, chunk), jnp.float32),
        ],
        compiler_params=params(),
        name="scan_backward",
    )(position, step_size, signal, grad, write_wide, read_wide, decays, skip, enter, totals, pulls)


def key_blocks(keys, span, count):
    meta = keys - count * span
    return [(0, meta, None)] + [(meta + b * span, span, b) for b in range(count)]


def masked(scores, place, count, position, other):
    if place is None:
        return scores
    row = lax.broadcasted_iota(jnp.int32, scores.shape, 0)
    column = lax.broadcasted_iota(jnp.int32, scores.shape, 1)
    if place == count - 1:
        return jnp.where(row <= column, scores, other)
    there = position + place >= count - 1
    if place == 0:
        return jnp.where((row > column) & there, scores, other)
    return jnp.where(there, scores, other)


def attend_kernel(count, position_ref, query_ref, key_ref, value_ref, out_ref, log_ref):
    position = position_ref[0]
    span = query_ref.shape[1]
    group = query_ref.shape[0] // HEAD
    blocks = key_blocks(key_ref.shape[1], span, count)
    for head in range(group):
        rows = slice(head * HEAD, (head + 1) * HEAD)
        query = query_ref[rows, :] * (HEAD**-0.5)
        scores = [
            masked(
                jnp.dot(key_ref[0, at : at + size, :], query, preferred_element_type=jnp.float32),
                place, count, position, -1e30,
            )
            for at, size, place in blocks
        ]
        top = functools.reduce(jnp.maximum, [jnp.max(part, axis=0, keepdims=True) for part in scores])
        powers = [jnp.exp(part - top) for part in scores]
        total = sum(jnp.sum(part, axis=0, keepdims=True) for part in powers)
        out = sum(
            jnp.dot(value_ref[:, at : at + size], part.astype(jnp.bfloat16), preferred_element_type=jnp.float32)
            for (at, size, place), part in zip(blocks, powers)
        )
        out_ref[rows, :] = out / total
        log_ref[0, head : head + 1, :] = top + jnp.log(total)


def attend_back_kernel(
    count, position_ref, query_ref, grad_ref, out_ref, log_ref, key_ref, value_ref, key_turned_ref,
    query_grad_ref, key_grad_ref, value_grad_ref,
):
    position = position_ref[0]
    span = query_ref.shape[1]
    group = query_ref.shape[0] // HEAD
    blocks = key_blocks(key_ref.shape[1], span, count)
    turned = (((1,), (1,)), ((), ()))
    for head in range(group):
        rows = slice(head * HEAD, (head + 1) * HEAD)
        query = query_ref[rows, :] * (HEAD**-0.5)
        grad = grad_ref[rows, :]
        along = jnp.sum(grad.astype(jnp.float32) * out_ref[rows, :], axis=0, keepdims=True)
        log_total = log_ref[0, head : head + 1, :]
        query_sum = jnp.zeros((HEAD, span), jnp.float32)
        for at, size, place in blocks:
            keys = slice(at, at + size)
            score = jnp.dot(key_ref[0, keys, :], query, preferred_element_type=jnp.float32)
            prob = jnp.exp(masked(score, place, count, position, -1e30) - log_total)
            prob_grad = jnp.dot(value_ref[0, keys, :], grad, preferred_element_type=jnp.float32)
            score_grad = (prob * (prob_grad - along)).astype(jnp.bfloat16)
            query_sum += jnp.dot(key_turned_ref[:, keys], score_grad, preferred_element_type=jnp.float32)
            by_key = lax.dot_general(score_grad, query, turned, preferred_element_type=jnp.float32)
            by_value = lax.dot_general(prob.astype(jnp.bfloat16), grad, turned, preferred_element_type=jnp.float32)
            if head == 0:
                key_grad_ref[0, keys, :] = by_key
                value_grad_ref[0, keys, :] = by_value
            else:
                key_grad_ref[0, keys, :] += by_key
                value_grad_ref[0, keys, :] += by_value
        query_grad_ref[rows, :] = (query_sum * (HEAD**-0.5)).astype(query_grad_ref.dtype)


def by_head(rows, columns):
    return pl.BlockSpec((rows, columns), lambda g: (g, 0))


def head_stack(rows, columns):
    return pl.BlockSpec((1, rows, columns), lambda g: (g, 0, 0))


def attend(position, query_turned, keys, value_turned, count):
    span = query_turned.shape[1]
    group = query_turned.shape[0] // KVHEADS
    total = keys.shape[1]
    return pl.pallas_call(
        functools.partial(attend_kernel, count),
        grid=(KVHEADS,),
        in_specs=[
            pl.BlockSpec(memory_space=pltpu.SMEM),
            by_head(group, span), head_stack(total, HEAD), by_head(HEAD, total),
        ],
        out_specs=[by_head(group, span), head_stack(8, span)],
        out_shape=[
            jax.ShapeDtypeStruct(query_turned.shape, jnp.float32),
            jax.ShapeDtypeStruct((KVHEADS, 8, span), jnp.float32),
        ],
        compiler_params=params(),
        name="attend",
    )(position, query_turned, keys, value_turned)


def attend_back(position, query_turned, grad_turned, out_turned, logs, keys, values, key_turned, count):
    span = query_turned.shape[1]
    group = query_turned.shape[0] // KVHEADS
    total = keys.shape[1]
    return pl.pallas_call(
        functools.partial(attend_back_kernel, count),
        grid=(KVHEADS,),
        in_specs=[
            pl.BlockSpec(memory_space=pltpu.SMEM),
            by_head(group, span), by_head(group, span), by_head(group, span), head_stack(8, span),
            head_stack(total, HEAD), head_stack(total, HEAD), by_head(HEAD, total),
        ],
        out_specs=[by_head(group, span), head_stack(total, HEAD), head_stack(total, HEAD)],
        out_shape=[
            jax.ShapeDtypeStruct(query_turned.shape, jnp.bfloat16),
            jax.ShapeDtypeStruct(keys.shape, jnp.float32),
            jax.ShapeDtypeStruct(keys.shape, jnp.float32),
        ],
        compiler_params=params(),
        name="attend_back",
    )(position, query_turned, grad_turned, out_turned, logs, keys, values, key_turned)


SEQ = ("chip", "core")
ALL = ("dp",) + SEQ


def from_behind(array, by):
    size = lax.axis_size("chip") * lax.axis_size("core")
    pairs = [(i, i + by) for i in range(size) if 0 <= i + by < size]
    return lax.ppermute(array, SEQ, pairs)


def swap(array, axis="dp"):
    return lax.ppermute(array, axis, [(0, 1), (1, 0)])


def sum_everywhere(array):
    array = array + swap(array, "core")
    chips = lax.axis_size("chip")
    step = 1
    while step < chips:
        array = array + lax.ppermute(array, "chip", [(i, i ^ step) for i in range(chips)])
        step *= 2
    return array + swap(array)


def parity_kernel(parts, block, core_ref, in_ref, own_ref, other_ref):
    values = in_ref[...].astype(jnp.float32)
    even, odd = [
        jnp.concatenate(
            [values[:, at * block : (at + 1) * block] for at in range(core, parts, 2)], axis=1
        )
        for core in (0, 1)
    ]
    own = core_ref[0] == 0
    own_ref[...] = jnp.where(own, even, odd).astype(own_ref.dtype)
    other_ref[...] = jnp.where(own, odd, even).astype(other_ref.dtype)


def parity_columns(array, parts, block):
    rows = array.shape[0]
    step = 64 if rows % 64 == 0 else rows
    half = pl.BlockSpec((step, parts // 2 * block), lambda r: (r, 0))
    return pl.pallas_call(
        functools.partial(parity_kernel, parts, block),
        grid=(rows // step,),
        in_specs=[
            pl.BlockSpec(memory_space=pltpu.SMEM),
            pl.BlockSpec((step, parts * block), lambda r: (r, 0)),
        ],
        out_specs=[half, half],
        out_shape=[jax.ShapeDtypeStruct((rows, parts // 2 * block), array.dtype)] * 2,
        compiler_params=params(),
        name="parity_columns",
    )(jnp.reshape(lax.axis_index("core"), (1,)).astype(jnp.int32), array)


def grad_parts(left, right, scale=1.0):
    kept, given = left
    sent = (scale * dot_rows(given, right)).astype(jnp.bfloat16)
    got = swap(sent, "core")
    return (scale * dot_rows(kept, right) + got.astype(jnp.float32)).astype(jnp.bfloat16)


def scatter_rows(total, rows):
    chips = lax.axis_size("chip")
    return lax.psum_scatter(total.reshape(chips, rows, -1), "chip", scatter_dimension=0)


def rms_norm(values, gain_row, count):
    mean = jnp.sum(values * values, axis=-1, keepdims=True) * (1.0 / count)
    return values * lax.rsqrt(mean + epsilon) * gain_row


def silu_gate(values):
    return values * jax.nn.sigmoid(values)


def softplus(values):
    return jnp.log1p(jnp.exp(values))


def ceil8(rows):
    return -(-rows // 8) * 8


def pad_rows(array, rows):
    return jnp.pad(array, ((0, rows - array.shape[0]), (0, 0)))


MESH = pl.DeviceIdType.MESH


def chip_at(place, chips):
    place = place % chips
    late = place // (chips // 2)
    return (1 - late) * 2 * place + late * (2 * (chips - 1 - place) + 1)


def place_of(chip, chips):
    odd = chip % 2
    return (1 - odd) * (chip // 2) + odd * (chips - 1 - chip // 2)


def gather_kernel(cuts, others, *refs):
    count = len(cuts)
    whole = count + others
    ins, singles = refs[:count], refs[count:whole]
    outs, singles_out = refs[whole : whole + count], refs[whole + count : 2 * whole]
    local_sem, send_sem, recv_sem = refs[2 * whole :]
    dp, chip, core = (lax.axis_index(name) for name in ALL)
    chips = lax.axis_size("chip")
    place = place_of(chip, chips)
    ahead, behind = chip_at(place + 1, chips), chip_at(place + chips - 1, chips)
    to_ahead, to_behind = (dp, ahead, core), (dp, behind, core)
    across, beside = (1 - dp, chip, core), (dp, chip, 1 - core)
    sent = []

    def start(source, target, device):
        index = len(sent)
        copy = pltpu.make_async_remote_copy(
            src_ref=source,
            dst_ref=target,
            send_sem=send_sem.at[index],
            recv_sem=recv_sem.at[index],
            device_id=device,
            device_id_type=MESH,
        )
        copy.start()
        sent.append(copy)
        return copy

    kept = [
        pltpu.make_async_copy(ins[t], outs[t].at[dp, chip, core], local_sem.at[t])
        for t in range(count)
    ]
    for copy in kept:
        copy.start()

    barrier = pltpu.get_barrier_semaphore()
    for device in (to_ahead, to_behind, across, beside):
        pl.semaphore_signal(barrier, inc=1, device_id=device, device_id_type=MESH)
    pl.semaphore_wait(barrier, 4)

    def early(t, at):
        return outs[t].at[:, chip_at(at, chips), core, :, pl.ds(0, cuts[t])]

    def late(t, side, at):
        wide = outs[t].shape[-1] - cuts[t]
        return outs[t].at[side, chip_at(at, chips), core, :, pl.ds(cuts[t], wide)]

    def forward(t, at):
        return late(t, dp, at)

    has_late = [t for t in range(count) if outs[t].shape[-1] > cuts[t]]
    crossing = []
    for t in range(count):
        columns = pl.ds(0, cuts[t])
        crossing.append(
            start(ins[t].at[:, columns], outs[t].at[dp, chip, core, :, columns], across)
        )
    for copy in kept:
        copy.wait()

    up_late, down_late = (chips - 1) // 2, chips // 2
    up_early, down_early = chips // 2, (chips - 1) // 2
    landed = []
    crossed = []

    def pass_late(t, at):
        crossed.append((t, at, start(forward(t, at), forward(t, at), across)))
        landed.append(start(forward(t, at), forward(t, at), beside))

    rings = []
    for t in has_late:
        up = start(forward(t, place), forward(t, place), to_ahead)
        down = start(forward(t, place), forward(t, place), to_behind)
        pass_late(t, place)
        rings.append([t, up, down])
    landed += [start(one, two, across) for one, two in zip(singles, singles_out)]
    early_rings = []
    for t in range(count):
        crossing[t].wait_recv()
        up = start(early(t, place), early(t, place), to_ahead)
        down = start(early(t, place), early(t, place), to_behind)
        landed.append(start(early(t, place), early(t, place), beside))
        early_rings.append([t, up, down])
    for hop in range(1, chips // 2 + 1):
        above, below = place + chips - hop, place + hop
        for ring in rings:
            t, up, down = ring
            if hop <= up_late:
                up.wait_recv()
                if hop < up_late:
                    ring[1] = start(forward(t, above), forward(t, above), to_ahead)
                pass_late(t, above)
            if hop <= down_late:
                down.wait_recv()
                if hop < down_late:
                    ring[2] = start(forward(t, below), forward(t, below), to_behind)
                pass_late(t, below)
        for ring in early_rings:
            t, up, down = ring
            if hop <= up_early:
                up.wait_recv()
                if hop < up_early:
                    ring[1] = start(early(t, above), early(t, above), to_ahead)
                landed.append(start(early(t, above), early(t, above), beside))
            if hop <= down_early:
                down.wait_recv()
                if hop < down_early:
                    ring[2] = start(early(t, below), early(t, below), to_behind)
                landed.append(start(early(t, below), early(t, below), beside))
    for t, at, copy in crossed:
        copy.wait_recv()
        landed.append(start(late(t, 1 - dp, at), late(t, 1 - dp, at), beside))
    for copy in landed:
        copy.wait_recv()
    for copy in sent:
        copy.wait_send()


def gather_everywhere(shards_of, cuts, others):
    chips = lax.axis_size("chip")
    slots = len(others)
    for part, cut in zip(shards_of, cuts):
        slots += 2 * chips + (4 * chips - 1 if part.shape[1] > cut else 0)
    arrays = list(shards_of) + list(others)
    outs = [jax.ShapeDtypeStruct((2, chips, 2) + part.shape, part.dtype) for part in shards_of]
    outs += [jax.ShapeDtypeStruct(part.shape, part.dtype) for part in others]
    moved = sum(4 * chips * part.size * 2 for part in shards_of)
    return pl.pallas_call(
        functools.partial(gather_kernel, cuts, len(others)),
        in_specs=[pl.BlockSpec(memory_space=pl.ANY)] * len(arrays),
        out_specs=[pl.BlockSpec(memory_space=pl.ANY)] * len(arrays),
        out_shape=outs,
        scratch_shapes=[
            pltpu.SemaphoreType.DMA((len(shards_of),)),
            pltpu.SemaphoreType.DMA((slots,)),
            pltpu.SemaphoreType.DMA((slots,)),
        ],
        compiler_params=pltpu.CompilerParams(collective_id=0, has_side_effects=True),
        cost_estimate=pl.CostEstimate(flops=0, bytes_accessed=6 * moved, transcendentals=0),
        name="gather_everywhere",
    )(*arrays)


def ring_kernel(cuts, *refs):
    count = len(cuts)
    ins, outs = refs[:count], refs[count : 2 * count]
    slots = [refs[2 * count + 2 * t : 2 * count + 2 * t + 2] for t in range(count)]
    send_sem, recv_sem = refs[4 * count :]
    dp, chip, core = (lax.axis_index(name) for name in ALL)
    chips = lax.axis_size("chip")
    place = place_of(chip, chips)
    ahead, behind = chip_at(place + 1, chips), chip_at(place + chips - 1, chips)
    devices = ((dp, ahead, core), (dp, behind, core))

    barrier = pltpu.get_barrier_semaphore()
    for device in devices:
        pl.semaphore_signal(barrier, inc=1, device_id=device, device_id_type=MESH)
    pl.semaphore_wait(barrier, 2)

    def columns(t, way):
        return pl.ds(0, cuts[t]) if way == 0 else pl.ds(cuts[t], ins[t].shape[-1] - cuts[t])

    def block(t, way, step):
        at = place + 2 * chips - 2 - step if way == 0 else place + 2 + step
        return ins[t].at[chip_at(at, chips), :, columns(t, way)]

    def copy(t, way, step, source):
        return pltpu.make_async_remote_copy(
            src_ref=source,
            dst_ref=slots[t][way].at[step],
            send_sem=send_sem.at[t, way, step],
            recv_sem=recv_sem.at[t, way, step],
            device_id=devices[way],
            device_id_type=MESH,
        )

    pairs = [(t, way) for t in range(count) for way in (0, 1)]
    for t, way in pairs:
        copy(t, way, 0, block(t, way, -1)).start()

    def hop(step, carry):
        for t, way in pairs:
            slot = slots[t][way].at[step - 1]
            copy(t, way, step - 1, slot).wait_recv()
            own = block(t, way, step - 1)[...].astype(jnp.float32)
            slot[...] = (slot[...].astype(jnp.float32) + own).astype(jnp.bfloat16)
            copy(t, way, step, slot).start()
        return carry

    lax.fori_loop(1, chips - 1, hop, 0)
    last = chips - 2
    for t, way in pairs:
        slot = slots[t][way].at[last]
        copy(t, way, last, slot).wait_recv()
        total = slot[...].astype(jnp.float32) + block(t, way, last)[...].astype(jnp.float32)
        outs[t][:, columns(t, way)] = total.astype(outs[t].dtype)

    def finish(step, carry):
        for t, way in pairs:
            copy(t, way, step, slots[t][way].at[step]).wait_send()
        return carry

    lax.fori_loop(0, chips - 1, finish, 0)


def ring_scatter(totals):
    chips = lax.axis_size("chip")
    cuts = [-(-total.shape[2] // (2 * LANES)) * LANES for total in totals]
    vmem = pl.BlockSpec(memory_space=pltpu.VMEM)
    slots = []
    for total, cut in zip(totals, cuts):
        for width in (cut, total.shape[2] - cut):
            slots.append(pltpu.VMEM((chips - 1, total.shape[1], width), jnp.bfloat16))
    return pl.pallas_call(
        functools.partial(ring_kernel, cuts),
        in_specs=[vmem] * len(totals),
        out_specs=[vmem] * len(totals),
        out_shape=[jax.ShapeDtypeStruct(total.shape[1:], jnp.float32) for total in totals],
        scratch_shapes=slots
        + [
            pltpu.SemaphoreType.DMA((len(totals), 2, chips - 1)),
            pltpu.SemaphoreType.DMA((len(totals), 2, chips - 1)),
        ],
        compiler_params=pltpu.CompilerParams(
            collective_id=1, has_side_effects=True, vmem_limit_bytes=VMEM_LIMIT
        ),
        cost_estimate=pl.CostEstimate(
            flops=0, bytes_accessed=sum(8 * total.size for total in totals), transcendentals=0
        ),
        name="ring_scatter",
    )(*totals)


def meet(one, two, bit, send):
    kept, given = jnp.where(bit == 0, one, two), jnp.where(bit == 0, two, one)
    return kept.astype(jnp.float32) + send(given).astype(jnp.float32)


def halve_dp(total):
    columns = total.shape[-1] // 2
    return meet(total[..., :columns], total[..., columns:], lax.axis_index("dp"), swap)


def split_lanes(array):
    half = array.shape[1] // 2
    return jnp.concatenate([pad_lanes(array[:, :half]), pad_lanes(array[:, half:])], axis=1)


def pad_lanes(array):
    columns = array.shape[1]
    return jnp.pad(array, ((0, 0), (0, -columns % LANES)))


def repack_kernel(count, source, target, start, keep, in_ref, out_ref):
    rows = in_ref.shape[0]
    pieces = []
    for block in range(count):
        at = block * source + start
        pieces.append(in_ref[:, at : at + keep].astype(jnp.float32))
        if target > keep:
            pieces.append(jnp.zeros((rows, target - keep), jnp.float32))
    out_ref[...] = jnp.concatenate(pieces, axis=1).astype(out_ref.dtype)


def repack(array, count, source, target, start=0, keep=None):
    keep = min(source, target) if keep is None else keep
    rows = array.shape[0]
    if source == target and keep == source:
        return array
    step = 64 if rows % 64 == 0 else rows
    return pl.pallas_call(
        functools.partial(repack_kernel, count, source, target, start, keep),
        grid=(rows // step,),
        in_specs=[pl.BlockSpec((step, count * source), lambda r: (r, 0))],
        out_specs=pl.BlockSpec((step, count * target), lambda r: (r, 0)),
        out_shape=jax.ShapeDtypeStruct((rows, count * target), array.dtype),
        compiler_params=params(),
        name="repack",
    )(array)


def weave_kernel(count, source, keep, one_ref, two_ref, out_ref):
    pieces = []
    for block in range(count):
        for ref in (one_ref, two_ref):
            pieces.append(ref[:, block * source : block * source + keep].astype(jnp.float32))
    out_ref[...] = jnp.concatenate(pieces, axis=1)


def weave(one, two, count, source, keep):
    rows = one.shape[0]
    return pl.pallas_call(
        functools.partial(weave_kernel, count, source, keep),
        out_shape=jax.ShapeDtypeStruct((rows, 2 * count * keep), jnp.float32),
        compiler_params=pltpu.CompilerParams(vmem_limit_bytes=VMEM_LIMIT),
        name="weave",
    )(one, two)


def convolve(extended, kernel, bias_row):
    length = extended.shape[0] - kernel.shape[1] + 1
    convolved = bias_row
    for offset in range(kernel.shape[1]):
        convolved = convolved + kernel[:, offset] * extended[offset : offset + length, :]
    return convolved


def decay_rates(decay_wide):
    return -jnp.exp(decay_wide.T)


def gating(scanned, gate_path):
    return scanned * silu_gate(gate_path)


def activate(gate_pre, up_pre):
    return silu_gate(gate_pre) * up_pre


def dot(left, right):
    return jnp.dot(left, right, preferred_element_type=jnp.float32)


def dot_rows(left, right):
    return lax.dot_general(left, right, (((0,), (0,)), ((), ())), preferred_element_type=jnp.float32)


def dot_columns(left, right):
    return lax.dot_general(left, right, (((1,), (1,)), ((), ())), preferred_element_type=jnp.float32)


def combine_paths(attended, mamba_path, attention_row, mamba_row):
    return jnp.concatenate(
        [
            rms_norm(attended, attention_row, attended.shape[-1]),
            rms_norm(mamba_path, mamba_row, mamba_path.shape[-1]),
        ],
        axis=-1,
    )


def shards(
    tokens,
    cotangent,
    input_gain,
    merged_weight,
    meta_tokens,
    select_weight,
    step_weight,
    decay_log,
    conv_weight,
    conv_bias,
    step_bias,
    skip_gain,
    attention_gain,
    mamba_gain,
    output_weight,
    second_gain,
    expand_weight,
    down_weight,
):
    parts = lax.axis_size("chip") * lax.axis_size("core")
    position = lax.axis_index(SEQ)
    first = lax.axis_index("dp") == 0
    tokens = tokens[0]
    cotangent = cotangent[0]
    local_len, width = tokens.shape
    query_width = HEADS * HEAD
    key_width = KVHEADS * HEAD
    inner_start = query_width + 2 * key_width
    half = merged_weight.shape[1]
    reach_count = (WINDOW - 1) // local_len + 1
    rows_in = merged_weight.shape[0]
    rows_pad = ceil8(rows_in)
    rows_channel = select_weight.shape[0]
    channel_pad = ceil8(rows_channel)
    rows_joined = output_weight.shape[0]
    joined_pad = ceil8(rows_joined)
    rows_hidden = down_weight.shape[0]
    hidden_half = rows_hidden // 2
    hidden_pad = ceil8(hidden_half)
    hidden_width = parts * hidden_pad
    wide = lambda row: row.astype(jnp.float32)
    conv_bias_wide = wide(conv_bias)
    step_bias_wide = wide(step_bias)
    skip_wide = wide(skip_gain)[None]
    input_row, second_row = wide(input_gain), wide(second_gain)
    attention_row, mamba_row = wide(attention_gain), wide(mamba_gain)

    columns = [weight.shape[1] for weight in (select_weight, step_weight, decay_log, conv_weight)]
    small = jnp.concatenate([select_weight, step_weight, decay_log, conv_weight], axis=1)
    small = jnp.pad(small, ((0, channel_pad - rows_channel), (0, LANES - sum(columns))))
    meta_part = jnp.pad(
        meta_tokens, ((0, rows_pad - rows_in), (0, LANES - meta_tokens.shape[1]))
    )
    small = jnp.concatenate([small, meta_part], axis=0)
    expand_rows = pad_rows(expand_weight, rows_pad)
    expand_halves = [
        repack(expand_rows, parts, rows_hidden, hidden_pad, at, hidden_half)
        for at in (0, hidden_half)
    ]
    down_halves = [
        pad_rows(down_weight[:hidden_half], hidden_pad),
        pad_rows(down_weight[hidden_half:], hidden_pad),
    ]
    cut = output_weight.shape[1]
    merged_full, output_full, small_full, expand_got, down_got, cotangent_got = gather_everywhere(
        [
            pad_lanes(pad_rows(merged_weight, rows_pad)),
            pad_lanes(pad_rows(output_weight, joined_pad)),
            small,
        ],
        (17 * LANES, 4 * LANES, LANES),
        [
            jnp.where(first, expand_halves[1], expand_halves[0]),
            jnp.where(first, down_halves[1], down_halves[0]),
            cotangent,
        ],
    )
    merged_full = merged_full.reshape(2, parts * rows_pad, -1)
    output_full = output_full.reshape(2, parts * joined_pad, -1)
    small_full = small_full.reshape(2, parts, channel_pad + rows_pad, LANES)
    kept = jnp.where(first, expand_halves[0], expand_halves[1])
    expand_mine = jnp.concatenate(
        [jnp.where(first, kept, expand_got), jnp.where(first, expand_got, kept)], axis=1
    )
    kept = jnp.where(first, down_halves[0], down_halves[1])
    down_mine = jnp.concatenate(
        [jnp.where(first, kept, down_got), jnp.where(first, down_got, kept)], axis=1
    )
    small_full, merged_full, expand_mine, down_mine = lax.optimization_barrier(
        (small_full, merged_full, expand_mine, down_mine)
    )
    expand_full = lax.all_gather(expand_mine, SEQ).reshape(parts * rows_pad, 2 * hidden_width)
    down_full = lax.all_gather(down_mine, SEQ).reshape(hidden_width, width)
    cotangent_both = jnp.concatenate([cotangent, cotangent_got], axis=0)
    channel_rows = [part[:, :rows_channel].reshape(MINNER, LANES) for part in small_full]
    pieces, at = [], 0
    for count in columns:
        pieces.append(jnp.concatenate([channel_rows[h][:, at : at + count] for h in (0, 1)], axis=1))
        at += count
    select_full, step_full, decay_full, kernel_full = pieces
    meta_full = jnp.concatenate(
        [
            small_full[h][:, channel_pad:, : meta_tokens.shape[1]].reshape(
                parts * rows_pad, meta_tokens.shape[1]
            )
            for h in (0, 1)
        ],
        axis=1,
    )

    tokens_wide = wide(tokens)
    normed_wide, norm_back = jax.vjp(lambda v, g: rms_norm(v, g, width), tokens_wide, input_row)
    normed = repack(normed_wide.astype(jnp.bfloat16), parts, rows_in, rows_pad)
    input_row_pad = jnp.pad(
        input_row.reshape(parts, rows_in), ((0, 0), (0, rows_pad - rows_in))
    ).reshape(parts * rows_pad)
    meta_wide, meta_back = jax.vjp(
        lambda v, g: rms_norm(v, g, width), wide(meta_full).T, input_row_pad
    )
    stacked_normed = jnp.concatenate([normed, meta_wide.astype(jnp.bfloat16)], axis=0)
    projected_one = dot(stacked_normed, merged_full[0])
    projected_two = dot(normed, merged_full[1])
    queries = projected_one[:local_len, :query_width].astype(jnp.bfloat16)
    pairs_own = projected_one[:local_len, query_width:inner_start].astype(jnp.bfloat16)
    meta_pairs = projected_one[local_len:, query_width:inner_start].astype(jnp.bfloat16)
    inner_path = jnp.concatenate(
        [
            projected_one[:local_len, inner_start:half].astype(jnp.bfloat16),
            projected_two[:, : inner_start + MINNER - half].astype(jnp.bfloat16),
        ],
        axis=1,
    )
    gate_path = projected_two[:, inner_start + MINNER - half : half]

    pairs = jnp.concatenate(
        [meta_pairs]
        + [from_behind(pairs_own, behind) for behind in range(reach_count, 0, -1)]
        + [pairs_own],
        axis=0,
    )
    where = jnp.reshape(position, (1,)).astype(jnp.int32)
    heads_first = lambda rows: jnp.moveaxis(rows.reshape(rows.shape[0], KVHEADS, HEAD), 1, 0)
    keys, values = heads_first(pairs[:, :key_width]), heads_first(pairs[:, key_width:])
    key_turned, value_turned = pairs[:, :key_width].T, pairs[:, key_width:].T
    query_turned = queries.T
    attended_turned, logs = attend(where, query_turned, keys, value_turned, reach_count + 1)
    attended = attended_turned.T

    previous = from_behind(inner_path[local_len - (CONV - 1) :], 1)
    extended = wide(jnp.concatenate([previous, inner_path], axis=0))
    kernel = wide(kernel_full)
    convolved, convolve_back = jax.vjp(convolve, extended, kernel, conv_bias_wide)
    activated, silu_back = jax.vjp(silu_gate, convolved)
    signal = activated.astype(jnp.bfloat16)
    selected = dot(signal, select_full)
    step_raw = selected[:, :DTR].astype(jnp.bfloat16)
    spread_lanes = lambda mix: jnp.broadcast_to(mix[:, :, None], (local_len, STATE, LANES))
    write_wide = spread_lanes(selected[:, DTR : DTR + STATE])
    read_wide = spread_lanes(selected[:, DTR + STATE :])
    step_pre = dot_columns(step_raw, step_full) + step_bias_wide
    step_size = softplus(step_pre)
    decays, decay_back = jax.vjp(decay_rates, wide(decay_full))
    ends = scan_ends(step_size, signal, write_wide, decays)
    ends, expand_full = lax.optimization_barrier((ends, expand_full))
    carried = lax.all_gather(
        jnp.concatenate([ends, jnp.sum(step_size, axis=0, keepdims=True)], axis=0), SEQ
    )
    totals = carried[:, STATE:]
    scanned, enter = scan_forward(
        where, step_size, signal, write_wide, read_wide, decays, skip_wide, totals, carried[:, :STATE]
    )
    mamba_path, gating_back = jax.vjp(gating, scanned, gate_path)
    joined_wide, paths_back = jax.vjp(
        combine_paths, attended, mamba_path, attention_row, mamba_row
    )
    joined = repack(joined_wide.astype(jnp.bfloat16), parts, rows_joined, joined_pad)
    hidden = tokens_wide + 0.5 * jnp.concatenate(
        [dot(joined, output_full[0])[:, :cut], dot(joined, output_full[1])[:, :cut]], axis=1
    )

    normed_two_wide, norm_two_back = jax.vjp(lambda v, g: rms_norm(v, g, width), hidden, second_row)
    normed_two = repack(normed_two_wide.astype(jnp.bfloat16), parts, rows_in, rows_pad)
    normed_both = jnp.concatenate([normed_two, swap(normed_two)], axis=0)
    expanded = dot(normed_both, expand_full)
    active_wide, activate_back = jax.vjp(
        activate, expanded[:, :hidden_width], expanded[:, hidden_width:]
    )
    active = active_wide.astype(jnp.bfloat16)
    down_out = dot(active, down_full)
    block_output = (
        hidden + down_out[:local_len] + wide(swap(down_out[local_len:].astype(jnp.bfloat16)))
    ).astype(jnp.bfloat16)

    hidden_columns = parity_columns(active, parts, hidden_pad)
    down_grad = grad_parts(hidden_columns, pad_lanes(cotangent_both))
    down_sum = scatter_rows(down_grad, hidden_pad)
    active_grad = dot_columns(cotangent_both, down_full)
    gate_grad, up_grad = activate_back(active_grad)
    expand_in = jnp.concatenate(
        [gate_grad.astype(jnp.bfloat16), up_grad.astype(jnp.bfloat16)], axis=1
    )
    second_both = dot_columns(expand_in, expand_full)
    second_normed_grad = repack(
        second_both[:local_len] + wide(swap(second_both[local_len:].astype(jnp.bfloat16))),
        parts,
        rows_pad,
        rows_in,
    )
    hidden_part, second_gain_grad = norm_two_back(second_normed_grad)
    hidden_grad = hidden_part + wide(cotangent)
    mixed_in = hidden_grad.astype(jnp.bfloat16)
    mixed_split = split_lanes(mixed_in)
    cut_pad = mixed_split.shape[1] // 2
    joined_grad = repack(
        0.5
        * (
            dot_columns(mixed_split[:, :cut_pad], output_full[0])
            + dot_columns(mixed_split[:, cut_pad:], output_full[1])
        ),
        parts,
        joined_pad,
        rows_joined,
    )
    attended_grad, mamba_grad, attention_gain_grad, mamba_gain_grad = paths_back(joined_grad)
    scanned_grad, gate_path_grad = gating_back(mamba_grad)
    own_pull = scan_pulls(step_size, scanned_grad, read_wide, decays)
    pulls = lax.all_gather(own_pull, SEQ)

    normed_both, joined, own_pull, down_sum = lax.optimization_barrier(
        (normed_both, joined, own_pull, down_sum)
    )
    both_split = parity_columns(normed_both, parts, rows_pad)
    gate_total = grad_parts(both_split, expand_in[:, :hidden_width])
    up_total = grad_parts(both_split, expand_in[:, hidden_width:])
    output_grad = grad_parts(parity_columns(joined, parts, joined_pad), mixed_split, 0.5)
    attended_in, gate_total, up_total, output_grad, pulls = lax.optimization_barrier(
        (attended_grad.astype(jnp.bfloat16), gate_total, up_total, output_grad, pulls)
    )
    gate_sum = scatter_rows(gate_total, rows_pad)
    up_sum = scatter_rows(up_total, rows_pad)
    output_grad = halve_dp(output_grad).astype(jnp.bfloat16)
    output_sum = scatter_rows(output_grad, joined_pad)

    query_grad_turned, key_grads, value_grads = attend_back(
        where,
        query_turned,
        attended_in.T,
        attended_turned,
        logs,
        keys,
        values,
        key_turned,
        reach_count + 1,
    )
    heads_last = lambda grads: jnp.moveaxis(grads, 0, 1).reshape(grads.shape[1], key_width)
    pair_grads = jnp.concatenate([heads_last(key_grads), heads_last(value_grads)], axis=1)
    meta_pair_grad, window_grad = pair_grads[:META], pair_grads[META:]
    own_grad = window_grad[reach_count * local_len :]
    for behind in range(1, reach_count + 1):
        own_grad = own_grad + wide(
            from_behind(
                window_grad[
                    (reach_count - behind) * local_len : (reach_count - behind + 1) * local_len
                ].astype(jnp.bfloat16),
                -behind,
            )
        )

    own_grad, meta_pair_grad, gate_sum = lax.optimization_barrier(
        (own_grad, meta_pair_grad, gate_sum)
    )
    with_meta = lambda rows, meta: jnp.concatenate([rows, meta], axis=0)
    query_in = with_meta(query_grad_turned.T, jnp.zeros((META, query_width), jnp.bfloat16))
    pair_in = with_meta(own_grad, meta_pair_grad).astype(jnp.bfloat16)
    gate_in = with_meta(gate_path_grad.astype(jnp.bfloat16), jnp.zeros((META, MINNER), jnp.bfloat16))
    normed_split = parity_columns(stacked_normed, parts, rows_pad)
    early_grad = grad_parts(
        normed_split, pad_lanes(jnp.concatenate([gate_in, query_in, pair_in], axis=1))
    )
    scanned_grad, early_grad = lax.optimization_barrier((scanned_grad, early_grad))
    gate_early = early_grad[:, :MINNER]
    pair_early = jnp.pad(
        early_grad[:, MINNER : MINNER + inner_start], ((0, 0), (0, MINNER - inner_start))
    )
    early_grad = meet(pair_early, gate_early, lax.axis_index("dp"), swap).astype(jnp.bfloat16)
    signal_grad, step_grad, write_parts, read_parts, decays_grad, skip_parts = scan_backward(
        where,
        step_size,
        signal,
        scanned_grad,
        write_wide,
        read_wide,
        decays,
        skip_wide,
        enter,
        totals,
        pulls,
    )
    step_grad, up_sum = lax.optimization_barrier((step_grad, up_sum))
    step_pre_grad = step_grad * jax.nn.sigmoid(step_pre)
    step_in = step_pre_grad.astype(jnp.bfloat16)
    step_weight_grad = dot_rows(step_in, step_raw)
    selected_in = jnp.concatenate(
        [dot(step_in, step_full), jnp.sum(write_parts, axis=-1), jnp.sum(read_parts, axis=-1)],
        axis=-1,
    ).astype(jnp.bfloat16)
    select_grad = dot_rows(signal, selected_in)
    signal_grad = signal_grad + dot_columns(selected_in, select_full)
    extended_grad, kernel_grad, conv_bias_grad = convolve_back(silu_back(signal_grad)[0])
    returned_tail = wide(from_behind(extended_grad[: CONV - 1].astype(jnp.bfloat16), -1))
    inner_grad = extended_grad[CONV - 1 :] + jnp.pad(
        returned_tail, ((local_len - (CONV - 1), 0), (0, 0))
    )
    decay_grad = decay_back(decays_grad)[0]

    inner_in = with_meta(inner_grad.astype(jnp.bfloat16), jnp.zeros((META, MINNER), jnp.bfloat16))
    inner_in, output_sum = lax.optimization_barrier((inner_in, output_sum))
    inner_cut = half - inner_start
    inner_first = -(-inner_cut // LANES) * LANES
    inner_grads = grad_parts(
        normed_split,
        jnp.concatenate([pad_lanes(inner_in[:, :inner_cut]), pad_lanes(inner_in[:, inner_cut:])], axis=1),
    )
    one_in = pad_lanes(jnp.concatenate([query_in, pair_in, inner_in[:, :inner_cut]], axis=1))
    two_in = pad_lanes(
        jnp.concatenate([inner_in[:local_len, inner_cut:], gate_in[:local_len]], axis=1)
    )
    stacked_grad = dot_columns(one_in, merged_full[0])
    normed_grad = repack(
        stacked_grad[:local_len] + dot_columns(two_in, merged_full[1]), parts, rows_pad, rows_in
    )
    meta_rows_grad, meta_gain_grad = meta_back(stacked_grad[local_len:])
    tokens_part, input_gain_part = norm_back(normed_grad)
    tokens_grad = hidden_grad + tokens_part
    input_gain_grad = input_gain_part + (
        meta_gain_grad.reshape(parts, rows_pad)[:, :rows_in].reshape(width)
    )

    count = meta_tokens.shape[1]
    meta_grads = jnp.pad(
        meta_rows_grad.T.reshape(parts, rows_pad, META),
        ((0, 0), (0, channel_pad - rows_pad), (0, 0)),
    )
    sides = []
    for h in (0, 1):
        cuts = [
            grad[:, h * size : (h + 1) * size]
            for grad, size in zip((select_grad, step_weight_grad, decay_grad, kernel_grad), columns)
        ]
        side = jnp.concatenate(cuts, axis=1).reshape(parts, rows_channel, sum(columns))
        side = jnp.pad(
            side, ((0, 0), (0, channel_pad - rows_channel), (0, LANES - sum(columns)))
        )
        meta_side = meta_grads[:, :, h * count : (h + 1) * count]
        sides += [side, jnp.pad(meta_side, ((0, 0), (0, 0), (0, LANES - count)))]
    small_grads = jnp.concatenate(sides, axis=2).astype(jnp.bfloat16)
    small_grads = small_grads.reshape(parts // 2, 2, channel_pad, 4 * LANES)
    small_sum = meet(
        small_grads[:, 0],
        small_grads[:, 1],
        lax.axis_index("core"),
        lambda array: swap(array, "core"),
    )
    inner_sum, early_out, small_sum = ring_scatter(
        [
            inner_grads.reshape(parts // 2, rows_pad, -1),
            early_grad.reshape(parts // 2, rows_pad, -1),
            small_sum.astype(jnp.bfloat16),
        ]
    )
    output_out = wide(output_sum)[:rows_joined, :cut]
    early_out = early_out[:rows_in]
    small_sum = halve_dp(small_sum)
    inner_one, inner_two = inner_sum[:, :inner_first], inner_sum[:, inner_first:]
    inner_two = jnp.pad(inner_two, ((0, 0), (0, inner_first - inner_two.shape[1])))
    inner_out = meet(
        inner_one, inner_two, lax.axis_index("dp"), lambda array: swap(array.astype(jnp.bfloat16))
    )[:rows_in]
    small_outs, at = [], 0
    for size in columns:
        small_outs.append(small_sum[:rows_channel, at : at + size])
        at += size
    meta_sum = small_sum[:rows_in, LANES : LANES + count]

    vectors = (
        second_gain_grad,
        attention_gain_grad,
        mamba_gain_grad,
        jnp.sum(skip_parts, axis=0),
        jnp.sum(step_pre_grad, axis=0),
        conv_bias_grad,
        input_gain_grad,
    )
    flat = jnp.concatenate(vectors)
    padded = -(-flat.shape[0] // (8 * LANES)) * 8 * LANES
    flat = sum_everywhere(jnp.pad(flat, (0, padded - flat.shape[0])).reshape(-1, LANES))
    flat = flat.reshape(-1)
    sums, at = [], 0
    for vector in vectors:
        sums.append(flat[at : at + vector.shape[0]])
        at += vector.shape[0]

    rest = half - MINNER
    merged_out = jnp.where(
        first,
        jnp.concatenate([early_out[:, :inner_start], inner_out[:, :inner_cut]], axis=1),
        jnp.concatenate([inner_out[:, :rest], early_out], axis=1),
    )
    gate_part, up_part = gate_sum, up_sum
    kept = jnp.where(first, gate_part, up_part)
    got = swap(jnp.where(first, up_part, gate_part))
    expand_out = weave(
        jnp.where(first, kept, got), jnp.where(first, got, kept), parts, hidden_pad, hidden_half
    )[:rows_in]
    kept = jnp.where(first, down_sum[:, :cut], down_sum[:, cut : 2 * cut])
    got = swap(jnp.where(first, down_sum[:, cut : 2 * cut], down_sum[:, :cut]))
    down_out_grad = jnp.concatenate(
        [
            jnp.where(first, kept, got)[:hidden_half],
            jnp.where(first, got, kept)[:hidden_half],
        ],
        axis=0,
    )
    return (
        block_output[None],
        tokens_grad[None],
        sums[6],
        merged_out,
        meta_sum,
        small_outs[0],
        small_outs[1],
        small_outs[2],
        small_outs[3],
        sums[5],
        sums[4],
        sums[3],
        sums[1],
        sums[2],
        output_out,
        sums[0],
        expand_out,
        wide(down_out_grad),
    )


def solution(mesh):
    split = Mesh(mesh.devices.reshape(2, -1, 2), ALL)
    rows, matrix, copied = P("dp", SEQ, None), P(SEQ, "dp"), P()
    return jax.shard_map(
        shards,
        mesh=split,
        in_specs=(rows, rows, copied) + (matrix,) * 6 + (copied,) * 5 + (matrix, copied, matrix, matrix),
        out_specs=(rows, rows, copied) + (matrix,) * 6 + (copied,) * 5 + (matrix, copied, matrix, matrix),
        check_vma=False,
    )
```

time: 4590 us -> 1480 us (0.32)
  blocking collectives: 2140 us -> 0 us
  other arithmetic: 880 us -> 135 us
  Pallas kernels: 0 us -> 620 us
  local copies, waits for them, and re-layouts: 591 us -> 167 us
  matrix products: 403 us -> 230 us
  waiting for transfers between devices: 388 us -> 252 us
  starting transfers between devices: 112 us -> 49.8 us
    unnamed x6 -> x0, blocking collectives: 1980 us -> none
    pallas_call x0 -> x21, Pallas kernels: none -> 620 us  [the longest x1 251 us: gather_everywhere(): pl.pallas_call(functools.partial(gather_kernel, cuts, len(others)), in_sp...]
    reduce_sum x562 -> x14, other arithmetic: 459 us -> 28.4 us  [the longest x5 14.3 us: rms_norm(): return values * lax.rsqrt(mean + epsilon) * gain_row]
    dynamic_update_slice x773 -> x0, other arithmetic: 254 us -> none  [the longest x256 234 us: local_scan(): final_state, outputs = lax.scan(jax.checkpoint(run_block), initial, pieces)]
    unnamed x232 -> x357, local copies, waits for them, and re-layouts: 224 us -> 35.9 us
    dot_general x91 -> x30, matrix products: 401 us -> 230 us  [the longest x14 88.5 us: dot_rows(): lax.dot_general(left, right, (((0,), (0,)), ((), ())), preferred_element_...]
    all_gather x11 -> x0, blocking collectives: 156 us -> none  [the longest x2 50.1 us: spread(): lax.all_gather(halves[2], 'seq', axis=0, tiled=True)]
    ppermute x10 -> x31, waiting for transfers between devices: 30.6 us -> 179 us  [the longest x18 173 us: swap(): return lax.ppermute(array, axis, [(0, 1), (1, 0)])]
where the time goes in v1:
time: 1480 us; the launch traced here: 1470 us
  Pallas kernels  620 us (42%)
  waiting for transfers between devices  252 us (17%)
  matrix products  230 us (16%)
  local copies, waits for them, and re-layouts  167 us (11%)
  other arithmetic  135 us (9%)
  starting transfers between devices  49.8 us (3%)
  between operations  16.8 us (1%)
    pallas_call x1, Pallas kernels, gather_everywhere(): pl.pallas_call(functools.partial(gather_kernel, cuts, len(others)), in_sp...  251 us
    ppermute x18, waiting for transfers between devices, swap(): return lax.ppermute(array, axis, [(0, 1), (1, 0)])  173 us
    pallas_call x1, Pallas kernels, ring_scatter(): pl.pallas_call(functools.partial(ring_kernel, cuts), in_specs=[vmem] * le...  136 us
    dot_general x14, matrix products, dot_rows(): lax.dot_general(left, right, (((0,), (0,)), ((), ())), preferred_element_...  88.5 us
    dot_general x8, matrix products, dot_columns(): lax.dot_general(left, right, (((1,), (1,)), ((), ())), preferred_element_...  84.9 us
    pallas_call x1, Pallas kernels, scan_backward(): pl.pallas_call(scan_back_kernel, grid=(channels // chunk,), in_specs=[pl....  58.4 us
    dot_general x8, matrix products, dot(): return jnp.dot(left, right, preferred_element_type=jnp.float32)  56.6 us
    pallas_call x1, Pallas kernels, attend_back(): pl.pallas_call(functools.partial(attend_back_kernel, count), grid=(KVHEAD...  42.6 us
  transfers between devices with their start and end apart: 39, of which 16 were waited for; matrix products, arithmetic and copies ran while one was open for 32% of the time, Pallas kernels for 24%

profile of v1, /device:TPU:0, one launch (start us, length us, event | category | flops | bytes accessed | tf_op | source)
XLA Modules:
  0.0 1471.7 jit_solution(12872864974048642040)
XLA Ops:
  23.8 251.0 %gather_everywhere.1 = (bf16[2,8,2,104,4352]{4,3,2,1,0:T(8,128)(2,1)}, bf16[2,8,2,304,896]{4,3,2,1,0:T(8,128)(2,1)}, bf16[2,8,2,304,128]{4,3,2,1,0:T(8,128)(2,1)...) custom-call(bf16[104,4352]{1,0:T(8,128)(2,1)} %pad.242.refs_0_, ...), custom_call_target="tpu_custom_call" | custom-call | bytes 293339136 | tf_op jit(solution)/shard_map/gather_everywhere/pallas_call | solution.py:693
  285.6 8.6 fusion.2
  301.4 10.1 fusion.16
  335.9 6.1 fusion.142
  343.9 14.5 scan_ends.1
  358.4 20.0 %all-gather.10.cloned.1.call-done = bf16[1664,5632]{1,0:T(8,128)(2,1)} async-done(((bf16[104,5632]{1,0:T(8,128)(2,1)}), bf16[1664,5632]{1,0:T(8,128)(2,1)}) %all-gather.10.cloned.1.call-update) | async-done | bytes 18743312 | tf_op jit(solution)/shard_map/all_gather | solution.py:999
  394.3 11.8 fusion.148
  424.4 19.1 %attend.1 = (f32[1600,256]{1,0:T(8,128)}, f32[5,8,256]{2,1,0:T(8,128)}) custom-call(s32[1]{0:T(128)} %bitcast.1.position_ref, bf16[1600,256]{1,0:T(8,128)(2,1)} %copy.183.query_ref, bf16[5,1408,64]{2,1,0:T(8,128)(2,1)} %bitcast.207, bf16[320,1408]{1,0:T(8,128)(2,1)} %copy.184.value_ref), custom_call_target="tpu_custom_call" | custom-call | tf_op jit(solution)/shard_map/attend/pallas_call | solution.py:424
  454.9 28.3 %scan_forward.1 = (f32[256,3200]{1,0:T(8,128)}, f32[16,3200]{1,0:T(8,128)}) custom-call(s32[1]{0:T(128)} %bitcast.1.position_ref, f32[256,3200]{1,0:T(8,128)} %get-tuple-element.235.step_ref, bf16[256,3200]{1,0:T(8,128)(2,1)} %copy-done.8, f32[256,16,128]{2,1,0:T(8,128)} %broadcast_in_dim.32.write_ref, f32[256,16,128]{2,1,0:T(8,128)} %broadcast_in_dim.66.read_ref, ...), custom_call_target="tpu_custom_call" | custom-call | tf_op jit(solution)/shard_map/scan_forward/pallas_call | solution.py:281
  495.9 7.2 fusion.12
  517.1 17.3 %collective-permute-done.5 = bf16[256,1664]{1,0:T(8,128)(2,1)S(1)} collective-permute-done((bf16[256,1664]{1,0:T(8,128)(2,1)}, bf16[256,1664]{1,0:T(8,128)(2,1)S(1)}, u32[]{:S(2)}, u32[]{:S(2)}) %collective-permute-start.5) | collective-permute-done | bytes 852000 | tf_op jit(solution)/shard_map/ppermute | solution.py:475
  535.3 17.1 %fusion.144 = f32[512,5632]{1,0:T(8,128)} fusion(bf16[1664,5632]{1,0:T(8,128)(2,1)} %all-gather.10.cloned.1.call-done, bf16[256,1664]{1,0:T(8,128)(2,1)S(1)} %collective-permute-done.5, bf16[256,1664]{1,0:T(8,128)(2,1)S(1)} %copy-done.55), kind=kOutput, calls=%fused_computation.311 | convolution fusion | flops 9599975424 | bytes 31981568 | tf_op jit(solution)/shard_map/dot_general | solution.py:886
  552.4 14.0 fusion.22
  566.4 6.6 parity_columns.4
  578.0 7.8 collective-permute-done.8
  591.0 18.1 %fusion.23 = f32[512,1664]{1,0:T(8,128)} fusion(bf16[1664,5632]{1,0:T(8,128)(2,1)} %all-gather.10.cloned.1.call-done, bf16[512,2816]{1,0:T(8,128)(2,1)} %get-tuple-element.226, bf16[512,2816]{1,0:T(8,128)(2,1)} %get-tuple-element.225), kind=kOutput, calls=%fused_computation.35 | convolution fusion | flops 9608101888 | bytes 27918336 | tf_op jit(solution)/shard_map/dot_general | solution.py:894
  615.2 16.7 %collective-permute-done.7 = bf16[256,1664]{1,0:T(8,128)(2,1)S(1)} collective-permute-done((bf16[256,1664]{1,0:T(8,128)(2,1)S(1)}, bf16[256,1664]{1,0:T(8,128)(2,1)S(1)}, u32[]{:S(2)}, u32[]{:S(2)}) %collective-permute-start.7) | collective-permute-done | bytes 852000 | tf_op jit(solution)/shard_map/ppermute | solution.py:475
  649.2 6.4 fusion.19.in_ref
  665.5 6.6 fusion.68
  672.1 13.4 scan_pulls.1
  685.5 11.7 reduce-scatter.5.cloned.1.call-done
  701.9 7.1 multiply_convert_fusion
  709.0 6.1 parity_columns.5
  715.1 7.0 convolution_convert_fusion.4
  732.9 7.3 add_convert_fusion.5
  740.2 7.3 add_convert_fusion.4
  747.5 7.5 add_convert_fusion.1
  755.0 19.4 %all-gather.14.cloned.1.call-done = f32[256,3200]{1,0:T(8,128)} async-done(((f32[16,3200]{1,0:T(8,128)}), f32[256,3200]{1,0:T(8,128)}) %all-gather.14.cloned.1.call-update) | async-done | bytes 3276816 | tf_op jit(solution)/shard_map/all_gather | solution.py:1134
  781.0 42.6 %attend_back.1 = (bf16[1600,256]{1,0:T(8,128)(2,1)}, f32[5,1408,64]{2,1,0:T(8,128)}, f32[5,1408,64]{2,1,0:T(8,128)}) custom-call(s32[1]{0:T(128)} %bitcast.1.position_ref, bf16[1600,256]{1,0:T(8,128)(2,1)} %copy.183.query_ref, bf16[1600,256]{1,0:T(8,128)(2,1)} %copy.199.grad_ref, f32[1600,256]{1,0:T(8,128)} %get-tuple-element.77.out_ref, ...), custom_call_target="tpu_custom_call" | custom-call | tf_op jit(solution)/shard_map/attend_back/pallas_call | solution.py:445
  862.1 21.3 %reduce-scatter.7.cloned.1.call-done = bf16[1,104,2816]{2,1,0:T(8,128)(2,1)} async-done(((bf16[8,104,2816]{2,1,0:T(8,128)(2,1)}), bf16[1,104,2816]{2,1,0:T(8,128)(2,1)}) %reduce-scatter.7.cloned.1.call-update) | async-done | bytes 585744 | tf_op jit(solution)/shard_map/reduce_scatter | solution.py:528
  884.6 7.9 concatenate.150
  892.5 10.8 convolution_convert_fusion
  907.5 8.2 fusion.157
  923.9 96.8 %collective-permute-done.6 = bf16[256,1600]{0,1:T(8,128)(2,1)S(1)} collective-permute-done((bf16[256,1600]{0,1:T(8,128)(2,1)}, bf16[256,1600]{0,1:T(8,128)(2,1)S(1)}, u32[]{:S(2)}, u32[]{:S(2)}) %collective-permute-start.6) | collective-permute-done | bytes 819232 | tf_op jit(solution)/shard_map/ppermute | solution.py:475
  1028.5 7.4 add_convert_fusion.7
  1037.1 13.4 add_convert_fusion
  1050.5 58.4 %scan_backward.1 = (f32[256,3200]{1,0:T(8,128)}, f32[256,3200]{1,0:T(8,128)}, f32[256,16,128]{2,1,0:T(8,128)}, f32[256,16,128]{2,1,0:T(8,128)}, f32[16,3200]{1,0:T(8,128)}, /*index=5*/f32[8,3200]{1,0:T(8,128)}) custom-call(s32[1]{0:T(128)} %bitcast.1.position_ref, f32[256,3200]{1,0:T(8,128)} %get-tuple-element.235.step_ref, bf16[256,3200]{1,0:T(8,128)(2,1)} %copy-done.8, ...), custom_call_target="tpu_custom_call" | custom-call | tf_op jit(solution)/shard_map/scan_backward/pallas_call | solution.py:303
  1118.4 9.4 multiply_reduce_fusion.3
  1139.1 7.5 pad_select_fusion
  1165.5 6.7 concatenate.153
  1172.3 13.9 fusion.4
  1188.3 11.5 fusion.46.in_ref
  1228.3 8.3 collective-permute-start.20
  1255.5 23.0 %collective-permute-done.23 = f32[144,128]{1,0:T(8,128)S(1)} collective-permute-done((f32[144,128]{1,0:T(8,128)S(1)}, f32[144,128]{1,0:T(8,128)S(1)}, u32[]{:S(2)}, u32[]{:S(2)}) %collective-permute-start.23) | collective-permute-done | bytes 73760 | tf_op jit(solution)/shard_map/ppermute | solution.py:475
  1284.3 8.6 add_convert_fusion.3
  1292.8 7.2 add_convert_fusion.2
  1300.1 136.4 %ring_scatter.1 = (f32[104,3328]{1,0:T(8,128)}, f32[104,3200]{1,0:T(8,128)}, f32[200,512]{1,0:T(8,128)}) custom-call(bf16[8,104,3328]{2,1,0:T(8,128)(2,1)} %bitcast.227, bf16[8,104,3200]{2,1,0:T(8,128)(2,1)} %bitcast.202, bf16[8,200,512]{2,1,0:T(8,128)(2,1)} %fusion.44.refs_2_), custom_call_target="tpu_custom_call" | custom-call | bytes 50003968 | tf_op jit(solution)/shard_map/ring_scatter/pallas_call | solution.py:779
  1448.2 6.2 collective-permute-done.28
  (648 shorter events, 375.2 us)
Async XLA Ops:
  7.2 371.2 %all-gather.10.cloned.1.call-start = ((), (), s32[]{:S(2)}) async-start(), calls=%async_computation.8 | async-start | bytes 19914752 | tf_op jit(solution)/shard_map/all_gather | solution.py:999
  279.4 167.4 %all-gather.16.cloned.1.call-start = ((), (), s32[]{:S(2)}) async-start(), calls=%async_computation.11 | async-start | bytes 5222400 | tf_op jit(solution)/shard_map/all_gather | solution.py:1072
  312.1 18.4 %collective-permute-start.4 = (bf16[3,3200]{1,0:T(4,128)(2,1)S(1)}, bf16[3,3200]{1,0:T(4,128)(2,1)S(1)}, u32[]{:S(2)}, u32[]{:S(2)}) collective-permute-start(bf16[3,3200]{1,0:T(4,128)(2,1)S(1)} %fusion.111), channel_id=1, source_target_pairs={{0,1},{1,2},{2,3},{3,4},{4,5},{5,6},{6,7},{7,8},{8,9},{9,10},{10,1... | collective-permute-start | bytes 57608 | tf_op jit(solution)/shard_map/ppermute | solution.py:471
  380.1 172.3 %all-gather.12.cloned.1.call-start = ((), (), s32[]{:S(2)}) async-start(), calls=%async_computation.9 | async-start | bytes 9957376 | tf_op jit(solution)/shard_map/all_gather | solution.py:1000
  380.8 316.5 %reduce-scatter.5.cloned.1.call-start = ((), (), s32[]{:S(2)}) async-start(), calls=%async_computation.4 | async-start | bytes 5271552 | tf_op jit(solution)/shard_map/reduce_scatter | solution.py:528
  382.0 29.0 %collective-permute-start = (bf16[256,640]{1,0:T(8,128)(2,1)S(1)}, bf16[256,640]{1,0:T(8,128)(2,1)S(1)}, u32[]{:S(2)}, u32[]{:S(2)}) collective-permute-start(bf16[256,640]{1,0:T(8,128)(2,1)S(1)} %slice.505), channel_id=1, source_target_pairs={{0,4},{1,5},{2,6},{3,7},{4,8},{5,9},{6,10},{7,11},{8,12},{9,13},{1... | collective-permute-start | bytes 983048 | tf_op jit(solution)/shard_map/ppermute | solution.py:471
  385.5 26.4 %collective-permute-start.1 = (bf16[256,640]{1,0:T(8,128)(2,1)S(1)}, bf16[256,640]{1,0:T(8,128)(2,1)S(1)}, u32[]{:S(2)}, u32[]{:S(2)}) collective-permute-start(bf16[256,640]{1,0:T(8,128)(2,1)S(1)} %slice.505), channel_id=1, source_target_pairs={{0,3},{1,4},{2,5},{3,6},{4,7},{5,8},{6,9},{7,10},{8,11},{9,12},{10... | collective-permute-start | bytes 983048 | tf_op jit(solution)/shard_map/ppermute | solution.py:471
  388.2 24.3 %collective-permute-start.2 = (bf16[256,640]{1,0:T(8,128)(2,1)S(1)}, bf16[256,640]{1,0:T(8,128)(2,1)S(1)}, u32[]{:S(2)}, u32[]{:S(2)}) collective-permute-start(bf16[256,640]{1,0:T(8,128)(2,1)S(1)} %slice.505), channel_id=1, source_target_pairs={{0,2},{1,3},{2,4},{3,5},{4,6},{5,7},{6,8},{7,9},{8,10},{9,11},{10,... | collective-permute-start | bytes 983048 | tf_op jit(solution)/shard_map/ppermute | solution.py:471
  391.8 21.5 %collective-permute-start.3 = (bf16[256,640]{1,0:T(8,128)(2,1)S(1)}, bf16[256,640]{1,0:T(8,128)(2,1)S(1)}, u32[]{:S(2)}, u32[]{:S(2)}) collective-permute-start(bf16[256,640]{1,0:T(8,128)(2,1)S(1)} %slice.505), channel_id=1, source_target_pairs={{0,1},{1,2},{2,3},{3,4},{4,5},{5,6},{6,7},{7,8},{8,9},{9,10},{10,1... | collective-permute-start | bytes 983048 | tf_op jit(solution)/shard_map/ppermute | solution.py:471
  410.9 34.6 %copy-start.98 = (f32[1600]{0:T(1024)}, f32[1600]{0:T(1024)S(1)}, u32[]{:S(2)}) copy-start(f32[1600]{0:T(1024)S(1)} %convert_element_type.263) | copy-start | bytes 19204
  410.9 229.6 %copy-start.94 = (f32[1600]{0:T(1024)}, f32[1600]{0:T(1024)S(1)}, u32[]{:S(2)}) copy-start(f32[1600]{0:T(1024)S(1)} %convert_element_type.271) | copy-start | bytes 19204
  506.6 133.9 %copy-start.114 = (f32[256]{0:T(256)}, f32[256]{0:T(256)S(1)}, u32[]{:S(2)}) copy-start(f32[256]{0:T(256)S(1)} %fusion.115) | copy-start | bytes 3076
  512.6 22.7 %copy-start.55 = (bf16[256,1664]{1,0:T(8,128)(2,1)S(1)}, bf16[256,1664]{1,0:T(8,128)(2,1)}, u32[]{:S(2)}) copy-start(bf16[256,1664]{1,0:T(8,128)(2,1)} %repack.12) | copy-start | bytes 2555908
  512.6 21.8 %collective-permute-start.5 = (bf16[256,1664]{1,0:T(8,128)(2,1)}, bf16[256,1664]{1,0:T(8,128)(2,1)S(1)}, u32[]{:S(2)}, u32[]{:S(2)}) collective-permute-start(bf16[256,1664]{1,0:T(8,128)(2,1)} %repack.12), channel_id=1, source_target_pairs={{0,16},{16,0},{1,17},{17,1},{2,18},{18,2},{3,19},{19,3},{4,20},{20... | collective-permute-start | bytes 2555912 | tf_op jit(solution)/shard_map/ppermute | solution.py:475
  578.0 7.9 collective-permute-start.8
  591.0 183.4 %all-gather.14.cloned.1.call-start = ((), (), s32[]{:S(2)}) async-start(), calls=%async_computation.10 | async-start | bytes 3481600 | tf_op jit(solution)/shard_map/all_gather | solution.py:1134
  609.1 22.8 %copy-start.67 = (f32[512,1664]{1,0:T(8,128)S(1)}, f32[512,1664]{1,0:T(8,128)}, u32[]{:S(2)}) copy-start(f32[512,1664]{1,0:T(8,128)} %fusion.23) | copy-start | bytes 10223620
  610.8 21.0 %collective-permute-start.7 = (bf16[256,1664]{1,0:T(8,128)(2,1)S(1)}, bf16[256,1664]{1,0:T(8,128)(2,1)S(1)}, u32[]{:S(2)}, u32[]{:S(2)}) collective-permute-start(bf16[256,1664]{1,0:T(8,128)(2,1)S(1)} %slice.728), channel_id=1, source_target_pairs={{0,16},{16,0},{1,17},{17,1},{2,18},{18,2},{3,19},{19,3},{4,20},{20... | collective-permute-start | bytes 2555912 | tf_op jit(solution)/shard_map/ppermute | solution.py:475
  709.0 38.4 %collective-permute-start.11 = (bf16[2432,1792]{1,0:T(8,128)(2,1)}, bf16[2432,1792]{1,0:T(8,128)(2,1)}, u32[]{:S(2)}, u32[]{:S(2)}) collective-permute-start(bf16[2432,1792]{1,0:T(8,128)(2,1)} %multiply_convert_fusion), channel_id=1, source_target_pairs={{0,1},{1,0},{2,3},{3,2},{4,5},{5,4},{6,7},{7,6},{8,9},{9,8},{10,11... | collective-permute-start | bytes 26148872 | tf_op jit(solution)/shard_map/ppermute | solution.py:475
  722.1 10.7 collective-permute-start.9
  727.4 12.8 collective-permute-start.10
  727.4 156.0 %reduce-scatter.7.cloned.1.call-start = ((), (), s32[]{:S(2)}) async-start(), calls=%async_computation.5 | async-start | bytes 5271552 | tf_op jit(solution)/shard_map/reduce_scatter | solution.py:528
  774.4 337.8 %reduce-scatter.9.cloned.1.call-start = ((), (), s32[]{:S(2)}) async-start(), calls=%async_computation.6 | async-start | bytes 5271552 | tf_op jit(solution)/shard_map/reduce_scatter | solution.py:528
  839.2 19.2 %collective-permute-start.15 = (bf16[256,640]{1,0:T(8,128)(2,1)}, bf16[256,640]{1,0:T(8,128)(2,1)}, u32[]{:S(2)}, u32[]{:S(2)}) collective-permute-start(bf16[256,640]{1,0:T(8,128)(2,1)} %get-tuple-element.239), channel_id=1, source_target_pairs={{4,0},{5,1},{6,2},{7,3},{8,4},{9,5},{10,6},{11,7},{12,8},{13,9},{1... | collective-permute-start | bytes 983048 | tf_op jit(solution)/shard_map/ppermute | solution.py:471
  840.5 17.9 %collective-permute-start.14 = (bf16[256,640]{1,0:T(8,128)(2,1)}, bf16[256,640]{1,0:T(8,128)(2,1)}, u32[]{:S(2)}, u32[]{:S(2)}) collective-permute-start(bf16[256,640]{1,0:T(8,128)(2,1)} %get-tuple-element.240), channel_id=1, source_target_pairs={{3,0},{4,1},{5,2},{6,3},{7,4},{8,5},{9,6},{10,7},{11,8},{12,9},{13... | collective-permute-start | bytes 983048 | tf_op jit(solution)/shard_map/ppermute | solution.py:471
  841.8 18.1 %collective-permute-start.13 = (bf16[256,640]{1,0:T(8,128)(2,1)}, bf16[256,640]{1,0:T(8,128)(2,1)}, u32[]{:S(2)}, u32[]{:S(2)}) collective-permute-start(bf16[256,640]{1,0:T(8,128)(2,1)} %get-tuple-element.241), channel_id=1, source_target_pairs={{2,0},{3,1},{4,2},{5,3},{6,4},{7,5},{8,6},{9,7},{10,8},{11,9},{12,... | collective-permute-start | bytes 983048 | tf_op jit(solution)/shard_map/ppermute | solution.py:471
  843.1 16.8 %collective-permute-start.12 = (bf16[256,640]{1,0:T(8,128)(2,1)}, bf16[256,640]{1,0:T(8,128)(2,1)}, u32[]{:S(2)}, u32[]{:S(2)}) collective-permute-start(bf16[256,640]{1,0:T(8,128)(2,1)} %get-tuple-element.238), channel_id=1, source_target_pairs={{1,0},{2,1},{3,2},{4,3},{5,4},{6,5},{7,6},{8,7},{9,8},{10,9},{11,1... | collective-permute-start | bytes 983048 | tf_op jit(solution)/shard_map/ppermute | solution.py:471
  856.2 28.4 %copy-start.27 = (bf16[384,1600]{1,0:T(8,128)(2,1)}, bf16[384,1600]{1,0:T(8,128)(2,1)S(1)}, u32[]{:S(2)}) copy-start(bf16[384,1600]{1,0:T(8,128)(2,1)S(1)} %concatenate.146) | copy-start | bytes 3686404
  856.2 305.6 %reduce-scatter.11.cloned.1.call-start = ((), (), s32[]{:S(2)}) async-start(), calls=%async_computation.7 | async-start | bytes 4902912 | tf_op jit(solution)/shard_map/reduce_scatter | solution.py:528
  903.3 132.7 %collective-permute-start.16 = (bf16[832,5504]{1,0:T(8,128)(2,1)}, bf16[832,5504]{1,0:T(8,128)(2,1)}, u32[]{:S(2)}, u32[]{:S(2)}) collective-permute-start(bf16[832,5504]{1,0:T(8,128)(2,1)} %convolution_convert_fusion), channel_id=1, source_target_pairs={{0,1},{1,0},{2,3},{3,2},{4,5},{5,4},{6,7},{7,6},{8,9},{9,8},{10,11... | collective-permute-start | bytes 27475976 | tf_op jit(solution)/shard_map/ppermute | solution.py:475
  906.0 122.5 %collective-permute-start.18 = (bf16[2432,896]{1,0:T(8,128)(2,1)}, bf16[2432,896]{1,0:T(8,128)(2,1)}, u32[]{:S(2)}, u32[]{:S(2)}) collective-permute-start(bf16[2432,896]{1,0:T(8,128)(2,1)} %broadcast_select_fusion), channel_id=1, source_target_pairs={{0,16},{16,0},{1,17},{17,1},{2,18},{18,2},{3,19},{19,3},{4,20},{20... | collective-permute-start | bytes 13074440 | tf_op jit(solution)/shard_map/ppermute | solution.py:475
  918.4 102.3 %collective-permute-start.6 = (bf16[256,1600]{0,1:T(8,128)(2,1)}, bf16[256,1600]{0,1:T(8,128)(2,1)S(1)}, u32[]{:S(2)}, u32[]{:S(2)}) collective-permute-start(bf16[256,1600]{0,1:T(8,128)(2,1)} %slice.729), channel_id=1, source_target_pairs={{0,16},{16,0},{1,17},{17,1},{2,18},{18,2},{3,19},{19,3},{4,20},{20... | collective-permute-start | bytes 2457608 | tf_op jit(solution)/shard_map/ppermute | solution.py:475
  919.2 107.7 %collective-permute-start.30 = (bf16[176,800]{1,0:T(8,128)(2,1)S(1)}, bf16[176,800]{1,0:T(8,128)(2,1)S(1)}, u32[]{:S(2)}, u32[]{:S(2)}) collective-permute-start(bf16[176,800]{1,0:T(8,128)(2,1)S(1)} %get-tuple-element.261), channel_id=1, source_target_pairs={{0,16},{16,0},{1,17},{17,1},{2,18},{18,2},{3,19},{19,3},{4,20},{20... | collective-permute-start | bytes 844808 | tf_op jit(solution)/shard_map/ppermute | solution.py:475
  1134.8 26.6 %collective-permute-start.17 = (bf16[3,3200]{1,0:T(4,128)(2,1)S(1)}, bf16[3,3200]{1,0:T(4,128)(2,1)S(1)}, u32[]{:S(2)}, u32[]{:S(2)}) collective-permute-start(bf16[3,3200]{1,0:T(4,128)(2,1)S(1)} %slice.731), channel_id=1, source_target_pairs={{1,0},{2,1},{3,2},{4,3},{5,4},{6,5},{7,6},{8,7},{9,8},{10,9},{11,1... | collective-permute-start | bytes 57608 | tf_op jit(solution)/shard_map/ppermute | solution.py:471
  1146.6 137.6 %collective-permute-start.25 = (bf16[832,3200]{1,0:T(8,128)(2,1)}, bf16[832,3200]{1,0:T(8,128)(2,1)}, u32[]{:S(2)}, u32[]{:S(2)}) collective-permute-start(bf16[832,3200]{1,0:T(8,128)(2,1)} %pad_select_fusion), channel_id=1, source_target_pairs={{0,16},{16,0},{1,17},{17,1},{2,18},{18,2},{3,19},{19,3},{4,20},{20... | collective-permute-start | bytes 15974408 | tf_op jit(solution)/shard_map/ppermute | solution.py:475
  1160.9 281.8 %collective-permute-start.29 = (bf16[104,2816]{1,0:T(8,128)(2,1)}, bf16[104,2816]{1,0:T(8,128)(2,1)}, u32[]{:S(2)}, u32[]{:S(2)}) collective-permute-start(bf16[104,2816]{1,0:T(8,128)(2,1)} %broadcast_select_fusion.3), channel_id=1, source_target_pairs={{0,16},{16,0},{1,17},{17,1},{2,18},{18,2},{3,19},{19,3},{4,20},{20... | collective-permute-start | bytes 1757192 | tf_op jit(solution)/shard_map/ppermute | solution.py:475
  1213.8 11.8 collective-permute-start.19
  1220.7 72.1 %collective-permute-start.24 = (bf16[832,3328]{1,0:T(8,128)(2,1)}, bf16[832,3328]{1,0:T(8,128)(2,1)}, u32[]{:S(2)}, u32[]{:S(2)}) collective-permute-start(bf16[832,3328]{1,0:T(8,128)(2,1)} %convolution_convert_fusion.2), channel_id=1, source_target_pairs={{0,1},{1,0},{2,3},{3,2},{4,5},{5,4},{6,7},{7,6},{8,9},{9,8},{10,11... | collective-permute-start | bytes 16613384 | tf_op jit(solution)/shard_map/ppermute | solution.py:475
  1224.9 22.9 %copy-start.20 = (f32[256,1600]{1,0:T(8,128)S(1)}, f32[256,1600]{1,0:T(8,128)}, u32[]{:S(2)}) copy-start(f32[256,1600]{1,0:T(8,128)} %repack.15) | copy-start | bytes 4915204
  1224.9 22.9 %copy-start.32 = (f32[256,1600]{1,0:T(8,128)S(1)}, f32[256,1600]{1,0:T(8,128)}, u32[]{:S(2)}) copy-start(f32[256,1600]{1,0:T(8,128)} %copy.232) | copy-start | bytes 4915204
  1225.5 22.3 %copy-start.5 = (f32[256,1600]{1,0:T(8,128)S(1)}, f32[256,1600]{1,0:T(8,128)}, u32[]{:S(2)}) copy-start(f32[256,1600]{1,0:T(8,128)} %copy-done.3) | copy-start | bytes 4915204
  1228.3 10.7 collective-permute-start.20
  1238.0 41.8 %collective-permute-start.26 = (bf16[8,200,512]{2,1,0:T(8,128)(2,1)}, bf16[8,200,512]{2,1,0:T(8,128)(2,1)}, u32[]{:S(2)}, u32[]{:S(2)}) collective-permute-start(bf16[8,200,512]{2,1,0:T(8,128)(2,1)} %select_bitcast_fusion), channel_id=1, source_target_pairs={{0,1},{1,0},{2,3},{3,2},{4,5},{5,4},{6,7},{7,6},{8,9},{9,8},{10,11... | collective-permute-start | bytes 4915208 | tf_op jit(solution)/shard_map/ppermute | solution.py:475
  1240.0 4.6 collective-permute-start.21
  1244.6 5.6 collective-permute-start.22
  1250.1 28.3 %collective-permute-start.23 = (f32[144,128]{1,0:T(8,128)S(1)}, f32[144,128]{1,0:T(8,128)S(1)}, u32[]{:S(2)}, u32[]{:S(2)}) collective-permute-start(f32[144,128]{1,0:T(8,128)S(1)} %add.304), channel_id=1, source_target_pairs={{0,16},{16,0},{1,17},{17,1},{2,18},{18,2},{3,19},{19,3},{4,20},{20... | collective-permute-start | bytes 221192 | tf_op jit(solution)/shard_map/ppermute | solution.py:475
  1438.9 22.4 %collective-permute-start.27 = (bf16[104,2176]{1,0:T(8,128)(2,1)S(1)}, bf16[104,2176]{1,0:T(8,128)(2,1)}, u32[]{:S(2)}, u32[]{:S(2)}) collective-permute-start(bf16[104,2176]{1,0:T(8,128)(2,1)S(1)} %fusion.82), channel_id=1, source_target_pairs={{0,16},{16,0},{1,17},{17,1},{2,18},{18,2},{3,19},{19,3},{4,20},{20... | collective-permute-start | bytes 1357832 | tf_op jit(solution)/shard_map/ppermute | solution.py:475
  1442.1 12.3 collective-permute-start.28
  (158 other events, 1154.2 us)
Sparse Core Ops, SparseCore 0:
  279.5 98.8 all-gather.9
  380.6 66.2 all-gather.15
  449.0 79.4 all-gather.11
  591.1 106.1 reduce-scatter.4
  727.6 46.7 all-gather.13
  777.7 105.7 reduce-scatter.6
  886.9 95.8 reduce-scatter.8
  1036.1 94.8 reduce-scatter.10

commit v2 on v1

--- a/solution.py
+++ b/solution.py
@@ -623,8 +623,9 @@
     for copy in kept:
         copy.wait()
 
-    up_late, down_late = (chips - 1) // 2, chips // 2
-    up_early, down_early = chips // 2, (chips - 1) // 2
+    longer, shorter = chips // 2, (chips - 1) // 2
+    hops_late = [(shorter, longer) if t % 2 == 0 else (longer, shorter) for t in range(count)]
+    hops_early = [(longer, shorter) if t % 2 == 0 else (shorter, longer) for t in range(count)]
     landed = []
     crossed = []
 
@@ -650,6 +651,7 @@
         above, below = place + chips - hop, place + hop
         for ring in rings:
             t, up, down = ring
+            up_late, down_late = hops_late[t]
             if hop <= up_late:
                 up.wait_recv()
                 if hop < up_late:
@@ -662,6 +664,7 @@
                 pass_late(t, below)
         for ring in early_rings:
             t, up, down = ring
+            up_early, down_early = hops_early[t]
             if hop <= up_early:
                 up.wait_recv()
                 if hop < up_early:
@@ -1069,10 +1072,12 @@
     decays, decay_back = jax.vjp(decay_rates, wide(decay_full))
     ends = scan_ends(step_size, signal, write_wide, decays)
     ends, expand_full = lax.optimization_barrier((ends, expand_full))
+    total = jnp.sum(step_size, axis=0, keepdims=True)
+    coarse = lax.reduce_precision(total, 8, 7)
     carried = lax.all_gather(
-        jnp.concatenate([ends, jnp.sum(step_size, axis=0, keepdims=True)], axis=0), SEQ
-    )
-    totals = carried[:, STATE:]
+        jnp.concatenate([ends, coarse, total - coarse], axis=0).astype(jnp.bfloat16), SEQ
+    )
+    totals = wide(carried[:, STATE : STATE + 1]) + wide(carried[:, STATE + 1 :])
     scanned, enter = scan_forward(
         where, step_size, signal, write_wide, read_wide, decays, skip_wide, totals, carried[:, :STATE]
     )
@@ -1106,6 +1111,7 @@
     expand_in = jnp.concatenate(
         [gate_grad.astype(jnp.bfloat16), up_grad.astype(jnp.bfloat16)], axis=1
     )
+    expand_in, block_output = lax.optimization_barrier((expand_in, block_output))
     second_both = dot_columns(expand_in, expand_full)
     second_normed_grad = repack(
         second_both[:local_len] + wide(swap(second_both[local_len:].astype(jnp.bfloat16))),
@@ -1130,7 +1136,7 @@
     )
     attended_grad, mamba_grad, attention_gain_grad, mamba_gain_grad = paths_back(joined_grad)
     scanned_grad, gate_path_grad = gating_back(mamba_grad)
-    own_pull = scan_pulls(step_size, scanned_grad, read_wide, decays)
+    own_pull = scan_pulls(step_size, scanned_grad, read_wide, decays).astype(jnp.bfloat16)
     pulls = lax.all_gather(own_pull, SEQ)
 
     normed_both, joined, own_pull, down_sum = lax.optimization_barrier(
@@ -1140,13 +1146,21 @@
     gate_total = grad_parts(both_split, expand_in[:, :hidden_width])
     up_total = grad_parts(both_split, expand_in[:, hidden_width:])
     output_grad = grad_parts(parity_columns(joined, parts, joined_pad), mixed_split, 0.5)
-    attended_in, gate_total, up_total, output_grad, pulls = lax.optimization_barrier(
-        (attended_grad.astype(jnp.bfloat16), gate_total, up_total, output_grad, pulls)
+    kept = jnp.where(first, down_sum[:, :cut], down_sum[:, cut : 2 * cut])
+    got = swap(jnp.where(first, down_sum[:, cut : 2 * cut], down_sum[:, :cut]))
+    down_out_grad = jnp.concatenate(
+        [
+            jnp.where(first, kept, got)[:hidden_half],
+            jnp.where(first, got, kept)[:hidden_half],
+        ],
+        axis=0,
+    )
+    attended_in, gate_total, up_total, output_grad, pulls, down_out_grad = lax.optimization_barrier(
+        (attended_grad.astype(jnp.bfloat16), gate_total, up_total, output_grad, pulls, down_out_grad)
     )
     gate_sum = scatter_rows(gate_total, rows_pad)
     up_sum = scatter_rows(up_total, rows_pad)
     output_grad = halve_dp(output_grad).astype(jnp.bfloat16)
-    output_sum = scatter_rows(output_grad, joined_pad)
 
     query_grad_turned, key_grads, value_grads = attend_back(
         where,
@@ -1173,9 +1187,10 @@
             )
         )
 
-    own_grad, meta_pair_grad, gate_sum = lax.optimization_barrier(
-        (own_grad, meta_pair_grad, gate_sum)
-    )
+    own_grad, meta_pair_grad, gate_sum, output_grad = lax.optimization_barrier(
+        (own_grad, meta_pair_grad, gate_sum, output_grad)
+    )
+    output_sum = scatter_rows(output_grad, joined_pad)
     with_meta = lambda rows, meta: jnp.concatenate([rows, meta], axis=0)
     query_in = with_meta(query_grad_turned.T, jnp.zeros((META, query_width), jnp.bfloat16))
     pair_in = with_meta(own_grad, meta_pair_grad).astype(jnp.bfloat16)
@@ -1185,11 +1200,6 @@
         normed_split, pad_lanes(jnp.concatenate([gate_in, query_in, pair_in], axis=1))
     )
     scanned_grad, early_grad = lax.optimization_barrier((scanned_grad, early_grad))
-    gate_early = early_grad[:, :MINNER]
-    pair_early = jnp.pad(
-        early_grad[:, MINNER : MINNER + inner_start], ((0, 0), (0, MINNER - inner_start))
-    )
-    early_grad = meet(pair_early, gate_early, lax.axis_index("dp"), swap).astype(jnp.bfloat16)
     signal_grad, step_grad, write_parts, read_parts, decays_grad, skip_parts = scan_backward(
         where,
         step_size,
@@ -1276,7 +1286,15 @@
         ]
     )
     output_out = wide(output_sum)[:rows_joined, :cut]
-    early_out = early_out[:rows_in]
+    pair_early = jnp.pad(
+        early_out[:, MINNER : MINNER + inner_start], ((0, 0), (0, MINNER - inner_start))
+    )
+    early_out = meet(
+        pair_early,
+        early_out[:, :MINNER],
+        lax.axis_index("dp"),
+        lambda array: swap(array.astype(jnp.bfloat16)),
+    )[:rows_in]
     small_sum = halve_dp(small_sum)
     inner_one, inner_two = inner_sum[:, :inner_first], inner_sum[:, inner_first:]
     inner_two = jnp.pad(inner_two, ((0, 0), (0, inner_first - inner_two.shape[1])))
@@ -1319,15 +1337,6 @@
     expand_out = weave(
         jnp.where(first, kept, got), jnp.where(first, got, kept), parts, hidden_pad, hidden_half
     )[:rows_in]
-    kept = jnp.where(first, down_sum[:, :cut], down_sum[:, cut : 2 * cut])
-    got = swap(jnp.where(first, down_sum[:, cut : 2 * cut], down_sum[:, :cut]))
-    down_out_grad = jnp.concatenate(
-        [
-            jnp.where(first, kept, got)[:hidden_half],
-            jnp.where(first, got, kept)[:hidden_half],
-        ],
-        axis=0,
-    )
     return (
         block_output[None],
         tokens_grad[None],

time: 1480 us -> 1390 us (0.939)
  waiting for transfers between devices: 252 us -> 159 us
  Pallas kernels: 620 us -> 638 us
    ppermute x18, waiting for transfers between devices: 173 us -> 84.3 us  [swap(): return lax.ppermute(array, axis, [(0, 1), (1, 0)])]
    pallas_call x1, Pallas kernels: 136 us -> 162 us  [ring_scatter(): pl.pallas_call(functools.partial(ring_kernel, cuts), in_specs=[vmem] * le...]
    all_gather x1, waiting for transfers between devices: 19.4 us -> 2.39 us  [shards(): pulls = lax.all_gather(own_pull, SEQ)]
    unnamed x357 -> x381, local copies, waits for them, and re-layouts: 35.9 us -> 37 us
  transfers between devices with their start and end apart: 39 -> 39, of which waited for: 16 -> 16; matrix products, arithmetic and copies ran while one was open for 32% -> 32% of each run, Pallas kernels for 24% -> 16%
where the time goes in v2:
time: 1390 us; the launch traced here: 1380 us
  Pallas kernels  638 us (46%)
  matrix products  235 us (17%)
  local copies, waits for them, and re-layouts  159 us (11%)
  waiting for transfers between devices  159 us (11%)
  other arithmetic  124 us (9%)
  starting transfers between devices  48.7 us (4%)
  between operations  16.8 us (1%)
    pallas_call x1, Pallas kernels, gather_everywhere(): pl.pallas_call(functools.partial(gather_kernel, cuts, len(others)), in_sp...  243 us
    pallas_call x1, Pallas kernels, ring_scatter(): pl.pallas_call(functools.partial(ring_kernel, cuts), in_specs=[vmem] * le...  162 us
    dot_general x14, matrix products, dot_rows(): lax.dot_general(left, right, (((0,), (0,)), ((), ())), preferred_element_...  95.7 us
    ppermute x18, waiting for transfers between devices, swap(): return lax.ppermute(array, axis, [(0, 1), (1, 0)])  84.3 us
    dot_general x8, matrix products, dot_columns(): lax.dot_general(left, right, (((1,), (1,)), ((), ())), preferred_element_...  82.6 us
    pallas_call x1, Pallas kernels, scan_backward(): pl.pallas_call(scan_back_kernel, grid=(channels // chunk,), in_specs=[pl....  58.5 us
    dot_general x8, matrix products, dot(): return jnp.dot(left, right, preferred_element_type=jnp.float32)  56.5 us
    reduce_scatter x4, waiting for transfers between devices, scatter_rows(): lax.psum_scatter(total.reshape(chips, rows, -1), 'chip', scatter_dimensio...  42.6 us
  transfers between devices with their start and end apart: 39, of which 16 were waited for; matrix products, arithmetic and copies ran while one was open for 32% of the time, Pallas kernels for 16%

profile of v2, /device:TPU:0, one launch (start us, length us, event | category | flops | bytes accessed | tf_op | source)
XLA Modules:
  0.0 1381.1 jit_solution(18407574807683483175)
XLA Ops:
  22.5 242.7 %gather_everywhere.1 = (bf16[2,8,2,104,4352]{4,3,2,1,0:T(8,128)(2,1)}, bf16[2,8,2,304,896]{4,3,2,1,0:T(8,128)(2,1)}, bf16[2,8,2,304,128]{4,3,2,1,0:T(8,128)(2,1)...) custom-call(bf16[104,4352]{1,0:T(8,128)(2,1)} %pad.243.refs_0_, ...), custom_call_target="tpu_custom_call" | custom-call | bytes 293339136 | tf_op jit(solution)/shard_map/gather_everywhere/pallas_call | solution.py:696
  275.4 8.4 fusion.2
  293.8 10.2 fusion.16
  328.6 6.2 fusion.152
  336.8 14.4 %scan_ends.1 = f32[16,3200]{1,0:T(8,128)} custom-call(f32[256,3200]{1,0:T(8,128)} %get-tuple-element.243.step_ref, bf16[256,3200]{1,0:T(8,128)(2,1)} %copy-done.9, f32[256,16,128]{2,1,0:T(8,128)} %broadcast_in_dim.30.write_ref, f32[16,3200]{1,0:T(8,128)} %bitcast_negate_fusion.decay_ref), custom_call_target="tpu_custom_call" | custom-call | tf_op jit(solution)/shard_map/scan_ends/pallas_call | solution.py:252
  351.3 16.6 %all-gather.12.cloned.1.call-done = bf16[1664,5632]{1,0:T(8,128)(2,1)} async-done(((bf16[104,5632]{1,0:T(8,128)(2,1)}), bf16[1664,5632]{1,0:T(8,128)(2,1)}) %all-gather.12.cloned.1.call-update) | async-done | bytes 18743312 | tf_op jit(solution)/shard_map/all_gather | solution.py:1002
  383.5 11.8 fusion.158
  416.3 19.1 %attend.1 = (f32[1600,256]{1,0:T(8,128)}, f32[5,8,256]{2,1,0:T(8,128)}) custom-call(s32[1]{0:T(128)} %bitcast.4.position_ref, bf16[1600,256]{1,0:T(8,128)(2,1)} %copy.183.query_ref, bf16[5,1408,64]{2,1,0:T(8,128)(2,1)} %bitcast.204, bf16[320,1408]{1,0:T(8,128)(2,1)} %copy.184.value_ref), custom_call_target="tpu_custom_call" | custom-call | tf_op jit(solution)/shard_map/attend/pallas_call | solution.py:424
  446.9 27.9 %scan_forward.1 = (f32[256,3200]{1,0:T(8,128)}, f32[16,3200]{1,0:T(8,128)}) custom-call(s32[1]{0:T(128)} %bitcast.4.position_ref, f32[256,3200]{1,0:T(8,128)} %get-tuple-element.243.step_ref, bf16[256,3200]{1,0:T(8,128)(2,1)} %copy-done.9, f32[256,16,128]{2,1,0:T(8,128)} %broadcast_in_dim.30.write_ref, f32[256,16,128]{2,1,0:T(8,128)} %broadcast_in_dim.31.read_ref, ...), custom_call_target="tpu_custom_call" | custom-call | tf_op jit(solution)/shard_map/scan_forward/pallas_call | solution.py:281
  488.3 7.3 fusion.12
  507.1 19.0 %collective-permute-done.5 = bf16[256,1664]{1,0:T(8,128)(2,1)S(1)} collective-permute-done((bf16[256,1664]{1,0:T(8,128)(2,1)}, bf16[256,1664]{1,0:T(8,128)(2,1)S(1)}, u32[]{:S(2)}, u32[]{:S(2)}) %collective-permute-start.5) | collective-permute-done | bytes 852000 | tf_op jit(solution)/shard_map/ppermute | solution.py:475
  527.0 17.1 %fusion.153 = f32[512,5632]{1,0:T(8,128)} fusion(bf16[1664,5632]{1,0:T(8,128)(2,1)} %all-gather.12.cloned.1.call-done, bf16[256,1664]{1,0:T(8,128)(2,1)S(1)} %collective-permute-done.5, bf16[256,1664]{1,0:T(8,128)(2,1)S(1)} %copy-done.53), kind=kOutput, calls=%fused_computation.321 | convolution fusion | flops 9599975424 | bytes 31981568 | tf_op jit(solution)/shard_map/dot_general | solution.py:889
  544.1 14.5 %fusion.22 = (bf16[512,2816]{1,0:T(8,128)(2,1)}, bf16[512,2816]{1,0:T(8,128)(2,1)}, bf16[512,2816]{1,0:T(8,128)(2,1)}) fusion(f32[512,5632]{1,0:T(8,128)} %fusion.153, bf16[2816,1600]{1,0:T(8,128)(2,1)} %all-gather.10.cloned.1.call-done, bf16[256,1600]{1,0:T(8,128)(2,1)S(1)} %copy-done.77, bf16[256,1600]{1,0:T(8,128)(2,1)S(1)} %bitcast.202), kind=kOutput, calls=%fused_computation.33 | convolution fusion | flops 4640079872 | bytes 30834688 | tf_op jit(solution)/shard_map/dot_general | solution.py:897
  558.6 6.6 parity_columns.4
  565.2 7.1 convolution_convert_fusion.1
  572.4 8.2 fusion.167
  591.8 11.1 collective-permute-done.6
  607.1 7.3 add_convert_fusion.5
  614.5 15.8 %fusion.168 = f32[512,1664]{1,0:T(8,128)S(1)} fusion(bf16[512,5632]{1,0:T(8,128)(2,1)} %pad_maximum_fusion, bf16[1664,5632]{1,0:T(8,128)(2,1)} %all-gather.12.cloned.1.call-done), kind=kOutput, calls=%fused_computation.335 | convolution fusion | flops 9596567552 | bytes 27918336 | tf_op jit(solution)/shard_map/dot_general | solution.py:897
  633.1 17.8 %collective-permute-done.7 = bf16[256,1664]{1,0:T(8,128)(2,1)S(1)} collective-permute-done((bf16[256,1664]{1,0:T(8,128)(2,1)S(1)}, bf16[256,1664]{1,0:T(8,128)(2,1)S(1)}, u32[]{:S(2)}, u32[]{:S(2)}) %collective-permute-start.7) | collective-permute-done | bytes 852000 | tf_op jit(solution)/shard_map/ppermute | solution.py:475
  667.0 6.3 fusion.19.in_ref
  673.4 6.2 repack.14
  683.6 6.6 fusion.74
  690.2 13.0 scan_pulls.1
  705.0 6.5 reduce-scatter.5.cloned.1.call-done
  716.4 7.1 multiply_convert_fusion
  723.5 6.1 parity_columns.5
  729.6 7.0 convolution_convert_fusion.4
  737.1 6.6 convolution_convert_fusion.3
  757.6 8.1 add_convert_fusion.4
  765.7 7.6 add_convert_fusion.3
  773.3 7.5 add_convert_fusion.1
  797.3 42.6 %attend_back.1 = (bf16[1600,256]{1,0:T(8,128)(2,1)}, f32[5,1408,64]{2,1,0:T(8,128)}, f32[5,1408,64]{2,1,0:T(8,128)}) custom-call(s32[1]{0:T(128)} %bitcast.4.position_ref, bf16[1600,256]{1,0:T(8,128)(2,1)} %copy.183.query_ref, bf16[1600,256]{1,0:T(8,128)(2,1)} %copy.199.grad_ref, f32[1600,256]{1,0:T(8,128)} %get-tuple-element.83.out_ref, ...), custom_call_target="tpu_custom_call" | custom-call | tf_op jit(solution)/shard_map/attend_back/pallas_call | solution.py:445
  886.3 7.1 add_convert_fusion.6
  893.5 7.7 concatenate.168
  901.2 10.8 convolution_convert_fusion
  912.0 7.3 collective-permute-start.18
  921.9 11.7 collective-permute-done.18
  933.6 13.5 add_convert_fusion
  947.0 58.5 %scan_backward.1 = (f32[256,3200]{1,0:T(8,128)}, f32[256,3200]{1,0:T(8,128)}, f32[256,16,128]{2,1,0:T(8,128)}, f32[256,16,128]{2,1,0:T(8,128)}, f32[16,3200]{1,0:T(8,128)}, /*index=5*/f32[8,3200]{1,0:T(8,128)}) custom-call(s32[1]{0:T(128)} %bitcast.4.position_ref, f32[256,3200]{1,0:T(8,128)} %get-tuple-element.243.step_ref, bf16[256,3200]{1,0:T(8,128)(2,1)} %copy-done.9, ...), custom_call_target="tpu_custom_call" | custom-call | tf_op jit(solution)/shard_map/scan_backward/pallas_call | solution.py:303
  1015.5 9.8 multiply_reduce_fusion.3
  1049.4 36.1 %reduce-scatter.11.cloned.1.call-done = bf16[1,304,896]{2,1,0:T(8,128)(2,1)} async-done(((bf16[8,304,896]{2,1,0:T(8,128)(2,1)}), bf16[1,304,896]{2,1,0:T(8,128)(2,1)}) %reduce-scatter.11.cloned.1.call-update) | async-done | bytes 544784 | tf_op jit(solution)/shard_map/reduce_scatter | solution.py:528
  1088.3 6.7 concatenate.171
  1095.1 13.9 %fusion.4 = f32[384,1664]{1,0:T(8,128)} fusion(bf16[2,1664,4352]{2,1,0:T(8,128)(2,1)} %bitcast.262, bf16[384,4320]{1,0:T(8,128)(2,1)} %concatenate.171), kind=kOutput, calls=%fused_computation.7 | convolution fusion | flops 5561647104 | bytes 20381696 | tf_op jit(solution)/shard_map/dot_general | solution.py:897
  1115.6 10.6 fusion.42.in_ref
  1169.5 7.1 add_convert_fusion.2
  1176.6 162.4 %ring_scatter.1 = (f32[104,3328]{1,0:T(8,128)}, f32[104,5504]{1,0:T(8,128)}, f32[200,512]{1,0:T(8,128)}) custom-call(bf16[8,104,3328]{2,1,0:T(8,128)(2,1)} %bitcast.228, bf16[8,104,5504]{2,1,0:T(8,128)(2,1)} %bitcast.217, bf16[8,200,512]{2,1,0:T(8,128)(2,1)} %fusion.40.refs_2_), custom_call_target="tpu_custom_call" | custom-call | bytes 65339392 | tf_op jit(solution)/shard_map/ring_scatter/pallas_call | solution.py:782
  1346.7 13.4 collective-permute-done.29
  (676 shorter events, 367.5 us)
Async XLA Ops:
  7.2 360.6 %all-gather.12.cloned.1.call-start = ((), (), s32[]{:S(2)}) async-start(), calls=%async_computation.10 | async-start | bytes 19914752 | tf_op jit(solution)/shard_map/all_gather | solution.py:1002
  268.8 171.0 %all-gather.8.cloned.1.call-start = ((), (), s32[]{:S(2)}) async-start(), calls=%async_computation.4 | async-start | bytes 2611200 | tf_op jit(solution)/shard_map/all_gather | solution.py:1077
  270.2 228.5 %copy-start.12 = (bf16[1,256,1600]{2,1,0:T(8,128)(2,1)}, bf16[1,256,1600]{2,1,0:T(8,128)(2,1)S(1)}, u32[]{:S(2)}) copy-start(bf16[1,256,1600]{2,1,0:T(8,128)(2,1)S(1)} %copy.178) | copy-start | bytes 2457604
  304.6 18.6 %collective-permute-start.4 = (bf16[3,3200]{1,0:T(4,128)(2,1)S(1)}, bf16[3,3200]{1,0:T(4,128)(2,1)S(1)}, u32[]{:S(2)}, u32[]{:S(2)}) collective-permute-start(bf16[3,3200]{1,0:T(4,128)(2,1)S(1)} %fusion.119), channel_id=1, source_target_pairs={{0,1},{1,2},{2,3},{3,4},{4,5},{5,6},{6,7},{7,8},{8,9},{9,10},{10,1... | collective-permute-start | bytes 57608 | tf_op jit(solution)/shard_map/ppermute | solution.py:471
  307.4 19.6 %copy-start.21 = (bf16[16,200,128]{2,1,0:T(8,128)(2,1)}, bf16[16,200,128]{2,1,0:T(8,128)(2,1)S(1)}, u32[]{:S(2)}) copy-start(bf16[16,200,128]{2,1,0:T(8,128)(2,1)S(1)} %slice.522) | copy-start | bytes 2457604
  369.5 174.6 %all-gather.10.cloned.1.call-start = ((), (), s32[]{:S(2)}) async-start(), calls=%async_computation.9 | async-start | bytes 9957376 | tf_op jit(solution)/shard_map/all_gather | solution.py:1003
  370.3 341.3 %reduce-scatter.5.cloned.1.call-start = ((), (), s32[]{:S(2)}) async-start(), calls=%async_computation.5 | async-start | bytes 5271552 | tf_op jit(solution)/shard_map/reduce_scatter | solution.py:528
  371.5 30.7 %collective-permute-start = (bf16[256,640]{1,0:T(8,128)(2,1)S(1)}, bf16[256,640]{1,0:T(8,128)(2,1)S(1)}, u32[]{:S(2)}, u32[]{:S(2)}) collective-permute-start(bf16[256,640]{1,0:T(8,128)(2,1)S(1)} %slice.517), channel_id=1, source_target_pairs={{0,4},{1,5},{2,6},{3,7},{4,8},{5,9},{6,10},{7,11},{8,12},{9,13},{1... | collective-permute-start | bytes 983048 | tf_op jit(solution)/shard_map/ppermute | solution.py:471
  374.9 28.0 %collective-permute-start.1 = (bf16[256,640]{1,0:T(8,128)(2,1)S(1)}, bf16[256,640]{1,0:T(8,128)(2,1)S(1)}, u32[]{:S(2)}, u32[]{:S(2)}) collective-permute-start(bf16[256,640]{1,0:T(8,128)(2,1)S(1)} %slice.517), channel_id=1, source_target_pairs={{0,3},{1,4},{2,5},{3,6},{4,7},{5,8},{6,9},{7,10},{8,11},{9,12},{10... | collective-permute-start | bytes 983048 | tf_op jit(solution)/shard_map/ppermute | solution.py:471
  377.7 26.0 %collective-permute-start.2 = (bf16[256,640]{1,0:T(8,128)(2,1)S(1)}, bf16[256,640]{1,0:T(8,128)(2,1)S(1)}, u32[]{:S(2)}, u32[]{:S(2)}) collective-permute-start(bf16[256,640]{1,0:T(8,128)(2,1)S(1)} %slice.517), channel_id=1, source_target_pairs={{0,2},{1,3},{2,4},{3,5},{4,6},{5,7},{6,8},{7,9},{8,10},{9,11},{10,... | collective-permute-start | bytes 983048 | tf_op jit(solution)/shard_map/ppermute | solution.py:471
  381.3 23.2 %collective-permute-start.3 = (bf16[256,640]{1,0:T(8,128)(2,1)S(1)}, bf16[256,640]{1,0:T(8,128)(2,1)S(1)}, u32[]{:S(2)}, u32[]{:S(2)}) collective-permute-start(bf16[256,640]{1,0:T(8,128)(2,1)S(1)} %slice.517), channel_id=1, source_target_pairs={{0,1},{1,2},{2,3},{3,4},{4,5},{5,6},{6,7},{7,8},{8,9},{9,10},{10,1... | collective-permute-start | bytes 983048 | tf_op jit(solution)/shard_map/ppermute | solution.py:471
  398.9 80.3 %copy-start.98 = (f32[3200]{0:T(1024)}, f32[3200]{0:T(1024)S(1)}, u32[]{:S(2)}) copy-start(f32[3200]{0:T(1024)S(1)} %convert_element_type.286) | copy-start | bytes 38404
  499.3 159.7 %copy-start.2 = (f32[256,1600]{1,0:T(8,128)}, f32[256,1600]{1,0:T(8,128)S(1)}, u32[]{:S(2)}) copy-start(f32[256,1600]{1,0:T(8,128)S(1)} %get-tuple-element.226) | copy-start | bytes 4915204
  499.3 157.1 %copy-start.124 = (f32[256]{0:T(256)}, f32[256]{0:T(256)S(1)}, u32[]{:S(2)}) copy-start(f32[256]{0:T(256)S(1)} %fusion.126) | copy-start | bytes 3076
  504.3 22.7 %copy-start.53 = (bf16[256,1664]{1,0:T(8,128)(2,1)S(1)}, bf16[256,1664]{1,0:T(8,128)(2,1)}, u32[]{:S(2)}) copy-start(bf16[256,1664]{1,0:T(8,128)(2,1)} %repack.12) | copy-start | bytes 2555908
  504.3 21.7 %collective-permute-start.5 = (bf16[256,1664]{1,0:T(8,128)(2,1)}, bf16[256,1664]{1,0:T(8,128)(2,1)S(1)}, u32[]{:S(2)}, u32[]{:S(2)}) collective-permute-start(bf16[256,1664]{1,0:T(8,128)(2,1)} %repack.12), channel_id=1, source_target_pairs={{0,16},{16,0},{1,17},{17,1},{2,18},{18,2},{3,19},{19,3},{4,20},{20... | collective-permute-start | bytes 2555912 | tf_op jit(solution)/shard_map/ppermute | solution.py:475
  572.3 34.8 %collective-permute-start.8 = (bf16[1408,1664]{1,0:T(8,128)(2,1)}, bf16[1408,1664]{1,0:T(8,128)(2,1)}, u32[]{:S(2)}, u32[]{:S(2)}) collective-permute-start(bf16[1408,1664]{1,0:T(8,128)(2,1)} %convolution_convert_fusion.1), channel_id=1, source_target_pairs={{0,1},{1,0},{2,3},{3,2},{4,5},{5,4},{6,7},{7,6},{8,9},{9,8},{10,11... | collective-permute-start | bytes 14057480 | tf_op jit(solution)/shard_map/ppermute | solution.py:475
  582.1 20.7 %collective-permute-start.6 = (bf16[256,1600]{0,1:T(8,128)(2,1)S(1)}, bf16[256,1600]{0,1:T(8,128)(2,1)}, u32[]{:S(2)}, u32[]{:S(2)}) collective-permute-start(bf16[256,1600]{0,1:T(8,128)(2,1)S(1)} %slice.762), channel_id=1, source_target_pairs={{0,16},{16,0},{1,17},{17,1},{2,18},{18,2},{3,19},{19,3},{4,20},{20... | collective-permute-start | bytes 2457608 | tf_op jit(solution)/shard_map/ppermute | solution.py:475
  614.4 168.8 %all-gather.14.cloned.1.call-start = ((), (), s32[]{:S(2)}) async-start(), calls=%async_computation.11 | async-start | bytes 1740800 | tf_op jit(solution)/shard_map/all_gather | solution.py:1140
  630.4 20.5 %collective-permute-start.7 = (bf16[256,1664]{1,0:T(8,128)(2,1)S(1)}, bf16[256,1664]{1,0:T(8,128)(2,1)S(1)}, u32[]{:S(2)}, u32[]{:S(2)}) collective-permute-start(bf16[256,1664]{1,0:T(8,128)(2,1)S(1)} %slice.761), channel_id=1, source_target_pairs={{0,16},{16,0},{1,17},{17,1},{2,18},{18,2},{3,19},{19,3},{4,20},{20... | collective-permute-start | bytes 2555912 | tf_op jit(solution)/shard_map/ppermute | solution.py:475
  723.5 49.8 %collective-permute-start.11 = (bf16[2432,1792]{1,0:T(8,128)(2,1)}, bf16[2432,1792]{1,0:T(8,128)(2,1)}, u32[]{:S(2)}, u32[]{:S(2)}) collective-permute-start(bf16[2432,1792]{1,0:T(8,128)(2,1)} %multiply_convert_fusion), channel_id=1, source_target_pairs={{0,1},{1,0},{2,3},{3,2},{4,5},{5,4},{6,7},{7,6},{8,9},{9,8},{10,11... | collective-permute-start | bytes 26148872 | tf_op jit(solution)/shard_map/ppermute | solution.py:475
  736.6 21.0 %collective-permute-start.9 = (bf16[832,2816]{1,0:T(8,128)(2,1)}, bf16[832,2816]{1,0:T(8,128)(2,1)}, u32[]{:S(2)}, u32[]{:S(2)}) collective-permute-start(bf16[832,2816]{1,0:T(8,128)(2,1)} %convolution_convert_fusion.4), channel_id=1, source_target_pairs={{0,1},{1,0},{2,3},{3,2},{4,5},{5,4},{6,7},{7,6},{8,9},{9,8},{10,11... | collective-permute-start | bytes 14057480 | tf_op jit(solution)/shard_map/ppermute | solution.py:475
  743.7 22.0 %collective-permute-start.10 = (bf16[832,2816]{1,0:T(8,128)(2,1)}, bf16[832,2816]{1,0:T(8,128)(2,1)}, u32[]{:S(2)}, u32[]{:S(2)}) collective-permute-start(bf16[832,2816]{1,0:T(8,128)(2,1)} %convolution_convert_fusion.3), channel_id=1, source_target_pairs={{0,1},{1,0},{2,3},{3,2},{4,5},{5,4},{6,7},{7,6},{8,9},{9,8},{10,11... | collective-permute-start | bytes 14057480 | tf_op jit(solution)/shard_map/ppermute | solution.py:475
  743.8 149.6 %reduce-scatter.7.cloned.1.call-start = ((), (), s32[]{:S(2)}) async-start(), calls=%async_computation.6 | async-start | bytes 5271552 | tf_op jit(solution)/shard_map/reduce_scatter | solution.py:528
  746.7 9.8 collective-permute-start.12
  783.3 227.1 %reduce-scatter.9.cloned.1.call-start = ((), (), s32[]{:S(2)}) async-start(), calls=%async_computation.7 | async-start | bytes 5271552 | tf_op jit(solution)/shard_map/reduce_scatter | solution.py:528
  789.8 96.6 %collective-permute-start.17 = (bf16[2432,896]{1,0:T(8,128)(2,1)}, bf16[2432,896]{1,0:T(8,128)(2,1)}, u32[]{:S(2)}, u32[]{:S(2)}) collective-permute-start(bf16[2432,896]{1,0:T(8,128)(2,1)} %broadcast_select_fusion), channel_id=1, source_target_pairs={{0,16},{16,0},{1,17},{17,1},{2,18},{18,2},{3,19},{19,3},{4,20},{20... | collective-permute-start | bytes 13074440 | tf_op jit(solution)/shard_map/ppermute | solution.py:475
  855.5 22.7 %collective-permute-start.16 = (bf16[256,640]{1,0:T(8,128)(2,1)}, bf16[256,640]{1,0:T(8,128)(2,1)}, u32[]{:S(2)}, u32[]{:S(2)}) collective-permute-start(bf16[256,640]{1,0:T(8,128)(2,1)} %get-tuple-element.247), channel_id=1, source_target_pairs={{4,0},{5,1},{6,2},{7,3},{8,4},{9,5},{10,6},{11,7},{12,8},{13,9},{1... | collective-permute-start | bytes 983048 | tf_op jit(solution)/shard_map/ppermute | solution.py:471
  856.8 21.5 %collective-permute-start.15 = (bf16[256,640]{1,0:T(8,128)(2,1)}, bf16[256,640]{1,0:T(8,128)(2,1)}, u32[]{:S(2)}, u32[]{:S(2)}) collective-permute-start(bf16[256,640]{1,0:T(8,128)(2,1)} %get-tuple-element.248), channel_id=1, source_target_pairs={{3,0},{4,1},{5,2},{6,3},{7,4},{8,5},{9,6},{10,7},{11,8},{12,9},{13... | collective-permute-start | bytes 983048 | tf_op jit(solution)/shard_map/ppermute | solution.py:471
  858.1 20.2 %collective-permute-start.14 = (bf16[256,640]{1,0:T(8,128)(2,1)}, bf16[256,640]{1,0:T(8,128)(2,1)}, u32[]{:S(2)}, u32[]{:S(2)}) collective-permute-start(bf16[256,640]{1,0:T(8,128)(2,1)} %get-tuple-element.249), channel_id=1, source_target_pairs={{2,0},{3,1},{4,2},{5,3},{6,4},{7,5},{8,6},{9,7},{10,8},{11,9},{12,... | collective-permute-start | bytes 983048 | tf_op jit(solution)/shard_map/ppermute | solution.py:471
  859.4 18.9 %collective-permute-start.13 = (bf16[256,640]{1,0:T(8,128)(2,1)}, bf16[256,640]{1,0:T(8,128)(2,1)}, u32[]{:S(2)}, u32[]{:S(2)}) collective-permute-start(bf16[256,640]{1,0:T(8,128)(2,1)} %get-tuple-element.246), channel_id=1, source_target_pairs={{1,0},{2,1},{3,2},{4,3},{5,4},{6,5},{7,6},{8,7},{9,8},{10,9},{11,1... | collective-permute-start | bytes 983048 | tf_op jit(solution)/shard_map/ppermute | solution.py:471
  872.5 21.0 %copy-start.27 = (bf16[384,1600]{1,0:T(8,128)(2,1)}, bf16[384,1600]{1,0:T(8,128)(2,1)S(1)}, u32[]{:S(2)}) copy-start(bf16[384,1600]{1,0:T(8,128)(2,1)S(1)} %concatenate.164) | copy-start | bytes 3686404
  872.5 213.0 %reduce-scatter.11.cloned.1.call-start = ((), (), s32[]{:S(2)}) async-start(), calls=%async_computation.8 | async-start | bytes 4902912 | tf_op jit(solution)/shard_map/reduce_scatter | solution.py:528
  901.2 19.4 %copy-start.59 = (bf16[344,800]{1,0:T(8,128)(2,1)S(1)}, bf16[344,800]{1,0:T(8,128)(2,1)}, u32[]{:S(2)}) copy-start(bf16[344,800]{1,0:T(8,128)(2,1)} %pad_maximum_fusion.16) | copy-start | bytes 1651204
  912.0 21.5 %collective-permute-start.18 = (bf16[832,5504]{1,0:T(8,128)(2,1)}, bf16[832,5504]{1,0:T(8,128)(2,1)}, u32[]{:S(2)}, u32[]{:S(2)}) collective-permute-start(bf16[832,5504]{1,0:T(8,128)(2,1)} %convolution_convert_fusion), channel_id=1, source_target_pairs={{0,1},{1,0},{2,3},{3,2},{4,5},{5,4},{6,7},{7,6},{8,9},{9,8},{10,11... | collective-permute-start | bytes 27475976 | tf_op jit(solution)/shard_map/ppermute | solution.py:475
  1031.7 16.5 %collective-permute-start.19 = (bf16[3,3200]{1,0:T(4,128)(2,1)}, bf16[3,3200]{1,0:T(4,128)(2,1)}, u32[]{:S(2)}, u32[]{:S(2)}) collective-permute-start(bf16[3,3200]{1,0:T(4,128)(2,1)} %slice.764), channel_id=1, source_target_pairs={{1,0},{2,1},{3,2},{4,3},{5,4},{6,5},{7,6},{8,7},{9,8},{10,9},{11,1... | collective-permute-start | bytes 57608 | tf_op jit(solution)/shard_map/ppermute | solution.py:471
  1046.8 113.8 %collective-permute-start.30 = (bf16[104,2816]{1,0:T(8,128)(2,1)}, bf16[104,2816]{1,0:T(8,128)(2,1)}, u32[]{:S(2)}, u32[]{:S(2)}) collective-permute-start(bf16[104,2816]{1,0:T(8,128)(2,1)} %broadcast_select_fusion.3), channel_id=1, source_target_pairs={{0,16},{16,0},{1,17},{17,1},{2,18},{18,2},{3,19},{19,3},{4,20},{20... | collective-permute-start | bytes 1757192 | tf_op jit(solution)/shard_map/ppermute | solution.py:475
  1115.6 53.9 %collective-permute-start.25 = (bf16[832,3328]{1,0:T(8,128)(2,1)}, bf16[832,3328]{1,0:T(8,128)(2,1)}, u32[]{:S(2)}, u32[]{:S(2)}) collective-permute-start(bf16[832,3328]{1,0:T(8,128)(2,1)} %convolution_convert_fusion.2), channel_id=1, source_target_pairs={{0,1},{1,0},{2,3},{3,2},{4,5},{5,4},{6,7},{7,6},{8,9},{9,8},{10,11... | collective-permute-start | bytes 16613384 | tf_op jit(solution)/shard_map/ppermute | solution.py:475
  1135.9 3.9 collective-permute-start.20
  1139.8 4.4 collective-permute-start.21
  1144.2 4.4 collective-permute-start.22
  1144.9 21.2 %collective-permute-start.26 = (bf16[8,200,512]{2,1,0:T(8,128)(2,1)}, bf16[8,200,512]{2,1,0:T(8,128)(2,1)}, u32[]{:S(2)}, u32[]{:S(2)}) collective-permute-start(bf16[8,200,512]{2,1,0:T(8,128)(2,1)} %select_bitcast_fusion), channel_id=1, source_target_pairs={{0,1},{1,0},{2,3},{3,2},{4,5},{5,4},{6,7},{7,6},{8,9},{9,8},{10,11... | collective-permute-start | bytes 4915208 | tf_op jit(solution)/shard_map/ppermute | solution.py:475
  1148.7 6.1 collective-permute-start.23
  1154.8 4.4 collective-permute-start.24
  1342.2 27.9 %collective-permute-start.28 = (bf16[104,2176]{1,0:T(8,128)(2,1)}, bf16[104,2176]{1,0:T(8,128)(2,1)}, u32[]{:S(2)}, u32[]{:S(2)}) collective-permute-start(bf16[104,2176]{1,0:T(8,128)(2,1)} %fusion.90), channel_id=1, source_target_pairs={{0,16},{16,0},{1,17},{17,1},{2,18},{18,2},{3,19},{19,3},{4,20},{20... | collective-permute-start | bytes 1357832 | tf_op jit(solution)/shard_map/ppermute | solution.py:475
  1343.5 26.5 %copy-start.60 = (f32[104,3328]{1,0:T(8,128)S(1)}, f32[104,3328]{1,0:T(8,128)}, u32[]{:S(2)}) copy-start(f32[104,3328]{1,0:T(8,128)} %get-tuple-element.126) | copy-start | bytes 4153348
  1343.6 16.5 %collective-permute-start.29 = (f32[200,256]{1,0:T(8,128)S(1)}, f32[200,256]{1,0:T(8,128)S(1)}, u32[]{:S(2)}, u32[]{:S(2)}) collective-permute-start(f32[200,256]{1,0:T(8,128)S(1)} %slice_select_fusion.2), channel_id=1, source_target_pairs={{0,16},{16,0},{1,17},{17,1},{2,18},{18,2},{3,19},{19,3},{4,20},{20... | collective-permute-start | bytes 614408 | tf_op jit(solution)/shard_map/ppermute | solution.py:475
  1345.4 26.0 %collective-permute-start.27 = (bf16[104,3200]{1,0:T(8,128)(2,1)}, bf16[104,3200]{1,0:T(8,128)(2,1)S(1)}, u32[]{:S(2)}, u32[]{:S(2)}) collective-permute-start(bf16[104,3200]{1,0:T(8,128)(2,1)} %fusion.81), channel_id=1, source_target_pairs={{0,16},{16,0},{1,17},{17,1},{2,18},{18,2},{3,19},{19,3},{4,20},{20... | collective-permute-start | bytes 1996808 | tf_op jit(solution)/shard_map/ppermute | solution.py:475
  (170 other events, 1047.6 us)
Sparse Core Ops, SparseCore 0:
  269.0 98.8 all-gather.11
  370.0 49.2 all-gather.7
  421.5 79.0 all-gather.9
  614.6 96.9 reduce-scatter.4
  743.9 39.2 all-gather.13
  786.5 105.4 reduce-scatter.6
  895.5 97.8 reduce-scatter.8
  997.0 88.5 reduce-scatter.10

commit v3 on v2

--- a/solution.py
+++ b/solution.py
@@ -1111,8 +1111,8 @@
     expand_in = jnp.concatenate(
         [gate_grad.astype(jnp.bfloat16), up_grad.astype(jnp.bfloat16)], axis=1
     )
-    expand_in, block_output = lax.optimization_barrier((expand_in, block_output))
     second_both = dot_columns(expand_in, expand_full)
+    second_both, block_output = lax.optimization_barrier((second_both, block_output))
     second_normed_grad = repack(
         second_both[:local_len] + wide(swap(second_both[local_len:].astype(jnp.bfloat16))),
         parts,
@@ -1190,7 +1190,6 @@
     own_grad, meta_pair_grad, gate_sum, output_grad = lax.optimization_barrier(
         (own_grad, meta_pair_grad, gate_sum, output_grad)
     )
-    output_sum = scatter_rows(output_grad, joined_pad)
     with_meta = lambda rows, meta: jnp.concatenate([rows, meta], axis=0)
     query_in = with_meta(query_grad_turned.T, jnp.zeros((META, query_width), jnp.bfloat16))
     pair_in = with_meta(own_grad, meta_pair_grad).astype(jnp.bfloat16)
@@ -1200,6 +1199,7 @@
         normed_split, pad_lanes(jnp.concatenate([gate_in, query_in, pair_in], axis=1))
     )
     scanned_grad, early_grad = lax.optimization_barrier((scanned_grad, early_grad))
+    early_sum = scatter_rows(early_grad, rows_pad)
     signal_grad, step_grad, write_parts, read_parts, decays_grad, skip_parts = scan_backward(
         where,
         step_size,
@@ -1231,7 +1231,6 @@
     decay_grad = decay_back(decays_grad)[0]
 
     inner_in = with_meta(inner_grad.astype(jnp.bfloat16), jnp.zeros((META, MINNER), jnp.bfloat16))
-    inner_in, output_sum = lax.optimization_barrier((inner_in, output_sum))
     inner_cut = half - inner_start
     inner_first = -(-inner_cut // LANES) * LANES
     inner_grads = grad_parts(
@@ -1278,20 +1277,21 @@
         lax.axis_index("core"),
         lambda array: swap(array, "core"),
     )
-    inner_sum, early_out, small_sum = ring_scatter(
+    inner_grads, early_sum = lax.optimization_barrier((inner_grads, early_sum))
+    inner_sum, output_out, small_sum = ring_scatter(
         [
             inner_grads.reshape(parts // 2, rows_pad, -1),
-            early_grad.reshape(parts // 2, rows_pad, -1),
+            output_grad.reshape(parts // 2, joined_pad, -1),
             small_sum.astype(jnp.bfloat16),
         ]
     )
-    output_out = wide(output_sum)[:rows_joined, :cut]
+    output_out = output_out[:rows_joined, :cut]
     pair_early = jnp.pad(
-        early_out[:, MINNER : MINNER + inner_start], ((0, 0), (0, MINNER - inner_start))
+        early_sum[:, MINNER : MINNER + inner_start], ((0, 0), (0, MINNER - inner_start))
     )
     early_out = meet(
         pair_early,
-        early_out[:, :MINNER],
+        early_sum[:, :MINNER],
         lax.axis_index("dp"),
         lambda array: swap(array.astype(jnp.bfloat16)),
     )[:rows_in]

time: 1390 us -> 1400 us (level)
  waiting for transfers between devices: 159 us -> 214 us
  Pallas kernels: 638 us -> 600 us
    unnamed x8 -> x9, waiting for transfers between devices: 0.8 us -> 83.4 us
    pallas_call x1, Pallas kernels: 162 us -> 124 us  [ring_scatter(): pl.pallas_call(functools.partial(ring_kernel, cuts), in_specs=[vmem] * le...]
    reduce_scatter x4 -> x3, waiting for transfers between devices: 42.6 us -> 12.5 us  [scatter_rows(): lax.psum_scatter(total.reshape(chips, rows, -1), 'chip', scatter_dimensio...]
    unnamed x381 -> x372, local copies, waits for them, and re-layouts: 37 us -> 38 us
  transfers between devices with their start and end apart: 39 -> 39, of which waited for: 16 -> 16; matrix products, arithmetic and copies ran while one was open for 32% -> 29% of each run, Pallas kernels for 16% -> 16%
where the time goes in v3:
time: 1400 us; the launch traced here: 1390 us
  Pallas kernels  600 us (43%)
  matrix products  236 us (17%)
  waiting for transfers between devices  214 us (15%)
  local copies, waits for them, and re-layouts  157 us (11%)
  other arithmetic  118 us (8%)
  starting transfers between devices  48.3 us (3%)
  between operations  16.7 us (1%)
    pallas_call x1, Pallas kernels, gather_everywhere(): pl.pallas_call(functools.partial(gather_kernel, cuts, len(others)), in_sp...  243 us
    pallas_call x1, Pallas kernels, ring_scatter(): pl.pallas_call(functools.partial(ring_kernel, cuts), in_specs=[vmem] * le...  124 us
    dot_general x14, matrix products, dot_rows(): lax.dot_general(left, right, (((0,), (0,)), ((), ())), preferred_element_...  94.3 us
    dot_general x8, matrix products, dot_columns(): lax.dot_general(left, right, (((1,), (1,)), ((), ())), preferred_element_...  84.6 us
    unnamed x9, waiting for transfers between devices  83.4 us
    ppermute x18, waiting for transfers between devices, swap(): return lax.ppermute(array, axis, [(0, 1), (1, 0)])  75.6 us
    pallas_call x1, Pallas kernels, scan_backward(): pl.pallas_call(scan_back_kernel, grid=(channels // chunk,), in_specs=[pl....  58.4 us
    dot_general x8, matrix products, dot(): return jnp.dot(left, right, preferred_element_type=jnp.float32)  56.7 us
  transfers between devices with their start and end apart: 39, of which 16 were waited for; matrix products, arithmetic and copies ran while one was open for 29% of the time, Pallas kernels for 16%

profile of v3, /device:TPU:0, one launch (start us, length us, event | category | flops | bytes accessed | tf_op | source)
XLA Modules:
  0.0 1389.2 jit_solution(3492738219189718610)
XLA Ops:
  22.5 242.7 %gather_everywhere.1 = (bf16[2,8,2,104,4352]{4,3,2,1,0:T(8,128)(2,1)}, bf16[2,8,2,304,896]{4,3,2,1,0:T(8,128)(2,1)}, bf16[2,8,2,304,128]{4,3,2,1,0:T(8,128)(2,1)...) custom-call(bf16[104,4352]{1,0:T(8,128)(2,1)} %pad.243.refs_0_, ...), custom_call_target="tpu_custom_call" | custom-call | bytes 293339136 | tf_op jit(solution)/shard_map/gather_everywhere/pallas_call | solution.py:696
  275.3 8.4 fusion.2
  293.8 10.2 fusion.16
  328.7 6.3 fusion.146
  336.8 14.4 %scan_ends.1 = f32[16,3200]{1,0:T(8,128)} custom-call(f32[256,3200]{1,0:T(8,128)} %get-tuple-element.243.step_ref, bf16[256,3200]{1,0:T(8,128)(2,1)} %copy-done.9, f32[256,16,128]{2,1,0:T(8,128)} %broadcast_in_dim.30.write_ref, f32[16,3200]{1,0:T(8,128)} %bitcast_negate_fusion.decay_ref), custom_call_target="tpu_custom_call" | custom-call | tf_op jit(solution)/shard_map/scan_ends/pallas_call | solution.py:252
  351.3 16.5 %all-gather.12.cloned.1.call-done = bf16[1664,5632]{1,0:T(8,128)(2,1)} async-done(((bf16[104,5632]{1,0:T(8,128)(2,1)}), bf16[1664,5632]{1,0:T(8,128)(2,1)}) %all-gather.12.cloned.1.call-update) | async-done | bytes 18743312 | tf_op jit(solution)/shard_map/all_gather | solution.py:1002
  383.5 11.8 fusion.152
  416.2 19.1 %attend.1 = (f32[1600,256]{1,0:T(8,128)}, f32[5,8,256]{2,1,0:T(8,128)}) custom-call(s32[1]{0:T(128)} %bitcast.4.position_ref, bf16[1600,256]{1,0:T(8,128)(2,1)} %copy.183.query_ref, bf16[5,1408,64]{2,1,0:T(8,128)(2,1)} %bitcast.209, bf16[320,1408]{1,0:T(8,128)(2,1)} %copy.184.value_ref), custom_call_target="tpu_custom_call" | custom-call | tf_op jit(solution)/shard_map/attend/pallas_call | solution.py:424
  446.9 27.9 %scan_forward.1 = (f32[256,3200]{1,0:T(8,128)}, f32[16,3200]{1,0:T(8,128)}) custom-call(s32[1]{0:T(128)} %bitcast.4.position_ref, f32[256,3200]{1,0:T(8,128)} %get-tuple-element.243.step_ref, bf16[256,3200]{1,0:T(8,128)(2,1)} %copy-done.9, f32[256,16,128]{2,1,0:T(8,128)} %broadcast_in_dim.30.write_ref, f32[256,16,128]{2,1,0:T(8,128)} %broadcast_in_dim.31.read_ref, ...), custom_call_target="tpu_custom_call" | custom-call | tf_op jit(solution)/shard_map/scan_forward/pallas_call | solution.py:281
  488.2 7.3 fusion.12
  507.0 19.0 %collective-permute-done.5 = bf16[256,1664]{1,0:T(8,128)(2,1)S(1)} collective-permute-done((bf16[256,1664]{1,0:T(8,128)(2,1)}, bf16[256,1664]{1,0:T(8,128)(2,1)S(1)}, u32[]{:S(2)}, u32[]{:S(2)}) %collective-permute-start.5) | collective-permute-done | bytes 852000 | tf_op jit(solution)/shard_map/ppermute | solution.py:475
  527.0 17.1 %fusion.147 = f32[512,5632]{1,0:T(8,128)} fusion(bf16[1664,5632]{1,0:T(8,128)(2,1)} %all-gather.12.cloned.1.call-done, bf16[256,1664]{1,0:T(8,128)(2,1)S(1)} %collective-permute-done.5, bf16[256,1664]{1,0:T(8,128)(2,1)S(1)} %copy-done.49), kind=kOutput, calls=%fused_computation.320 | convolution fusion | flops 9599975424 | bytes 31981568 | tf_op jit(solution)/shard_map/dot_general | solution.py:889
  544.2 14.4 %fusion.22 = (bf16[512,2816]{1,0:T(8,128)(2,1)}, bf16[512,2816]{1,0:T(8,128)(2,1)}, bf16[512,2816]{1,0:T(8,128)(2,1)}) fusion(f32[512,5632]{1,0:T(8,128)} %fusion.147, bf16[2816,1600]{1,0:T(8,128)(2,1)} %all-gather.10.cloned.1.call-done, bf16[256,1600]{1,0:T(8,128)(2,1)S(1)} %copy-done.76, bf16[256,1600]{1,0:T(8,128)(2,1)S(1)} %bitcast.207), kind=kOutput, calls=%fused_computation.33 | convolution fusion | flops 4640079872 | bytes 30834688 | tf_op jit(solution)/shard_map/dot_general | solution.py:897
  558.6 6.6 parity_columns.4
  565.2 7.1 convolution_convert_fusion.1
  572.4 8.3 fusion.161
  582.3 6.4 add_convert_fusion.5
  588.8 17.9 %fusion.23 = f32[512,1664]{1,0:T(8,128)} fusion(bf16[1664,5632]{1,0:T(8,128)(2,1)} %all-gather.12.cloned.1.call-done, bf16[512,2816]{1,0:T(8,128)(2,1)} %get-tuple-element.234, bf16[512,2816]{1,0:T(8,128)(2,1)} %get-tuple-element.233), kind=kOutput, calls=%fused_computation.34 | convolution fusion | flops 9608101888 | bytes 27918336 | tf_op jit(solution)/shard_map/dot_general | solution.py:897
  618.7 18.8 %collective-permute-done.7 = bf16[256,1664]{1,0:T(8,128)(2,1)S(1)} collective-permute-done((bf16[256,1664]{1,0:T(8,128)(2,1)S(1)}, bf16[256,1664]{1,0:T(8,128)(2,1)S(1)}, u32[]{:S(2)}, u32[]{:S(2)}) %collective-permute-start.7) | collective-permute-done | bytes 852000 | tf_op jit(solution)/shard_map/ppermute | solution.py:475
  653.9 6.4 fusion.19.in_ref
  660.3 6.3 repack.14
  670.6 7.0 fusion.69
  677.6 13.0 scan_pulls.1
  697.0 7.1 multiply_convert_fusion
  710.2 7.0 convolution_convert_fusion.4
  735.9 7.3 add_convert_fusion.4
  743.3 7.4 add_convert_fusion.3
  750.6 7.5 add_convert_fusion.1
  758.1 7.7 all-gather.14.cloned.1.call-done
  766.1 6.1 broadcast_select_fusion
  779.8 42.5 %attend_back.1 = (bf16[1600,256]{1,0:T(8,128)(2,1)}, f32[5,1408,64]{2,1,0:T(8,128)}, f32[5,1408,64]{2,1,0:T(8,128)}) custom-call(s32[1]{0:T(128)} %bitcast.4.position_ref, bf16[1600,256]{1,0:T(8,128)(2,1)} %copy.183.query_ref, bf16[1600,256]{1,0:T(8,128)(2,1)} %copy.199.grad_ref, f32[1600,256]{1,0:T(8,128)} %get-tuple-element.83.out_ref, ...), custom_call_target="tpu_custom_call" | custom-call | tf_op jit(solution)/shard_map/attend_back/pallas_call | solution.py:445
  868.8 7.1 add_convert_fusion.6
  876.0 7.5 concatenate.168
  883.6 10.7 convolution_convert_fusion
  894.3 7.2 collective-permute-start.18
  904.2 11.4 collective-permute-done.18
  915.7 14.0 %add_convert_fusion = bf16[832,5504]{1,0:T(8,128)(2,1)} fusion(bf16[832,5504]{1,0:T(8,128)(2,1)} %collective-permute-done.18, bf16[384,832]{1,0:T(8,128)(2,1)} %get-tuple-element.109, bf16[384,5440]{1,0:T(8,128)(2,1)} %concatenate.168), kind=kOutput, calls=%fused_computation | convolution fusion | flops 3530661888 | bytes 23134208 | tf_op jit(solution)/shard_map/dot_general | solution.py:893
  929.7 58.4 %scan_backward.1 = (f32[256,3200]{1,0:T(8,128)}, f32[256,3200]{1,0:T(8,128)}, f32[256,16,128]{2,1,0:T(8,128)}, f32[256,16,128]{2,1,0:T(8,128)}, f32[16,3200]{1,0:T(8,128)}, /*index=5*/f32[8,3200]{1,0:T(8,128)}) custom-call(s32[1]{0:T(128)} %bitcast.4.position_ref, f32[256,3200]{1,0:T(8,128)} %get-tuple-element.243.step_ref, bf16[256,3200]{1,0:T(8,128)(2,1)} %copy-done.9, ...), custom_call_target="tpu_custom_call" | custom-call | tf_op jit(solution)/shard_map/scan_backward/pallas_call | solution.py:303
  992.7 12.5 reduce-scatter.11.cloned.1.call-done
  1012.5 9.2 multiply_reduce_fusion.3
  1046.5 6.3 concatenate.171
  1059.9 13.8 fusion.4
  1073.7 11.0 fusion.46.in_ref
  1110.1 6.6 collective-permute-done.23
  1131.5 7.1 add_convert_fusion.2
  1138.6 82.6 %reduce-scatter.13.cloned.1.call-done = bf16[1,104,5504]{2,1,0:T(8,128)(2,1)} async-done(((bf16[8,104,5504]{2,1,0:T(8,128)(2,1)}), bf16[1,104,5504]{2,1,0:T(8,128)(2,1)}) %reduce-scatter.13.cloned.1.call-update) | async-done | bytes 1144848
  1221.2 123.5 %ring_scatter.1 = (f32[104,3328]{1,0:T(8,128)}, f32[304,896]{1,0:T(8,128)}, f32[200,512]{1,0:T(8,128)}) custom-call(bf16[8,104,3328]{2,1,0:T(8,128)(2,1)} %bitcast.231, bf16[8,304,896]{2,1,0:T(8,128)(2,1)} %bitcast.208, bf16[8,200,512]{2,1,0:T(8,128)(2,1)} %fusion.44.refs_2_), custom_call_target="tpu_custom_call" | custom-call | bytes 46137344 | tf_op jit(solution)/shard_map/ring_scatter/pallas_call | solution.py:782
  1352.5 13.3 collective-permute-done.29
  (663 shorter events, 364.7 us)
Async XLA Ops:
  7.2 360.6 %all-gather.12.cloned.1.call-start = ((), (), s32[]{:S(2)}) async-start(), calls=%async_computation.9 | async-start | bytes 19914752 | tf_op jit(solution)/shard_map/all_gather | solution.py:1002
  268.8 171.0 %all-gather.8.cloned.1.call-start = ((), (), s32[]{:S(2)}) async-start(), calls=%async_computation.4 | async-start | bytes 2611200 | tf_op jit(solution)/shard_map/all_gather | solution.py:1077
  270.2 228.5 %copy-start.12 = (bf16[1,256,1600]{2,1,0:T(8,128)(2,1)}, bf16[1,256,1600]{2,1,0:T(8,128)(2,1)S(1)}, u32[]{:S(2)}) copy-start(bf16[1,256,1600]{2,1,0:T(8,128)(2,1)S(1)} %copy.178) | copy-start | bytes 2457604
  304.6 18.7 %collective-permute-start.4 = (bf16[3,3200]{1,0:T(4,128)(2,1)S(1)}, bf16[3,3200]{1,0:T(4,128)(2,1)S(1)}, u32[]{:S(2)}, u32[]{:S(2)}) collective-permute-start(bf16[3,3200]{1,0:T(4,128)(2,1)S(1)} %fusion.112), channel_id=1, source_target_pairs={{0,1},{1,2},{2,3},{3,4},{4,5},{5,6},{6,7},{7,8},{8,9},{9,10},{10,1... | collective-permute-start | bytes 57608 | tf_op jit(solution)/shard_map/ppermute | solution.py:471
  307.4 19.7 %copy-start.22 = (bf16[16,200,128]{2,1,0:T(8,128)(2,1)}, bf16[16,200,128]{2,1,0:T(8,128)(2,1)S(1)}, u32[]{:S(2)}) copy-start(bf16[16,200,128]{2,1,0:T(8,128)(2,1)S(1)} %slice.510) | copy-start | bytes 2457604
  369.5 174.7 %all-gather.10.cloned.1.call-start = ((), (), s32[]{:S(2)}) async-start(), calls=%async_computation.8 | async-start | bytes 9957376 | tf_op jit(solution)/shard_map/all_gather | solution.py:1003
  370.2 322.2 %reduce-scatter.7.cloned.1.call-start = ((), (), s32[]{:S(2)}) async-start(), calls=%async_computation.5 | async-start | bytes 5271552 | tf_op jit(solution)/shard_map/reduce_scatter | solution.py:528
  371.4 30.6 %collective-permute-start = (bf16[256,640]{1,0:T(8,128)(2,1)S(1)}, bf16[256,640]{1,0:T(8,128)(2,1)S(1)}, u32[]{:S(2)}, u32[]{:S(2)}) collective-permute-start(bf16[256,640]{1,0:T(8,128)(2,1)S(1)} %slice.505), channel_id=1, source_target_pairs={{0,4},{1,5},{2,6},{3,7},{4,8},{5,9},{6,10},{7,11},{8,12},{9,13},{1... | collective-permute-start | bytes 983048 | tf_op jit(solution)/shard_map/ppermute | solution.py:471
  374.9 28.0 %collective-permute-start.1 = (bf16[256,640]{1,0:T(8,128)(2,1)S(1)}, bf16[256,640]{1,0:T(8,128)(2,1)S(1)}, u32[]{:S(2)}, u32[]{:S(2)}) collective-permute-start(bf16[256,640]{1,0:T(8,128)(2,1)S(1)} %slice.505), channel_id=1, source_target_pairs={{0,3},{1,4},{2,5},{3,6},{4,7},{5,8},{6,9},{7,10},{8,11},{9,12},{10... | collective-permute-start | bytes 983048 | tf_op jit(solution)/shard_map/ppermute | solution.py:471
  377.6 25.9 %collective-permute-start.2 = (bf16[256,640]{1,0:T(8,128)(2,1)S(1)}, bf16[256,640]{1,0:T(8,128)(2,1)S(1)}, u32[]{:S(2)}, u32[]{:S(2)}) collective-permute-start(bf16[256,640]{1,0:T(8,128)(2,1)S(1)} %slice.505), channel_id=1, source_target_pairs={{0,2},{1,3},{2,4},{3,5},{4,6},{5,7},{6,8},{7,9},{8,10},{9,11},{10,... | collective-permute-start | bytes 983048 | tf_op jit(solution)/shard_map/ppermute | solution.py:471
  381.2 23.1 %collective-permute-start.3 = (bf16[256,640]{1,0:T(8,128)(2,1)S(1)}, bf16[256,640]{1,0:T(8,128)(2,1)S(1)}, u32[]{:S(2)}, u32[]{:S(2)}) collective-permute-start(bf16[256,640]{1,0:T(8,128)(2,1)S(1)} %slice.505), channel_id=1, source_target_pairs={{0,1},{1,2},{2,3},{3,4},{4,5},{5,6},{6,7},{7,8},{8,9},{9,10},{10,1... | collective-permute-start | bytes 983048 | tf_op jit(solution)/shard_map/ppermute | solution.py:471
  398.9 80.2 %copy-start.96 = (f32[3200]{0:T(1024)}, f32[3200]{0:T(1024)S(1)}, u32[]{:S(2)}) copy-start(f32[3200]{0:T(1024)S(1)} %convert_element_type.285) | copy-start | bytes 38404
  499.2 146.5 %copy-start.2 = (f32[256,1600]{1,0:T(8,128)}, f32[256,1600]{1,0:T(8,128)S(1)}, u32[]{:S(2)}) copy-start(f32[256,1600]{1,0:T(8,128)S(1)} %get-tuple-element.226) | copy-start | bytes 4915204
  499.2 143.9 %copy-start.122 = (f32[256]{0:T(256)}, f32[256]{0:T(256)S(1)}, u32[]{:S(2)}) copy-start(f32[256]{0:T(256)S(1)} %fusion.119) | copy-start | bytes 3076
  504.3 22.7 %copy-start.49 = (bf16[256,1664]{1,0:T(8,128)(2,1)S(1)}, bf16[256,1664]{1,0:T(8,128)(2,1)}, u32[]{:S(2)}) copy-start(bf16[256,1664]{1,0:T(8,128)(2,1)} %repack.12) | copy-start | bytes 2555908
  504.3 21.8 %collective-permute-start.5 = (bf16[256,1664]{1,0:T(8,128)(2,1)}, bf16[256,1664]{1,0:T(8,128)(2,1)S(1)}, u32[]{:S(2)}, u32[]{:S(2)}) collective-permute-start(bf16[256,1664]{1,0:T(8,128)(2,1)} %repack.12), channel_id=1, source_target_pairs={{0,16},{16,0},{1,17},{17,1},{2,18},{18,2},{3,19},{19,3},{4,20},{20... | collective-permute-start | bytes 2555912 | tf_op jit(solution)/shard_map/ppermute | solution.py:475
  572.3 10.0 collective-permute-start.8
  580.8 31.2 %collective-permute-start.6 = (bf16[256,1600]{0,1:T(8,128)(2,1)S(1)}, bf16[256,1600]{0,1:T(8,128)(2,1)}, u32[]{:S(2)}, u32[]{:S(2)}) collective-permute-start(bf16[256,1600]{0,1:T(8,128)(2,1)S(1)} %slice.740), channel_id=1, source_target_pairs={{0,16},{16,0},{1,17},{17,1},{2,18},{18,2},{3,19},{19,3},{4,20},{20... | collective-permute-start | bytes 2457608 | tf_op jit(solution)/shard_map/ppermute | solution.py:475
  588.7 177.1 %all-gather.14.cloned.1.call-start = ((), (), s32[]{:S(2)}) async-start(), calls=%async_computation.10 | async-start | bytes 1740800 | tf_op jit(solution)/shard_map/all_gather | solution.py:1140
  616.5 21.1 %collective-permute-start.7 = (bf16[256,1664]{1,0:T(8,128)(2,1)S(1)}, bf16[256,1664]{1,0:T(8,128)(2,1)S(1)}, u32[]{:S(2)}, u32[]{:S(2)}) collective-permute-start(bf16[256,1664]{1,0:T(8,128)(2,1)S(1)} %slice.739), channel_id=1, source_target_pairs={{0,16},{16,0},{1,17},{17,1},{2,18},{18,2},{3,19},{19,3},{4,20},{20... | collective-permute-start | bytes 2555912 | tf_op jit(solution)/shard_map/ppermute | solution.py:475
  704.1 46.5 %collective-permute-start.11 = (bf16[2432,1792]{1,0:T(8,128)(2,1)}, bf16[2432,1792]{1,0:T(8,128)(2,1)}, u32[]{:S(2)}, u32[]{:S(2)}) collective-permute-start(bf16[2432,1792]{1,0:T(8,128)(2,1)} %multiply_convert_fusion), channel_id=1, source_target_pairs={{0,1},{1,0},{2,3},{3,2},{4,5},{5,4},{6,7},{7,6},{8,9},{9,8},{10,11... | collective-permute-start | bytes 26148872 | tf_op jit(solution)/shard_map/ppermute | solution.py:475
  717.2 18.7 %collective-permute-start.9 = (bf16[832,2816]{1,0:T(8,128)(2,1)}, bf16[832,2816]{1,0:T(8,128)(2,1)}, u32[]{:S(2)}, u32[]{:S(2)}) collective-permute-start(bf16[832,2816]{1,0:T(8,128)(2,1)} %convolution_convert_fusion.4), channel_id=1, source_target_pairs={{0,1},{1,0},{2,3},{3,2},{4,5},{5,4},{6,7},{7,6},{8,9},{9,8},{10,11... | collective-permute-start | bytes 14057480 | tf_op jit(solution)/shard_map/ppermute | solution.py:475
  722.6 20.6 %collective-permute-start.10 = (bf16[832,2816]{1,0:T(8,128)(2,1)}, bf16[832,2816]{1,0:T(8,128)(2,1)}, u32[]{:S(2)}, u32[]{:S(2)}) collective-permute-start(bf16[832,2816]{1,0:T(8,128)(2,1)} %convolution_convert_fusion.3), channel_id=1, source_target_pairs={{0,1},{1,0},{2,3},{3,2},{4,5},{5,4},{6,7},{7,6},{8,9},{9,8},{10,11... | collective-permute-start | bytes 14057480 | tf_op jit(solution)/shard_map/ppermute | solution.py:475
  722.6 153.3 %reduce-scatter.9.cloned.1.call-start = ((), (), s32[]{:S(2)}) async-start(), calls=%async_computation.6 | async-start | bytes 5271552 | tf_op jit(solution)/shard_map/reduce_scatter | solution.py:528
  725.0 9.9 collective-permute-start.12
  765.9 239.3 %reduce-scatter.11.cloned.1.call-start = ((), (), s32[]{:S(2)}) async-start(), calls=%async_computation.7 | async-start | bytes 5271552 | tf_op jit(solution)/shard_map/reduce_scatter | solution.py:528
  772.3 96.6 %collective-permute-start.17 = (bf16[2432,896]{1,0:T(8,128)(2,1)}, bf16[2432,896]{1,0:T(8,128)(2,1)}, u32[]{:S(2)}, u32[]{:S(2)}) collective-permute-start(bf16[2432,896]{1,0:T(8,128)(2,1)} %broadcast_select_fusion), channel_id=1, source_target_pairs={{0,16},{16,0},{1,17},{17,1},{2,18},{18,2},{3,19},{19,3},{4,20},{20... | collective-permute-start | bytes 13074440 | tf_op jit(solution)/shard_map/ppermute | solution.py:475
  838.0 22.8 %collective-permute-start.16 = (bf16[256,640]{1,0:T(8,128)(2,1)}, bf16[256,640]{1,0:T(8,128)(2,1)}, u32[]{:S(2)}, u32[]{:S(2)}) collective-permute-start(bf16[256,640]{1,0:T(8,128)(2,1)} %get-tuple-element.247), channel_id=1, source_target_pairs={{4,0},{5,1},{6,2},{7,3},{8,4},{9,5},{10,6},{11,7},{12,8},{13,9},{1... | collective-permute-start | bytes 983048 | tf_op jit(solution)/shard_map/ppermute | solution.py:471
  839.3 21.5 %collective-permute-start.15 = (bf16[256,640]{1,0:T(8,128)(2,1)}, bf16[256,640]{1,0:T(8,128)(2,1)}, u32[]{:S(2)}, u32[]{:S(2)}) collective-permute-start(bf16[256,640]{1,0:T(8,128)(2,1)} %get-tuple-element.248), channel_id=1, source_target_pairs={{3,0},{4,1},{5,2},{6,3},{7,4},{8,5},{9,6},{10,7},{11,8},{12,9},{13... | collective-permute-start | bytes 983048 | tf_op jit(solution)/shard_map/ppermute | solution.py:471
  840.6 20.2 %collective-permute-start.14 = (bf16[256,640]{1,0:T(8,128)(2,1)}, bf16[256,640]{1,0:T(8,128)(2,1)}, u32[]{:S(2)}, u32[]{:S(2)}) collective-permute-start(bf16[256,640]{1,0:T(8,128)(2,1)} %get-tuple-element.249), channel_id=1, source_target_pairs={{2,0},{3,1},{4,2},{5,3},{6,4},{7,5},{8,6},{9,7},{10,8},{11,9},{12,... | collective-permute-start | bytes 983048 | tf_op jit(solution)/shard_map/ppermute | solution.py:471
  841.9 18.9 %collective-permute-start.13 = (bf16[256,640]{1,0:T(8,128)(2,1)}, bf16[256,640]{1,0:T(8,128)(2,1)}, u32[]{:S(2)}, u32[]{:S(2)}) collective-permute-start(bf16[256,640]{1,0:T(8,128)(2,1)} %get-tuple-element.246), channel_id=1, source_target_pairs={{1,0},{2,1},{3,2},{4,3},{5,4},{6,5},{7,6},{8,7},{9,8},{10,9},{11,1... | collective-permute-start | bytes 983048 | tf_op jit(solution)/shard_map/ppermute | solution.py:471
  894.3 21.4 %collective-permute-start.18 = (bf16[832,5504]{1,0:T(8,128)(2,1)}, bf16[832,5504]{1,0:T(8,128)(2,1)}, u32[]{:S(2)}, u32[]{:S(2)}) collective-permute-start(bf16[832,5504]{1,0:T(8,128)(2,1)} %convolution_convert_fusion), channel_id=1, source_target_pairs={{0,1},{1,0},{2,3},{3,2},{4,5},{5,4},{6,7},{7,6},{8,9},{9,8},{10,11... | collective-permute-start | bytes 27475976 | tf_op jit(solution)/shard_map/ppermute | solution.py:475
  901.5 319.7 %reduce-scatter.13.cloned.1.call-start = ((), (), s32[]{:S(2)}) async-start(), calls=%async_computation.11 | async-start | bytes 10303488
  1029.0 12.9 collective-permute-start.19
  1040.4 82.0 %collective-permute-start.30 = (bf16[104,2816]{1,0:T(8,128)(2,1)}, bf16[104,2816]{1,0:T(8,128)(2,1)}, u32[]{:S(2)}, u32[]{:S(2)}) collective-permute-start(bf16[104,2816]{1,0:T(8,128)(2,1)} %broadcast_select_fusion.3), channel_id=1, source_target_pairs={{0,16},{16,0},{1,17},{17,1},{2,18},{18,2},{3,19},{19,3},{4,20},{20... | collective-permute-start | bytes 1757192 | tf_op jit(solution)/shard_map/ppermute | solution.py:475
  1059.0 72.4 %collective-permute-start.25 = (bf16[832,3328]{1,0:T(8,128)(2,1)}, bf16[832,3328]{1,0:T(8,128)(2,1)}, u32[]{:S(2)}, u32[]{:S(2)}) collective-permute-start(bf16[832,3328]{1,0:T(8,128)(2,1)} %convolution_convert_fusion.2), channel_id=1, source_target_pairs={{0,1},{1,0},{2,3},{3,2},{4,5},{5,4},{6,7},{7,6},{8,9},{9,8},{10,11... | collective-permute-start | bytes 16613384 | tf_op jit(solution)/shard_map/ppermute | solution.py:475
  1093.9 2.3 collective-permute-start.20
  1096.3 5.7 collective-permute-start.21
  1098.8 19.4 %copy-start.20 = (f32[256,1600]{1,0:T(8,128)S(1)}, f32[256,1600]{1,0:T(8,128)}, u32[]{:S(2)}) copy-start(f32[256,1600]{1,0:T(8,128)} %repack.15) | copy-start | bytes 4915204
  1102.0 7.7 collective-permute-start.22
  1109.7 7.0 collective-permute-start.23
  1110.0 18.0 %collective-permute-start.27 = (bf16[8,200,512]{2,1,0:T(8,128)(2,1)}, bf16[8,200,512]{2,1,0:T(8,128)(2,1)}, u32[]{:S(2)}, u32[]{:S(2)}) collective-permute-start(bf16[8,200,512]{2,1,0:T(8,128)(2,1)} %select_bitcast_fusion), channel_id=1, source_target_pairs={{0,1},{1,0},{2,3},{3,2},{4,5},{5,4},{6,7},{7,6},{8,9},{9,8},{10,11... | collective-permute-start | bytes 4915208 | tf_op jit(solution)/shard_map/ppermute | solution.py:475
  1116.7 4.4 collective-permute-start.24
  1221.2 128.1 %copy-start.55 = (bf16[1,104,5504]{2,1,0:T(8,128)(2,1)S(1)}, bf16[1,104,5504]{2,1,0:T(8,128)(2,1)}, u32[]{:S(2)}) copy-start(bf16[1,104,5504]{2,1,0:T(8,128)(2,1)} %reduce-scatter.13.cloned.1.call-done) | copy-start | bytes 3434500
  1347.8 27.9 %copy-start.57 = (f32[104,3328]{1,0:T(8,128)S(1)}, f32[104,3328]{1,0:T(8,128)}, u32[]{:S(2)}) copy-start(f32[104,3328]{1,0:T(8,128)} %get-tuple-element.126) | copy-start | bytes 4153348
  1347.8 27.9 %collective-permute-start.28 = (bf16[104,2176]{1,0:T(8,128)(2,1)}, bf16[104,2176]{1,0:T(8,128)(2,1)}, u32[]{:S(2)}, u32[]{:S(2)}) collective-permute-start(bf16[104,2176]{1,0:T(8,128)(2,1)} %fusion.83), channel_id=1, source_target_pairs={{0,16},{16,0},{1,17},{17,1},{2,18},{18,2},{3,19},{19,3},{4,20},{20... | collective-permute-start | bytes 1357832 | tf_op jit(solution)/shard_map/ppermute | solution.py:475
  1349.4 16.4 %collective-permute-start.29 = (f32[200,256]{1,0:T(8,128)S(1)}, f32[200,256]{1,0:T(8,128)S(1)}, u32[]{:S(2)}, u32[]{:S(2)}) collective-permute-start(f32[200,256]{1,0:T(8,128)S(1)} %slice_select_fusion.1), channel_id=1, source_target_pairs={{0,16},{16,0},{1,17},{17,1},{2,18},{18,2},{3,19},{19,3},{4,20},{20... | collective-permute-start | bytes 614408 | tf_op jit(solution)/shard_map/ppermute | solution.py:475
  1351.0 26.9 %collective-permute-start.26 = (bf16[104,3200]{1,0:T(8,128)(2,1)}, bf16[104,3200]{1,0:T(8,128)(2,1)}, u32[]{:S(2)}, u32[]{:S(2)}) collective-permute-start(bf16[104,3200]{1,0:T(8,128)(2,1)} %pad_select_fusion.2), channel_id=1, source_target_pairs={{0,16},{16,0},{1,17},{17,1},{2,18},{18,2},{3,19},{19,3},{4,20},{20... | collective-permute-start | bytes 1996808 | tf_op jit(solution)/shard_map/ppermute | solution.py:475
  (165 other events, 1019.6 us)
Sparse Core Ops, SparseCore 0:
  268.9 98.8 all-gather.11
  370.0 49.2 all-gather.7
  421.4 79.0 all-gather.9
  588.8 96.8 reduce-scatter.6
  722.8 43.0 all-gather.13
  769.2 105.1 reduce-scatter.8
  901.6 103.5 reduce-scatter.10
  1030.4 190.6 reduce-scatter.12
